TPU v7x, 32 devices: a whole 2x2x4 slice. The times are simulated.
32 devices in a mesh: fsdp: 8 (over y, x, core), tp: 4 (over z).
Axes of the slice: x: 2, y: 2, z: 4, core: 2. Of those that a mesh axis runs over, the one named last changes fastest.
Arguments:
- tokens: bfloat16 [32768, 1024], P(('fsdp', 'tp')), may hold values from -6 to 6
- segments: int32 [32, 1024], P('fsdp'), may hold values from 0 to 6, as said below
- attn_gain: bfloat16 [1024], replicated, may hold values from 0.099609375 to 1.8984375
- attn_shift: bfloat16 [1024], replicated, may hold values from -1.75 to 1.75
- mlp_gain: bfloat16 [1024], replicated, may hold values from 0.099609375 to 1.8984375
- mlp_shift: bfloat16 [1024], replicated, may hold values from -1.75 to 1.75
- qkv_weight: bfloat16 [1024, 3, 1024], P('fsdp', None, 'tp'), may hold values from -0.1875 to 0.1875
- qkv_bias: bfloat16 [3, 1024], replicated, may hold values from -3 to 3
- out_weight: bfloat16 [1024, 1024], P('tp', 'fsdp'), may hold values from -0.75 to 0.75
- out_bias: bfloat16 [1024], replicated, may hold values from -1.75 to 1.75
- up_weight: bfloat16 [1024, 4096], P('fsdp', 'tp'), may hold values from -0.1875 to 0.1875
- up_bias: bfloat16 [4096], replicated, may hold values from -3 to 3
- down_weight: bfloat16 [4096, 1024], P('tp', 'fsdp'), may hold values from -0.09375 to 0.09375
- down_bias: bfloat16 [1024], replicated, may hold values from -1.75 to 1.75
- cotangent: bfloat16 [32768, 1024], P(('fsdp', 'tp')), may hold values from -6 to 6
Outputs:
- output: bfloat16 [32768, 1024], P(('fsdp', 'tp'))
- input_grad: float32 [32768, 1024], P(('fsdp', 'tp'))
- attn_gain_grad: float32 [1024], replicated
- attn_shift_grad: float32 [1024], replicated
- mlp_gain_grad: float32 [1024], replicated
- mlp_shift_grad: float32 [1024], replicated
- qkv_weight_grad: float32 [1024, 3, 1024], P('fsdp', None, 'tp')
- qkv_bias_grad: float32 [3, 1024], replicated
- out_weight_grad: float32 [1024, 1024], P('tp', 'fsdp')
- out_bias_grad: float32 [1024], replicated
- up_weight_grad: float32 [1024, 4096], P('fsdp', 'tp')
- up_bias_grad: float32 [4096], replicated
- down_weight_grad: float32 [4096, 1024], P('tp', 'fsdp')
- down_bias_grad: float32 [1024], replicated
Inputs may be any that keep to these rules, and one draw needn't show every extreme that they name: `segments`: each packed sequence is a window of 1024 tokens cut from a stream of documents whose lengths lie between about 0.2 * 1024 and 2048; a sequence's segment numbers count its pieces from 0 and never fall, and only its first and last piece can be shorter than a whole document.
All inputs are finite; a program needn't handle non-finite values.
Results may differ from a plain program's by a relative error of at most 0.012.
Values may be sent and summed in bfloat16 or wider, within the bound.
No kernel may reach another device: no remote copies, remote signals or barrier semaphores. Data moves between devices by JAX's collectives and lax.ppermute only.
A program may use at most 256 MiB of HBM per device.

v0:
```python
from functools import partial
import math

import jax
import jax.numpy as jnp
from jax import lax
from jax.sharding import PartitionSpec as P

HD = 64
ROT = 16


EPS = 1e-05
NEG = -1000000000.0


def layer_norm(values, gain_row, shift_row):
    centre = values - jnp.mean(values, axis=-1, keepdims=True)
    spread = jnp.mean(centre * centre, axis=-1, keepdims=True)
    return centre * lax.rsqrt(spread + EPS) * gain_row + shift_row


def doc_positions(segment_ids):
    length = segment_ids.shape[-1]
    column = jnp.arange(length, dtype=jnp.int32)
    before = jnp.concatenate(
        [jnp.full(segment_ids.shape[:-1] + (1,), -1, jnp.int32), segment_ids[..., :-1]], axis=-1
    )
    starts = lax.cummax(jnp.where(segment_ids != before, column, 0), axis=segment_ids.ndim - 1)
    return column - starts


def rotary_tables(segment_ids):
    inverse_freq = jnp.power(10000.0, -jnp.arange(0, ROT, 2, dtype=jnp.float32) / ROT)
    places = doc_positions(segment_ids).reshape(-1).astype(jnp.float32)
    angles = places[:, None] * inverse_freq[None, :]
    return (jnp.cos(angles)[:, None, :], jnp.sin(angles)[:, None, :])


def rotate(head_values, cos_table, sine_table):
    half_dims = ROT // 2
    first_half = head_values[..., :half_dims]
    second = head_values[..., half_dims:ROT]
    return jnp.concatenate(
        [
            first_half * cos_table - second * sine_table,
            second * cos_table + first_half * sine_table,
            head_values[..., ROT:],
        ],
        axis=-1,
    )


def allowed(segment_ids):
    column = jnp.arange(segment_ids.shape[0], dtype=jnp.int32)
    return (column[:, None] >= column[None, :]) & (segment_ids[:, None] == segment_ids[None, :])


def masked_scores(queries, key_rows, segment_ids, score_scale):
    scores = (
        jnp.einsum("qhd,khd->hqk", queries, key_rows, preferred_element_type=jnp.float32)
        * score_scale
    )
    return jnp.where(allowed(segment_ids), scores, NEG)


def attend_block(inputs, score_scale):
    queries, key_rows, values, segment_ids = inputs
    scores = masked_scores(queries, key_rows, segment_ids, score_scale)
    maxima = jnp.max(scores, axis=-1, keepdims=True)
    exponent = jnp.exp(scores - maxima)
    totals = jnp.sum(exponent, axis=-1, keepdims=True)
    softmax_rows = (exponent / totals).astype(jnp.bfloat16)
    result = jnp.einsum("hqk,khd->qhd", softmax_rows, values, preferred_element_type=jnp.float32)
    return (result, (maxima + jnp.log(totals))[..., 0])


def attend_back(inputs, score_scale):
    queries, key_rows, values, segment_ids, logsum, grad_out = inputs
    scores = masked_scores(queries, key_rows, segment_ids, score_scale)
    softmax_rows = jnp.exp(scores - logsum[..., None])
    grad_values = jnp.einsum(
        "hqk,qhd->khd",
        softmax_rows.astype(jnp.bfloat16),
        grad_out,
        preferred_element_type=jnp.float32,
    )
    grad_probs = jnp.einsum("qhd,khd->hqk", grad_out, values, preferred_element_type=jnp.float32)
    grad_scores = (
        softmax_rows * (grad_probs - jnp.sum(softmax_rows * grad_probs, axis=-1, keepdims=True))
    ).astype(jnp.bfloat16)
    grad_queries = (
        jnp.einsum("hqk,khd->qhd", grad_scores, key_rows, preferred_element_type=jnp.float32)
        * score_scale
    )
    grad_keys = (
        jnp.einsum("hqk,qhd->khd", grad_scores, queries, preferred_element_type=jnp.float32)
        * score_scale
    )
    return (grad_queries, grad_keys, grad_values)


def body(
    tokens,
    segments,
    attn_gain,
    attn_shift,
    mlp_gain,
    mlp_shift,
    qkv_weight,
    qkv_bias,
    out_weight,
    out_bias,
    up_weight,
    up_bias,
    down_weight,
    down_bias,
    cotangent,
):
    lane_count = lax.axis_size("tp")
    lane_index = lax.axis_index("tp")
    own_rows = tokens.shape[0]
    group_rows = own_rows * lane_count
    seq_count = segments.shape[0]
    seq_length = segments.shape[1]
    head_width = qkv_weight.shape[2]
    local_heads = head_width // HD
    unit_width = up_weight.shape[1]
    score_scale = 1.0 / math.sqrt(HD)
    norm_terms = tuple(
        (member.astype(jnp.float32) for member in (attn_gain, attn_shift, mlp_gain, mlp_shift))
    )
    qkv_local = lax.dynamic_slice_in_dim(qkv_bias, lane_index * head_width, head_width, 1).astype(
        jnp.float32
    )
    up_local = lax.dynamic_slice_in_dim(up_bias, lane_index * unit_width, unit_width, 0).astype(
        jnp.float32
    )
    qkv_full, out_full, up_full, down_full = (
        lax.all_gather(qkv_weight, "fsdp", axis=0, tiled=True),
        lax.all_gather(out_weight, "fsdp", axis=1, tiled=True),
        lax.all_gather(up_weight, "fsdp", axis=0, tiled=True),
        lax.all_gather(down_weight, "fsdp", axis=1, tiled=True),
    )
    own_input = tokens.astype(jnp.float32)
    attn_normed = layer_norm(own_input, norm_terms[0], norm_terms[1]).astype(jnp.bfloat16)
    mlp_normed = layer_norm(own_input, norm_terms[2], norm_terms[3]).astype(jnp.bfloat16)
    attn_normed, mlp_normed = (
        lax.all_gather(attn_normed, "tp", axis=0, tiled=True),
        lax.all_gather(mlp_normed, "tp", axis=0, tiled=True),
    )
    mixed_rows = (
        jnp.einsum("rd,dcw->rcw", attn_normed, qkv_full, preferred_element_type=jnp.float32)
        + qkv_local
    )
    head_values = mixed_rows.reshape(group_rows, 3, local_heads, HD)
    cos_table, sine_table = rotary_tables(segments)
    queries = rotate(head_values[:, 0], cos_table, sine_table).astype(jnp.bfloat16)
    key_rows = rotate(head_values[:, 1], cos_table, sine_table).astype(jnp.bfloat16)
    values = head_values[:, 2].astype(jnp.bfloat16)
    seq_shape = (seq_count, seq_length, local_heads, HD)
    query_seqs = queries.reshape(seq_shape)
    key_seqs = key_rows.reshape(seq_shape)
    value_seqs = values.reshape(seq_shape)
    attn_rows, logsum = lax.map(
        partial(attend_block, score_scale=score_scale), (query_seqs, key_seqs, value_seqs, segments)
    )
    attended = attn_rows.reshape(group_rows, head_width).astype(jnp.bfloat16)
    gate_rows = jnp.dot(mlp_normed, up_full, preferred_element_type=jnp.float32) + up_local
    active = jax.nn.gelu(gate_rows, approximate=False).astype(jnp.bfloat16)
    partial_out = jnp.dot(attended, out_full, preferred_element_type=jnp.float32) + jnp.dot(
        active, down_full, preferred_element_type=jnp.float32
    )
    summed = lax.psum_scatter(
        partial_out.astype(jnp.bfloat16), "tp", scatter_dimension=0, tiled=True
    ).astype(jnp.float32)
    output = (
        own_input + summed + out_bias.astype(jnp.float32) + down_bias.astype(jnp.float32)
    ).astype(jnp.bfloat16)
    qkv_full, out_full, up_full, down_full = (
        lax.all_gather(qkv_weight, "fsdp", axis=0, tiled=True),
        lax.all_gather(out_weight, "fsdp", axis=1, tiled=True),
        lax.all_gather(up_weight, "fsdp", axis=0, tiled=True),
        lax.all_gather(down_weight, "fsdp", axis=1, tiled=True),
    )
    grad_rows = lax.all_gather(cotangent, "tp", axis=0, tiled=True)
    own_grad = cotangent.astype(jnp.float32)
    bias_grad = jnp.sum(own_grad, axis=0)
    grad_out_weight = jnp.einsum(
        "rw,rd->wd", attended, grad_rows, preferred_element_type=jnp.float32
    )
    grad_down_weight = jnp.einsum(
        "rf,rd->fd", active, grad_rows, preferred_element_type=jnp.float32
    )
    grad_active = jnp.einsum("rd,fd->rf", grad_rows, down_full, preferred_element_type=jnp.float32)
    gelu_pull = jax.vjp(lambda inner: jax.nn.gelu(inner, approximate=False), gate_rows)[1]
    grad_gate = gelu_pull(grad_active)[0].astype(jnp.bfloat16)
    up_bias_local = jnp.sum(grad_gate.astype(jnp.float32), axis=0)
    grad_up_weight = jnp.einsum(
        "rd,rf->df", mlp_normed, grad_gate, preferred_element_type=jnp.float32
    )
    grad_mlp_normed = jnp.einsum(
        "rf,df->rd", grad_gate, up_full, preferred_element_type=jnp.float32
    )
    grad_attended = jnp.einsum(
        "rd,wd->rw", grad_rows, out_full, preferred_element_type=jnp.float32
    ).astype(jnp.bfloat16)
    grad_queries, grad_keys, grad_values = lax.map(
        partial(attend_back, score_scale=score_scale),
        (query_seqs, key_seqs, value_seqs, segments, logsum, grad_attended.reshape(seq_shape)),
    )
    rotate_pull = jax.vjp(lambda inner: rotate(inner, cos_table, sine_table), head_values[:, 0])[1]
    grad_query_rows = rotate_pull(grad_queries.reshape(group_rows, local_heads, HD))[0]
    grad_key_rows = rotate_pull(grad_keys.reshape(group_rows, local_heads, HD))[0]
    grad_mixed = (
        jnp.stack(
            [grad_query_rows, grad_key_rows, grad_values.reshape(group_rows, local_heads, HD)],
            axis=1,
        )
        .reshape(group_rows, 3, head_width)
        .astype(jnp.bfloat16)
    )
    qkv_bias_local = jnp.sum(grad_mixed.astype(jnp.float32), axis=0)
    grad_qkv_weight = jnp.einsum(
        "rd,rcw->dcw", attn_normed, grad_mixed, preferred_element_type=jnp.float32
    )
    grad_attn_normed = jnp.einsum(
        "rcw,dcw->rd", grad_mixed, qkv_full, preferred_element_type=jnp.float32
    )
    grad_attn_own, grad_mlp_own = (
        lax.psum_scatter(
            grad_attn_normed.astype(jnp.bfloat16), "tp", scatter_dimension=0, tiled=True
        ).astype(jnp.float32),
        lax.psum_scatter(
            grad_mlp_normed.astype(jnp.bfloat16), "tp", scatter_dimension=0, tiled=True
        ).astype(jnp.float32),
    )
    attn_pull = jax.vjp(layer_norm, own_input, norm_terms[0], norm_terms[1])[1]
    mlp_pull = jax.vjp(layer_norm, own_input, norm_terms[2], norm_terms[3])[1]
    into_attn = attn_pull(grad_attn_own)
    into_mlp = mlp_pull(grad_mlp_own)
    input_grad = own_grad + into_attn[0] + into_mlp[0]
    qkv_bias_full = lax.dynamic_update_slice_in_dim(
        jnp.zeros(qkv_bias.shape, jnp.float32), qkv_bias_local, lane_index * head_width, 1
    )
    up_bias_full = lax.dynamic_update_slice_in_dim(
        jnp.zeros(up_bias.shape, jnp.float32), up_bias_local, lane_index * unit_width, 0
    )
    small_sums = lax.psum(
        (
            into_attn[1],
            into_attn[2],
            into_mlp[1],
            into_mlp[2],
            qkv_bias_full,
            bias_grad,
            up_bias_full,
        ),
        ("fsdp", "tp"),
    )
    weight_sums = (
        lax.psum_scatter(grad_qkv_weight, "fsdp", scatter_dimension=0, tiled=True),
        lax.psum_scatter(grad_out_weight, "fsdp", scatter_dimension=1, tiled=True),
        lax.psum_scatter(grad_up_weight, "fsdp", scatter_dimension=0, tiled=True),
        lax.psum_scatter(grad_down_weight, "fsdp", scatter_dimension=1, tiled=True),
    )
    return (
        output,
        input_grad,
        small_sums[0],
        small_sums[1],
        small_sums[2],
        small_sums[3],
        weight_sums[0],
        small_sums[4],
        weight_sums[1],
        small_sums[5],
        weight_sums[2],
        small_sums[6],
        weight_sums[3],
        small_sums[5],
    )


def solution(mesh):
    placed = (
        P(("fsdp", "tp"), None),
        P("fsdp", None),
        P(),
        P(),
        P(),
        P(),
        P("fsdp", None, "tp"),
        P(),
        P("tp", "fsdp"),
        P(),
        P("fsdp", "tp"),
        P(),
        P("tp", "fsdp"),
        P(),
        P(("fsdp", "tp"), None),
    )
    return jax.shard_map(
        body,
        mesh=mesh,
        in_specs=placed,
        out_specs=(
            P(("fsdp", "tp"), None),
            P(("fsdp", "tp"), None),
            P(),
            P(),
            P(),
            P(),
            P("fsdp", None, "tp"),
            P(),
            P("tp", "fsdp"),
            P(),
            P("fsdp", "tp"),
            P(),
            P("tp", "fsdp"),
            P(),
        ),
        check_vma=False,
    )
```

profile of v0, /device:TPU:0, one launch (start us, length us, event | category | flops | bytes accessed | tf_op | source)
XLA Modules:
  0.0 1460.1 jit_solution(3248964682099535267)
XLA Ops:
  23.3 13.8 all_gather.27
  39.8 152.0 %all-gather.7.cloned.1.call-done = bf16[4096,1024]{1,0:T(8,128)(2,1)} async-done(((bf16[1024,1024]{1,0:T(8,128)(2,1)}), bf16[4096,1024]{1,0:T(8,128)(2,1)}) %all-gather.7.cloned.1.call-update) | async-done | bytes 8388624 | tf_op jit(solution)/shard_map/all_gather | solution.py:149
  230.7 63.9 %while.26 = (s32[]{:T(128)}, bf16[4,1024,4,64]{1,3,2,0:T(8,128)(2,1)}, f32[4,4,1024]{2,1,0:T(4,128)}, bf16[4,1024,4,64]{1,3,2,0:T(8,128)(2,1)}, s32[4,1024]{1,0:...) while((s32[]{:T(128)}, ...), condition=%wide.region_7.8_spmd, body=%wide.region_4.7_spmd.sunk | while | flops 1127215104 | bytes 57293400 | solution.py:165
  294.6 46.7 %all-gather.17.cloned.1.call-done = bf16[4096,1024]{1,0:T(8,128)(2,1)} async-done(((bf16[1024,1024]{1,0:T(8,128)(2,1)}), bf16[4096,1024]{1,0:T(8,128)(2,1)}) %all-gather.17.cloned.1.call-update) | async-done | bytes 8388624 | tf_op jit(solution)/shard_map/all_gather | solution.py:186
  364.0 398.9 %while.27 = (s32[]{:T(128)}, f32[4,1024,4,64]{1,0,3,2:T(4,128)}, f32[4,1024,4,64]{1,0,3,2:T(4,128)}, bf16[4,1024,4,64]{1,3,2,0:T(8,128)(2,1)}, bf16[4,1024,4,64]...) while((s32[]{:T(128)}, f32[4,1024,4,64]{1,0,3,2:T(4,128)}, ...), condition=%wide.region_11.12_spmd, body=%wide.region_9.11_spmd.sunk | while | flops 2725769216 | bytes 260800816 | solution.py:208
  376.2 14.4 multiply_reduce_fusion.2
  409.5 20.0 %dynamic_update_slice.38 = f32[4,1024,4,64]{1,0,3,2:T(4,128)} dynamic-update-slice(f32[4,1024,4,64]{1,0,3,2:T(4,128)} %get-tuple-element.371, f32[1,1024,4,64]{1,0,3,2:T(1,128)S(1)} %copy.105, s32[]{:T(128)} %get-tuple-element.369, s32[]{:T(128)} %constant.69.clone.1..sunk, s32[]{:T(128)} %constant.69.clone.1..sunk, s32[]{:T(128)} %constant.69.clone.1..sunk) | dynamic-update-slice | bytes 2097156 | tf_op jit(solution)/shard_map/while/body/jit(dynamic_update_index_in_dim)/dynamic_update_slice | solution.py:165
  435.8 20.0 %dynamic_update_slice.37 = f32[4,1024,4,64]{1,0,3,2:T(4,128)} dynamic-update-slice(f32[4,1024,4,64]{1,0,3,2:T(4,128)} %get-tuple-element.370, f32[1,1024,4,64]{1,0,3,2:T(1,128)S(1)} %copy.104, s32[]{:T(128)} %get-tuple-element.369, s32[]{:T(128)} %constant.69.clone.1..sunk, s32[]{:T(128)} %constant.69.clone.1..sunk, s32[]{:T(128)} %constant.69.clone.1..sunk) | dynamic-update-slice | bytes 2097156 | tf_op jit(solution)/shard_map/while/body/jit(dynamic_update_index_in_dim)/dynamic_update_slice | solution.py:165
  508.8 20.0 %dynamic_update_slice.38 = f32[4,1024,4,64]{1,0,3,2:T(4,128)} dynamic-update-slice(f32[4,1024,4,64]{1,0,3,2:T(4,128)} %get-tuple-element.371, f32[1,1024,4,64]{1,0,3,2:T(1,128)S(1)} %copy.105, s32[]{:T(128)} %get-tuple-element.369, s32[]{:T(128)} %constant.69.clone.1..sunk, s32[]{:T(128)} %constant.69.clone.1..sunk, s32[]{:T(128)} %constant.69.clone.1..sunk) | dynamic-update-slice | bytes 2097156 | tf_op jit(solution)/shard_map/while/body/jit(dynamic_update_index_in_dim)/dynamic_update_slice | solution.py:165
  535.0 20.0 %dynamic_update_slice.37 = f32[4,1024,4,64]{1,0,3,2:T(4,128)} dynamic-update-slice(f32[4,1024,4,64]{1,0,3,2:T(4,128)} %get-tuple-element.370, f32[1,1024,4,64]{1,0,3,2:T(1,128)S(1)} %copy.104, s32[]{:T(128)} %get-tuple-element.369, s32[]{:T(128)} %constant.69.clone.1..sunk, s32[]{:T(128)} %constant.69.clone.1..sunk, s32[]{:T(128)} %constant.69.clone.1..sunk) | dynamic-update-slice | bytes 2097156 | tf_op jit(solution)/shard_map/while/body/jit(dynamic_update_index_in_dim)/dynamic_update_slice | solution.py:165
  607.9 19.9 %dynamic_update_slice.38 = f32[4,1024,4,64]{1,0,3,2:T(4,128)} dynamic-update-slice(f32[4,1024,4,64]{1,0,3,2:T(4,128)} %get-tuple-element.371, f32[1,1024,4,64]{1,0,3,2:T(1,128)S(1)} %copy.105, s32[]{:T(128)} %get-tuple-element.369, s32[]{:T(128)} %constant.69.clone.1..sunk, s32[]{:T(128)} %constant.69.clone.1..sunk, s32[]{:T(128)} %constant.69.clone.1..sunk) | dynamic-update-slice | bytes 2097156 | tf_op jit(solution)/shard_map/while/body/jit(dynamic_update_index_in_dim)/dynamic_update_slice | solution.py:165
  634.1 19.9 %dynamic_update_slice.37 = f32[4,1024,4,64]{1,0,3,2:T(4,128)} dynamic-update-slice(f32[4,1024,4,64]{1,0,3,2:T(4,128)} %get-tuple-element.370, f32[1,1024,4,64]{1,0,3,2:T(1,128)S(1)} %copy.104, s32[]{:T(128)} %get-tuple-element.369, s32[]{:T(128)} %constant.69.clone.1..sunk, s32[]{:T(128)} %constant.69.clone.1..sunk, s32[]{:T(128)} %constant.69.clone.1..sunk) | dynamic-update-slice | bytes 2097156 | tf_op jit(solution)/shard_map/while/body/jit(dynamic_update_index_in_dim)/dynamic_update_slice | solution.py:165
  707.0 19.9 %dynamic_update_slice.38 = f32[4,1024,4,64]{1,0,3,2:T(4,128)} dynamic-update-slice(f32[4,1024,4,64]{1,0,3,2:T(4,128)} %get-tuple-element.371, f32[1,1024,4,64]{1,0,3,2:T(1,128)S(1)} %copy.105, s32[]{:T(128)} %get-tuple-element.369, s32[]{:T(128)} %constant.69.clone.1..sunk, s32[]{:T(128)} %constant.69.clone.1..sunk, s32[]{:T(128)} %constant.69.clone.1..sunk) | dynamic-update-slice | bytes 2097156 | tf_op jit(solution)/shard_map/while/body/jit(dynamic_update_index_in_dim)/dynamic_update_slice | solution.py:165
  733.2 19.9 %dynamic_update_slice.37 = f32[4,1024,4,64]{1,0,3,2:T(4,128)} dynamic-update-slice(f32[4,1024,4,64]{1,0,3,2:T(4,128)} %get-tuple-element.370, f32[1,1024,4,64]{1,0,3,2:T(1,128)S(1)} %copy.104, s32[]{:T(128)} %get-tuple-element.369, s32[]{:T(128)} %constant.69.clone.1..sunk, s32[]{:T(128)} %constant.69.clone.1..sunk, s32[]{:T(128)} %constant.69.clone.1..sunk) | dynamic-update-slice | bytes 2097156 | tf_op jit(solution)/shard_map/while/body/jit(dynamic_update_index_in_dim)/dynamic_update_slice | solution.py:165
  813.5 16.5 %fusion.89 = f32[4096,1024]{1,0:T(8,128)} fusion(bf16[4096,1024]{1,0:T(8,128)(2,1)} %all-gather.11.cloned.1.call-done, bf16[1024,1024]{1,0:T(8,128)(2,1)} %all-gather.13.cloned.1.call-done), kind=kOutput, calls=%fused_computation.163 | convolution fusion | flops 8589934592 | bytes 27262976 | tf_op jit(solution)/shard_map/dot_general | solution.py:169
  830.0 51.6 %convert_reduce_fusion = (f32[1024]{0:T(1024)S(1)}, bf16[4096,1024]{1,0:T(8,128)(2,1)S(1)}, f32[4096,1024]{1,0:T(8,128)}) fusion(f32[4096,1024]{1,0:T(8,128)} %fusion.89, f32[1024]{0:T(1024)S(1)} %copy-done.35, bf16[4096,1024]{1,0:T(8,128)(2,1)} %all-gather.17.cloned.1.call-done, bf16[1024,1024]{1,0:T(8,128)(2,1)} %all-gather.15.cloned.1.call-done), kind=kOutput, calls=%fused_computation.61 | convolution fusion | flops 8904506368 | bytes 52436992 | tf_op jit(solution)/shard_map/rd,fd->rf/dot_general | solution.py:195
  954.8 15.2 %fusion.93 = f32[1024,1024]{1,0:T(8,128)} fusion(bf16[4096,1024]{1,0:T(8,128)(2,1)} %copy-done.12, bf16[4096,1024]{1,0:T(8,128)(2,1)} %all-gather.17.cloned.1.call-done), kind=kOutput, calls=%fused_computation.167 | convolution fusion | flops 8589934592 | bytes 20971520 | tf_op jit(solution)/shard_map/rf,rd->fd/dot_general | solution.py:192
  970.3 15.1 %fusion.92 = f32[1024,1024]{1,0:T(8,128)} fusion(bf16[4096,1024]{1,0:T(8,128)(2,1)} %all-gather.11.cloned.1.call-done, bf16[4096,1024]{1,0:T(8,128)(2,1)} %copy-done.41), kind=kOutput, calls=%fused_computation.166 | convolution fusion | flops 8589934592 | bytes 20971520 | tf_op jit(solution)/shard_map/rd,rf->df/dot_general | solution.py:199
  990.5 113.2 %reduce-scatter.12.cloned.1.call-done = bf16[1024,1024]{1,0:T(8,128)(2,1)} async-done(((bf16[4096,1024]{1,0:T(8,128)(2,1)}), bf16[1024,1024]{1,0:T(8,128)(2,1)}) %reduce-scatter.12.cloned.1.call-update) | async-done | bytes 2097168 | tf_op jit(solution)/shard_map/reduce_scatter | solution.py:234
  1112.2 139.2 %reduce-scatter.8.cloned.1.call-done = bf16[1024,1024]{1,0:T(8,128)(2,1)} async-done(((bf16[4096,1024]{1,0:T(8,128)(2,1)}), bf16[1024,1024]{1,0:T(8,128)(2,1)}) %reduce-scatter.8.cloned.1.call-update) | async-done | bytes 2097168 | tf_op jit(solution)/shard_map/reduce_scatter | solution.py:174
  1260.0 42.2 %all-reduce.7 = (f32[1024]{0:T(1024)}, f32[1024]{0:T(1024)}, f32[1024]{0:T(1024)}, f32[1024]{0:T(1024)}, f32[3,1024]{1,0:T(4,128)}, /*index=5*/f32[1024]{0:T(1024)S(1)}, f32[4096]{0:T(1024)}) all-reduce(f32[1024]{0:T(1024)S(1)} %get-tuple-element.143, ...), channel_id=1, replica_groups=mesh['fsdp'=8,'tp'=4] {'fsdp','tp'}, use_global_device_ids=true, to_apply=%region_19.20 | all-reduce | flops 12288 | bytes 98304 | tf_op jit(solution)/shard_map/psum | solution.py:249
  1302.2 39.7 %reduce-scatter.14.cloned.1.call-done = f32[128,3,256]{2,0,1:T(8,128)} async-done(((f32[1024,3,256]{2,0,1:T(8,128)}), f32[128,3,256]{2,0,1:T(8,128)}) %reduce-scatter.14.cloned.1.call-update) | async-done | bytes 393232 | tf_op jit(solution)/shard_map/reduce_scatter | solution.py:262
  1341.9 55.5 %reduce-scatter.20.cloned.1.call-done = f32[1024,128]{1,0:T(8,128)} async-done(((f32[1024,1024]{1,0:T(8,128)}), f32[1024,128]{1,0:T(8,128)}) %reduce-scatter.20.cloned.1.call-update) | async-done | bytes 524304 | tf_op jit(solution)/shard_map/reduce_scatter | solution.py:265
  1397.4 55.3 %reduce-scatter.18.cloned.1.call-done = f32[128,1024]{1,0:T(8,128)} async-done(((f32[1024,1024]{1,0:T(8,128)}), f32[128,1024]{1,0:T(8,128)}) %reduce-scatter.18.cloned.1.call-update) | async-done | bytes 524304 | tf_op jit(solution)/shard_map/reduce_scatter | solution.py:264
  (301 shorter events, 513.9 us)
Async XLA Ops:
  7.2 32.6 %all-gather.9.cloned.1.call-start = ((), (), s32[]{:S(2)}) async-start(), calls=%async_computation.8 | async-start | bytes 1769472 | tf_op jit(solution)/shard_map/all_gather | solution.py:140
  9.1 182.7 %all-gather.7.cloned.1.call-start = ((), (), s32[]{:S(2)}) async-start(), calls=%async_computation.7 | async-start | bytes 10485760 | tf_op jit(solution)/shard_map/all_gather | solution.py:149
  19.1 322.2 %all-gather.17.cloned.1.call-start = ((), (), s32[]{:S(2)}) async-start(), calls=%async_computation.13 | async-start | bytes 10485760 | tf_op jit(solution)/shard_map/all_gather | solution.py:186
  19.8 793.6 %all-gather.13.cloned.1.call-start = ((), (), s32[]{:S(2)}) async-start(), calls=%async_computation.10 | async-start | bytes 2359296 | tf_op jit(solution)/shard_map/all_gather | solution.py:142
  20.4 793.1 %all-gather.11.cloned.1.call-start = ((), (), s32[]{:S(2)}) async-start(), calls=%async_computation.9 | async-start | bytes 10485760 | tf_op jit(solution)/shard_map/all_gather | solution.py:150
  21.0 809.0 %all-gather.15.cloned.1.call-start = ((), (), s32[]{:S(2)}) async-start(), calls=%async_computation.11 | async-start | bytes 2359296 | tf_op jit(solution)/shard_map/all_gather | solution.py:143
  21.6 969.0 %reduce-scatter.10.cloned.1.call-start = ((), (), s32[]{:S(2)}) async-start(), calls=%async_computation.14 | async-start | bytes 10485760 | tf_op jit(solution)/shard_map/reduce_scatter | solution.py:231
  38.5 167.1 %copy-start.15 = (f32[4096,8]{0,1:T(8,128)}, f32[4096,8]{0,1:T(8,128)S(1)}, u32[]{:S(2)}) copy-start(f32[4096,8]{0,1:T(8,128)S(1)} %get-tuple-element.215) | copy-start | bytes 393220
  38.5 167.1 %copy-start.17 = (f32[4096,8]{0,1:T(8,128)}, f32[4096,8]{0,1:T(8,128)S(1)}, u32[]{:S(2)}) copy-start(f32[4096,8]{0,1:T(8,128)S(1)} %get-tuple-element.216) | copy-start | bytes 393220
  230.7 110.6 %copy-start.13 = (bf16[256,1024]{1,0:T(8,128)(2,1)S(1)}, bf16[256,1024]{1,0:T(8,128)(2,1)}, u32[]{:S(2)}) copy-start(bf16[256,1024]{1,0:T(8,128)(2,1)} %all_gather.27) | copy-start | bytes 1572868
  813.4 290.4 %reduce-scatter.12.cloned.1.call-start = ((), (), s32[]{:S(2)}) async-start(), calls=%async_computation.15 | async-start | bytes 10485760 | tf_op jit(solution)/shard_map/reduce_scatter | solution.py:234
  830.0 55.0 %copy-start.40 = (bf16[1024,1024]{1,0:T(8,128)(2,1)S(1)}, bf16[1024,1024]{1,0:T(8,128)(2,1)}, u32[]{:S(2)}) copy-start(bf16[1024,1024]{1,0:T(8,128)(2,1)} %all-gather.13.cloned.1.call-done) | copy-start | bytes 6291460
  896.1 355.3 %reduce-scatter.8.cloned.1.call-start = ((), (), s32[]{:S(2)}) async-start(), calls=%async_computation.12 | async-start | bytes 10485760 | tf_op jit(solution)/shard_map/reduce_scatter | solution.py:174
  935.4 366.8 %reduce-scatter.16.cloned.1.call-start = ((), (), s32[]{:S(2)}) async-start(), calls=%async_computation.17 | async-start | bytes 1179648 | tf_op jit(solution)/shard_map/reduce_scatter | solution.py:263
  942.4 399.5 %reduce-scatter.14.cloned.1.call-start = ((), (), s32[]{:S(2)}) async-start(), calls=%async_computation.16 | async-start | bytes 3538944 | tf_op jit(solution)/shard_map/reduce_scatter | solution.py:262
  954.8 442.7 %reduce-scatter.20.cloned.1.call-start = ((), (), s32[]{:S(2)}) async-start(), calls=%async_computation.19 | async-start | bytes 4718592 | tf_op jit(solution)/shard_map/reduce_scatter | solution.py:265
  970.0 482.7 %reduce-scatter.18.cloned.1.call-start = ((), (), s32[]{:S(2)}) async-start(), calls=%async_computation.18 | async-start | bytes 4718592 | tf_op jit(solution)/shard_map/reduce_scatter | solution.py:264
  986.2 117.6 %copy-start.3 = (bf16[1024,1024]{1,0:T(8,128)(2,1)S(1)}, bf16[1024,1024]{1,0:T(8,128)(2,1)}, u32[]{:S(2)}) copy-start(bf16[1024,1024]{1,0:T(8,128)(2,1)} %param.19) | copy-start | bytes 6291460
  986.2 117.6 %copy-start.25 = (f32[1024]{0:T(1024)S(1)}, f32[1024]{0:T(1024)}, u32[]{:S(2)}) copy-start(f32[1024]{0:T(1024)} %copy-done.24) | copy-start | bytes 12292
  986.2 117.6 %copy-start.27 = (f32[1024]{0:T(1024)S(1)}, f32[1024]{0:T(1024)}, u32[]{:S(2)}) copy-start(f32[1024]{0:T(1024)} %copy-done.26) | copy-start | bytes 12292
  986.2 117.6 %copy-start.29 = (f32[1024]{0:T(1024)S(1)}, f32[1024]{0:T(1024)}, u32[]{:S(2)}) copy-start(f32[1024]{0:T(1024)} %copy-done.28) | copy-start | bytes 12292
  990.5 117.2 %copy-start.34 = (f32[1024]{0:T(1024)S(1)}, f32[1024]{0:T(1024)}, u32[]{:S(2)}) copy-start(f32[1024]{0:T(1024)} %copy-done.33) | copy-start | bytes 12292
  990.5 117.2 %copy-start.32 = (f32[1024]{0:T(1024)S(1)}, f32[1024]{0:T(1024)}, u32[]{:S(2)}) copy-start(f32[1024]{0:T(1024)} %copy-done.31) | copy-start | bytes 12292
  1302.2 151.1 %copy-start.36 = (f32[1024]{0:T(1024)}, f32[1024]{0:T(1024)S(1)}, u32[]{:S(2)}) copy-start(f32[1024]{0:T(1024)S(1)} %get-tuple-element.420) | copy-start | bytes 12292
  (51 other events, 379.5 us)
Sparse Core Ops, SparseCore 0:
  10.5 29.2 all-gather.8
  41.9 149.8 all-gather.6
  193.4 147.8 all-gather.16
  343.0 26.1 all-gather.12
  370.6 149.6 all-gather.10
  522.0 26.4 all-gather.14
  813.5 142.6 reduce-scatter.9
  958.5 145.1 reduce-scatter.11
  1106.1 145.1 reduce-scatter.7
  1254.9 36.7 reduce-scatter.15
  1295.7 46.1 reduce-scatter.13
  1346.1 51.2 reduce-scatter.19
  1401.4 51.3 reduce-scatter.17
where the time goes:
time: 1470 us; the launch traced here: 1460 us
  waiting for transfers between devices  604 us (41%)
  matrix products  392 us (27%)
  local copies, waits for them, and re-layouts  260 us (18%)
  other arithmetic  132 us (9%)
  blocking collectives  56 us (4%)
    dynamic_update_slice x16, local copies, waits for them, and re-layouts, body(): lax.map(partial(attend_block, score_scale=score_scale), (query_seqs, key_...  168 us
    all_gather x1, waiting for transfers between devices, body(): lax.all_gather(attn_normed, 'tp', axis=0, tiled=True)  152 us
    reduce_scatter x1, waiting for transfers between devices, body(): lax.psum_scatter(partial_out.astype(jnp.bfloat16), 'tp', scatter_dimensio...  139 us
    reduce_scatter x1, waiting for transfers between devices, body(): lax.psum_scatter(grad_mlp_normed.astype(jnp.bfloat16), 'tp', scatter_dime...  113 us
    dot_general x8, matrix products, masked_scores(): jnp.einsum('qhd,khd->hqk', queries, key_rows, preferred_element_type=jnp....  68.8 us
    reduce_scatter x1, waiting for transfers between devices, body(): lax.psum_scatter(grad_down_weight, 'fsdp', scatter_dimension=1, tiled=True)  55.5 us
    reduce_scatter x1, waiting for transfers between devices, body(): lax.psum_scatter(grad_up_weight, 'fsdp', scatter_dimension=0, tiled=True)  55.3 us
    convert_element_type x4, other arithmetic, attend_back(): grad_scores = (softmax_rows * (grad_probs - jnp.sum(softmax_rows * grad_p...  54.5 us
  transfers between devices with their start and end apart: 13, of which 7 were waited for; matrix products, arithmetic and copies ran while one was open for 53% of the time, Pallas kernels for 0%

commit v1 on v0

v1 whole, which is shorter than its diff:
```python
from functools import partial
import math

import jax
import jax.numpy as jnp
from jax import lax
from jax.experimental import pallas as pl
from jax.experimental.pallas import tpu as pltpu
from jax.sharding import PartitionSpec as P

HD = 64
ROT = 16
EPS = 1e-05
MASKED = 1e30
F32 = jnp.float32
BF16 = jnp.bfloat16
VMEM_BYTES = 56 * 1024 * 1024
NT = (((1,), (1,)), ((), ()))
TN = (((0,), (0,)), ((), ()))
NN = (((1,), (0,)), ((), ()))

dot32 = partial(lax.dot_general, preferred_element_type=F32)


def attention_kernel(
    mixed_ref, dout_ref, cos_ref, sa_ref, sb_ref, qf_ref, kf_ref, att_ref, dmix_ref, dk_scr, dv_scr, *, bq
):
    length = mixed_ref.shape[0]
    width = 2 * HD
    cos, sa, sb = cos_ref[...], sa_ref[...], sb_ref[...]
    scale = 1.0 / math.sqrt(HD)
    half = ROT // 2

    def turn(v, c, a, b, sign):
        side = pltpu.roll(v, width - half, 1) * a + pltpu.roll(v, half, 1) * b
        return v * c + side if sign > 0 else v * c - side

    q = turn(mixed_ref[:, 0:width], cos, sa, sb, 1).astype(BF16)
    k = turn(mixed_ref[:, width : 2 * width], cos, sa, sb, 1).astype(BF16)
    v = mixed_ref[:, 2 * width : 3 * width].astype(BF16)
    do = dout_ref[...]
    lane = lax.broadcasted_iota(jnp.int32, (length, width), 1)
    zero = jnp.zeros((), BF16)
    qs = (q.astype(F32) * scale).astype(BF16)
    qf = qf_ref[...]
    kaug = jnp.concatenate([k, kf_ref[...]], axis=1)
    heads = []
    for h in range(2):
        m = (lane // HD) == h
        qm = jnp.where(m, qs, zero)
        heads.append(
            (
                jnp.concatenate([qm, qf], axis=1),
                qm,
                jnp.where(m, k, zero),
                jnp.where(m, v, zero),
                jnp.where(m, do, zero),
            )
        )
    causal = lax.broadcasted_iota(jnp.int32, (bq, bq), 1) <= lax.broadcasted_iota(jnp.int32, (bq, bq), 0)
    blocks = length // bq
    for i in range(blocks):
        r0 = i * bq
        w = r0 + bq
        att = dq = dkp = dvp = None
        for qaug, qm, km, vm, dom in heads:
            s = dot32(qaug[r0:w], kaug[:w], NT)
            diagonal = jnp.where(causal, s[:, r0:], -MASKED)
            s = diagonal if i == 0 else jnp.concatenate([s[:, :r0], diagonal], axis=1)
            e = jnp.exp(s - jnp.max(s, axis=1, keepdims=True))
            p = e * (1.0 / jnp.sum(e, axis=1, keepdims=True))
            pb = p.astype(BF16)
            o = dot32(pb, vm[:w], NN)
            dp = dot32(dom[r0:w], v[:w], NT)
            delta = jnp.sum(p * dp, axis=1, keepdims=True)
            ds = (p * (dp - delta)).astype(BF16)
            x = dot32(ds, km[:w], NN)
            a = dot32(pb, dom[r0:w], TN)
            b = dot32(ds, qm[r0:w], TN)
            if att is None:
                att, dq, dvp, dkp = o, x, a, b
            else:
                att, dq, dvp, dkp = att + o, dq + x, dvp + a, dkp + b
        att_ref[r0:w, :] = att.astype(BF16)
        dmix_ref[r0:w, 0:width] = turn(dq * scale, cos[r0:w], sa[r0:w], sb[r0:w], -1).astype(BF16)
        if i > 0:
            dk_scr[:r0] += dkp[:r0]
            dv_scr[:r0] += dvp[:r0]
        dk_scr[r0:w] = dkp[r0:]
        dv_scr[r0:w] = dvp[r0:]
    dmix_ref[:, width : 2 * width] = turn(dk_scr[...], cos, sa, sb, -1).astype(BF16)
    dmix_ref[:, 2 * width : 3 * width] = dv_scr[...].astype(BF16)


def attention(mixed, dout, tables, length):
    rows = mixed.shape[0]
    width = 2 * HD
    pairs = dout.shape[1] // width
    seqs = rows // length
    bq = min(512, length)
    table = pl.BlockSpec((length, width), lambda s, j: (s, 0))
    units = seqs * pairs
    return pl.pallas_call(
        partial(attention_kernel, bq=bq),
        grid=(seqs, pairs),
        in_specs=[
            pl.BlockSpec((length, 3 * width), lambda s, j: (s, j)),
            pl.BlockSpec((length, width), lambda s, j: (s, j)),
        ]
        + [table] * 5,
        out_specs=[
            pl.BlockSpec((length, width), lambda s, j: (s, j)),
            pl.BlockSpec((length, 3 * width), lambda s, j: (s, j)),
        ],
        out_shape=[
            jax.ShapeDtypeStruct((rows, pairs * width), BF16),
            jax.ShapeDtypeStruct((rows, pairs * 3 * width), BF16),
        ],
        scratch_shapes=[pltpu.VMEM((length, width), F32), pltpu.VMEM((length, width), F32)],
        compiler_params=pltpu.CompilerParams(vmem_limit_bytes=VMEM_BYTES),
        cost_estimate=pl.CostEstimate(
            flops=units * 24 * length * length * width,
            bytes_accessed=units * length * width * 40,
            transcendentals=units * 2 * length * length,
        ),
        name="attention",
    )(mixed, dout, *tables)


def mlp_kernel(mn_ref, dy_ref, up_ref, bias_ref, down_ref, act_ref, dgate_ref, sum_ref):
    gate = dot32(mn_ref[...], up_ref[...], NN) + bias_ref[...]
    dact = dot32(dy_ref[...], down_ref[...], NT)
    cdf = 0.5 + 0.5 * lax.erf(gate * math.sqrt(0.5))
    pdf = jnp.exp(gate * gate * -0.5) * (1.0 / math.sqrt(2.0 * math.pi))
    act_ref[...] = (gate * cdf).astype(BF16)
    dgate = (dact * (cdf + gate * pdf)).astype(BF16)
    dgate_ref[...] = dgate
    part = jnp.sum(dgate.astype(F32), axis=0, keepdims=True)

    @pl.when(pl.program_id(1) == 0)
    def _():
        sum_ref[...] = part

    @pl.when(pl.program_id(1) > 0)
    def _():
        sum_ref[...] += part


def mlp_front(mn, dy, up, bias, down):
    rows, depth = mn.shape
    units = up.shape[1]
    br, bc = min(512, rows), min(512, units)
    row = pl.BlockSpec((br, depth), lambda c, r: (r, 0))
    tile = pl.BlockSpec((br, bc), lambda c, r: (r, c))
    return pl.pallas_call(
        mlp_kernel,
        grid=(units // bc, rows // br),
        in_specs=[
            row,
            row,
            pl.BlockSpec((depth, bc), lambda c, r: (0, c)),
            pl.BlockSpec((1, bc), lambda c, r: (0, c)),
            pl.BlockSpec((bc, depth), lambda c, r: (c, 0)),
        ],
        out_specs=[tile, tile, pl.BlockSpec((1, bc), lambda c, r: (0, c))],
        out_shape=[
            jax.ShapeDtypeStruct((rows, units), BF16),
            jax.ShapeDtypeStruct((rows, units), BF16),
            jax.ShapeDtypeStruct((1, units), F32),
        ],
        compiler_params=pltpu.CompilerParams(vmem_limit_bytes=VMEM_BYTES),
        cost_estimate=pl.CostEstimate(
            flops=4 * rows * depth * units,
            bytes_accessed=(units // bc) * rows * depth * 4 + units * depth * 4 + rows * units * 4,
            transcendentals=2 * rows * units,
        ),
        name="mlp_front",
    )(mn, dy, up, bias, down)


class Links:
    def __init__(self):
        self.fsdp = lax.axis_size("fsdp")
        self.tp = lax.axis_size("tp")
        index = lax.axis_index("fsdp")
        self.core = index % 2
        self.place = index // 2
        self.lane = lax.axis_index("tp")
        self.places = self.fsdp // 2
        self.cores = [list(range(c, self.fsdp, 2)) for c in range(2)]
        self.bits = [1 << b for b in range((self.places - 1).bit_length())]

    def swap(self, value):
        return lax.ppermute(value, "fsdp", [(i, i ^ 1) for i in range(self.fsdp)])

    def hop(self, value, bit):
        return lax.ppermute(value, "fsdp", [(i, i ^ (2 * bit)) for i in range(self.fsdp)])

    def ring(self, value):
        return lax.ppermute(value, "tp", [(i, (i + 1) % self.tp) for i in range(self.tp)])

    def gather_places(self, piece, axis):
        size = piece.shape[axis]
        found = {0: piece}
        if self.places == 4:
            found[1] = self.hop(piece, 1)
            found[2] = self.hop(piece, 2)
            cut = piece.shape[1 - axis] // 2
            first = lax.slice_in_dim(found[2], 0, cut, axis=1 - axis)
            second = lax.slice_in_dim(found[1], cut, 2 * cut, axis=1 - axis)
            found[3] = (self.hop(first, 1), self.hop(second, 2))
        else:
            return lax.all_gather(piece, "fsdp", axis=axis, tiled=True, axis_index_groups=self.cores)
        shape = list(piece.shape)
        shape[axis] = size * self.places
        whole = jnp.zeros(shape, piece.dtype)
        for key, block in found.items():
            start = (self.place ^ key) * size
            at = [0, 0]
            at[axis] = start
            if isinstance(block, tuple):
                whole = lax.dynamic_update_slice(whole, block[0], tuple(at))
                at[1 - axis] = block[0].shape[1 - axis]
                whole = lax.dynamic_update_slice(whole, block[1], tuple(at))
            else:
                whole = lax.dynamic_update_slice(whole, block, tuple(at))
        return whole

    def scatter_places(self, whole, axis):
        size = whole.shape[axis] // self.places

        def block(key):
            return lax.dynamic_slice_in_dim(whole, (self.place ^ key) * size, size, axis)

        if self.places == 4:
            cut = whole.shape[1 - axis] // 2
            far = block(3)
            first = self.hop(lax.slice_in_dim(far, 0, cut, axis=1 - axis), 2)
            second = self.hop(lax.slice_in_dim(far, cut, 2 * cut, axis=1 - axis), 1)
            near = block(1)
            left = lax.slice_in_dim(near, 0, cut, axis=1 - axis).astype(F32) + first.astype(F32)
            one = jnp.concatenate(
                [left.astype(BF16), lax.slice_in_dim(near, cut, 2 * cut, axis=1 - axis)], axis=1 - axis
            )
            near = block(2)
            right = lax.slice_in_dim(near, cut, 2 * cut, axis=1 - axis).astype(F32) + second.astype(F32)
            two = jnp.concatenate(
                [lax.slice_in_dim(near, 0, cut, axis=1 - axis), right.astype(BF16)], axis=1 - axis
            )
            return block(0).astype(F32) + self.hop(one, 1).astype(F32) + self.hop(two, 2).astype(F32)
        return lax.psum_scatter(
            whole, "fsdp", scatter_dimension=axis, tiled=True, axis_index_groups=self.cores
        ).astype(F32)

    def scatter_lanes(self, slots):
        total = None
        for step in range(1, self.tp):
            total = slots[step] if total is None else total + slots[step]
            total = self.ring(total.astype(BF16)).astype(F32)
        return slots[0] if total is None else total + slots[0]

    def total(self, value):
        for bit in [1] + [2 * b for b in self.bits]:
            value = value + lax.ppermute(value, "fsdp", [(i, i ^ bit) for i in range(self.fsdp)])
        bit = 1
        while bit < self.tp:
            value = value + lax.ppermute(value, "tp", [(i, i ^ bit) for i in range(self.tp)])
            bit *= 2
        return value


def pick(value, index, axis):
    return lax.dynamic_index_in_dim(value, index, axis, keepdims=False)


def pair_blocks(links, shard, split_axis, join_axis):
    half = shard.shape[split_axis] // 2
    mine = lax.dynamic_slice_in_dim(shard, links.core * half, half, split_axis)
    other = links.swap(lax.dynamic_slice_in_dim(shard, (1 - links.core) * half, half, split_axis))
    first = jnp.where(links.core == 0, mine, other)
    second = jnp.where(links.core == 0, other, mine)
    return jnp.concatenate([first, second], axis=join_axis)


def unpair_blocks(links, block, split_axis, join_axis):
    half = block.shape[join_axis] // 2
    mine = lax.dynamic_slice_in_dim(block, links.core * half, half, join_axis)
    other = links.swap(lax.dynamic_slice_in_dim(block, (1 - links.core) * half, half, join_axis))
    first = jnp.where(links.core == 0, mine, other)
    second = jnp.where(links.core == 0, other, mine)
    return jnp.concatenate([first, second], axis=split_axis)


def tables_of(segment_rows):
    seqs, length = segment_rows.shape
    width = 2 * HD
    starts = jnp.sum((segment_rows[:, None, :] < segment_rows[:, :, None]).astype(jnp.int32), axis=-1)
    places = (jnp.arange(length, dtype=jnp.int32)[None] - starts).reshape(-1).astype(F32)
    inverse_freq = jnp.power(10000.0, -jnp.arange(0, ROT, 2, dtype=F32) / ROT)
    angles = places[:, None] * jnp.tile(inverse_freq, width // (ROT // 2))[None, :]
    lane = jnp.arange(width, dtype=jnp.int32)[None, :]
    turn = lane % HD
    cos = jnp.where(turn < ROT, jnp.cos(angles), 1.0)
    sine = jnp.sin(angles)
    sa = jnp.where(turn < ROT // 2, -sine, 0.0)
    sb = jnp.where((turn >= ROT // 2) & (turn < ROT), sine, 0.0)
    same = segment_rows.reshape(-1, 1) == lane
    key_mark = jnp.where(same, 1.0, 0.0).astype(BF16)
    query_mark = jnp.where(same | (lane >= 8), 0.0, -MASKED).astype(BF16)
    return cos, sa, sb, query_mark, key_mark


def body(
    tokens,
    segments,
    attn_gain,
    attn_shift,
    mlp_gain,
    mlp_shift,
    qkv_weight,
    qkv_bias,
    out_weight,
    out_bias,
    up_weight,
    up_bias,
    down_weight,
    down_bias,
    cotangent,
):
    links = Links()
    tp = links.tp
    rows, depth = tokens.shape
    length = segments.shape[1]
    head_cols = qkv_weight.shape[2] // 2
    unit_cols = up_weight.shape[1] // 2

    x2 = jnp.concatenate([tokens, links.swap(tokens)], axis=0)
    dy2 = jnp.concatenate([cotangent, links.swap(cotangent)], axis=0)
    own_segments = lax.dynamic_slice_in_dim(segments, links.lane * rows // length, rows // length, 0)
    tables = tables_of(jnp.concatenate([own_segments, links.swap(own_segments)], axis=0))

    qkv_piece = pair_blocks(links, qkv_weight, 2, 0)
    qkv_piece = qkv_piece.reshape(qkv_piece.shape[0], 3 * head_cols)
    out_piece = pair_blocks(links, out_weight, 0, 1)
    up_piece = pair_blocks(links, up_weight, 1, 0)
    down_piece = pair_blocks(links, down_weight, 0, 1)
    qkv_slots = [links.gather_places(qkv_piece, 0)]
    out_slots = [links.gather_places(out_piece, 1)]
    up_slots, down_slots = [up_piece], [down_piece]
    for _ in range(tp - 1):
        qkv_slots.append(links.ring(qkv_slots[-1]))
        out_slots.append(links.ring(out_slots[-1]))
        up_slots.append(links.ring(up_slots[-1]))
        down_slots.append(links.ring(down_slots[-1]))
    half = tp // 2
    per = max(1, 2 * HD // head_cols)

    def join_heads(slots):
        if per == 1:
            return jnp.concatenate(slots, axis=1)
        lead = slots[0].shape[0]
        blocks = [
            jnp.concatenate([v.reshape(lead, 3, head_cols) for v in slots[i : i + per]], axis=2).reshape(lead, -1)
            for i in range(0, len(slots), per)
        ]
        return jnp.concatenate(blocks, axis=1)

    def split_heads(joined):
        lead = joined.shape[0]
        blocks = joined.reshape(lead, -1, 3, per, head_cols)
        return [blocks[:, i, :, j] for i in range(blocks.shape[1]) for j in range(per)]

    groups = [list(range(0, half)), list(range(half, tp))]
    qkv_groups = [join_heads([qkv_slots[s] for s in g]) for g in groups]
    out_groups = [jnp.concatenate([out_slots[s] for s in g], axis=0) for g in groups]
    up_groups = [links.gather_places(jnp.concatenate([up_slots[s] for s in g], axis=1), 0) for g in groups]
    down_groups = [links.gather_places(jnp.concatenate([down_slots[s] for s in g], axis=0), 1) for g in groups]

    lane_of = [(links.lane - s) % tp for s in range(tp)]
    qkv_bias_lanes = pick(qkv_bias.reshape(3, tp, 2, head_cols), links.core, 2)
    up_bias_lanes = pick(up_bias.reshape(tp, 2, unit_cols), links.core, 1)
    qkv_bias_groups = [
        join_heads([pick(qkv_bias_lanes, lane_of[s], 1).reshape(1, -1) for s in g]).astype(F32) for g in groups
    ]
    up_bias_groups = [
        jnp.concatenate([pick(up_bias_lanes, lane_of[s], 0) for s in g]).astype(F32)[None] for g in groups
    ]

    x = x2.astype(F32)
    centre = x - jnp.mean(x, axis=-1, keepdims=True)
    rstd = lax.rsqrt(jnp.mean(centre * centre, axis=-1, keepdims=True) + EPS)
    xhat = centre * rstd
    gains = [v.astype(F32) for v in (attn_gain, attn_shift, mlp_gain, mlp_shift)]
    attn_normed = (xhat * gains[0] + gains[1]).astype(BF16)
    mlp_normed = (xhat * gains[2] + gains[3]).astype(BF16)

    def attention_part(g, normed, dy):
        mixed = dot32(normed, qkv_groups[g], NN) + qkv_bias_groups[g]
        dout = dot32(dy, out_groups[g], NT).astype(BF16)
        attended, dmixed = attention(mixed, dout, tables, length)
        return attended, dmixed

    def mlp_part(g, normed, dy):
        active, dgate, gate_sum = mlp_front(normed, dy, up_groups[g], up_bias_groups[g], down_groups[g])
        grad_up = dot32(normed, dgate, TN).astype(BF16)
        grad_down = dot32(active, dy, TN).astype(BF16)
        return active, dgate, gate_sum, grad_up, grad_down

    att0, dmix0 = attention_part(0, attn_normed, dy2)
    mlp_in, dy_mlp, att0, dmix0 = lax.optimization_barrier((mlp_normed, dy2, att0, dmix0))
    mlp = [mlp_part(g, mlp_in, dy_mlp) for g in range(2)]
    grad_qkv0 = dot32(attn_normed, dmix0, TN).astype(BF16)
    grad_out0 = dot32(att0, dy2, TN).astype(BF16)
    normed1, dy1, mlp = lax.optimization_barrier((attn_normed, dy2, mlp))
    att1, dmix1 = attention_part(1, normed1, dy1)
    grad_qkv1 = dot32(attn_normed, dmix1, TN).astype(BF16)
    grad_out1 = dot32(att1, dy2, TN).astype(BF16)

    def finish(parts, axis, split):
        slots = []
        for part in parts:
            slots += split(links.scatter_places(part, axis))
        return links.scatter_lanes(slots)

    def split_cols(piece):
        return jnp.split(piece, half, axis=1)

    def split_rows(piece):
        return jnp.split(piece, half, axis=0)

    up_grad = unpair_blocks(links, finish([mlp[0][3], mlp[1][3]], 0, split_cols), 1, 0)
    down_grad = unpair_blocks(links, finish([mlp[0][4], mlp[1][4]], 1, split_rows), 0, 1)
    qkv_grad = unpair_blocks(links, finish([grad_qkv0, grad_qkv1], 0, split_heads), 2, 0)
    out_grad = unpair_blocks(links, finish([grad_out0, grad_out1], 1, split_rows), 0, 1)

    partial_out = (
        dot32(mlp[0][0], down_groups[0], NN)
        + dot32(mlp[1][0], down_groups[1], NN)
        + dot32(jnp.concatenate([att0, att1], axis=1), jnp.concatenate(out_groups, axis=0), NN)
    )
    other_out = links.swap(partial_out[rows:].astype(BF16))
    output = (
        tokens.astype(F32)
        + partial_out[:rows]
        + other_out.astype(F32)
        + out_bias.astype(F32)
        + down_bias.astype(F32)
    ).astype(BF16)

    n_mlp = dot32(mlp[0][1], up_groups[0], NT) + dot32(mlp[1][1], up_groups[1], NT)
    n_attn = dot32(dmix0, qkv_groups[0], NT) + dot32(dmix1, qkv_groups[1], NT)
    pulled = n_attn * gains[0] + n_mlp * gains[2]
    other_pull = links.swap(pulled[rows:].astype(BF16))
    whole = pulled[:rows] + other_pull.astype(F32)
    own_hat = xhat[:rows]
    input_grad = cotangent.astype(F32) + rstd[:rows] * (
        whole
        - jnp.mean(whole, axis=-1, keepdims=True)
        - own_hat * jnp.mean(whole * own_hat, axis=-1, keepdims=True)
    )

    def spread(values):
        lead, cols = values[0].shape
        full = jnp.zeros((lead, tp, 2, cols), F32)
        for s, value in enumerate(values):
            full = lax.dynamic_update_slice(full, value.reshape(lead, 1, 1, cols), (0, lane_of[s], links.core, 0))
        return full.reshape(-1)

    qkv_sums = [jnp.sum(d.astype(F32), axis=0, keepdims=True) for d in (dmix0, dmix1)]
    qkv_bias_part = spread([v[0] for d in qkv_sums for v in split_heads(d)])
    up_bias_part = spread([v for part in mlp for v in jnp.split(part[2], half, axis=1)])
    bias_part = jnp.sum(cotangent.astype(F32), axis=0)
    pieces = [
        jnp.sum(n_attn * xhat, axis=0),
        jnp.sum(n_attn, axis=0),
        jnp.sum(n_mlp * xhat, axis=0),
        jnp.sum(n_mlp, axis=0),
        qkv_bias_part,
        bias_part,
        up_bias_part,
    ]
    sizes = [v.shape[0] for v in pieces]
    summed = links.total(jnp.concatenate(pieces).reshape(-1, 128)).reshape(-1)
    sums = []
    at = 0
    for size in sizes:
        sums.append(summed[at : at + size])
        at += size
    return (
        output,
        input_grad,
        sums[0],
        sums[1],
        sums[2],
        sums[3],
        qkv_grad,
        sums[4].reshape(qkv_bias.shape),
        out_grad,
        sums[5],
        up_grad,
        sums[6],
        down_grad,
        sums[5],
    )


def solution(mesh):
    placed = (
        P(("fsdp", "tp"), None),
        P("fsdp", None),
        P(),
        P(),
        P(),
        P(),
        P("fsdp", None, "tp"),
        P(),
        P("tp", "fsdp"),
        P(),
        P("fsdp", "tp"),
        P(),
        P("tp", "fsdp"),
        P(),
        P(("fsdp", "tp"), None),
    )
    return jax.shard_map(
        body,
        mesh=mesh,
        in_specs=placed,
        out_specs=(
            P(("fsdp", "tp"), None),
            P(("fsdp", "tp"), None),
            P(),
            P(),
            P(),
            P(),
            P("fsdp", None, "tp"),
            P(),
            P("tp", "fsdp"),
            P(),
            P("fsdp", "tp"),
            P(),
            P("tp", "fsdp"),
            P(),
        ),
        check_vma=False,
    )
```

time: 1470 us -> 567 us (0.39)
  waiting for transfers between devices: 604 us -> 174 us
  matrix products: 392 us -> 116 us
  local copies, waits for them, and re-layouts: 260 us -> 37.4 us
  Pallas kernels: 0 us -> 93.5 us
  starting transfers between devices: 0.99 us -> 77.4 us
  other arithmetic: 132 us -> 58.1 us
  blocking collectives: 56 us -> 0 us
    reduce_scatter x7 -> x0, waiting for transfers between devices: 403 us -> none  [the longest x1 139 us: body(): lax.psum_scatter(partial_out.astype(jnp.bfloat16), 'tp', scatter_dimensio...]
    dot_general x40 -> x19, matrix products: 392 us -> 116 us  [the longest x2 21.5 us: body(): n_attn = dot32(dmix0, qkv_groups[0], NT) + dot32(dmix1, qkv_groups[1], NT)]
    all_gather x6 -> x0, waiting for transfers between devices: 199 us -> none  [the longest x1 152 us: body(): lax.all_gather(attn_normed, 'tp', axis=0, tiled=True)]
    ppermute x0 -> x98, waiting for transfers between devices: none -> 174 us  [the longest x24 90.4 us: ring(): lax.ppermute(value, 'tp', [(i, (i + 1) % self.tp) for i in range(self.tp)])]
    dynamic_update_slice x18 -> x35, local copies, waits for them, and re-layouts: 169 us -> 1.18 us  [the longest x15 0.62 us: gather_places(): whole = lax.dynamic_update_slice(whole, block, tuple(at))]
    pallas_call x0 -> x4, Pallas kernels: none -> 93.5 us  [the longest x2 59.3 us: attention(): pl.pallas_call(partial(attention_kernel, bq=bq), grid=(seqs, pairs), in_s...]
    ppermute x0 -> x98, starting transfers between devices: none -> 77.4 us  [the longest x56 60.2 us: hop(): lax.ppermute(value, 'fsdp', [(i, i ^ 2 * bit) for i in range(self.fsdp)])]
    convert_element_type x15 -> x29, other arithmetic: 74 us -> 23.1 us  [the longest x8 7.15 us: scatter_places(): left.astype(BF16)]
  transfers between devices with their start and end apart: 13 -> 98, of which waited for: 7 -> 47; matrix products, arithmetic and copies ran while one was open for 53% -> 36% of each run, Pallas kernels for 0% -> 17%
where the time goes in v1:
time: 567 us; the launch traced here: 560 us
  waiting for transfers between devices  174 us (31%)
  matrix products  116 us (20%)
  Pallas kernels  93.5 us (16%)
  starting transfers between devices  77.4 us (14%)
  other arithmetic  58.1 us (10%)
  local copies, waits for them, and re-layouts  37.4 us (7%)
    ppermute x24, waiting for transfers between devices, ring(): lax.ppermute(value, 'tp', [(i, (i + 1) % self.tp) for i in range(self.tp)])  90.4 us
    ppermute x56, waiting for transfers between devices, hop(): lax.ppermute(value, 'fsdp', [(i, i ^ 2 * bit) for i in range(self.fsdp)])  74.8 us
    ppermute x56, starting transfers between devices, hop(): lax.ppermute(value, 'fsdp', [(i, i ^ 2 * bit) for i in range(self.fsdp)])  60.2 us
    pallas_call x2, Pallas kernels, attention(): pl.pallas_call(partial(attention_kernel, bq=bq), grid=(seqs, pairs), in_s...  59.3 us
    pallas_call x2, Pallas kernels, mlp_front(): pl.pallas_call(mlp_kernel, grid=(units // bc, rows // br), in_specs=[row,...  34.2 us
    dot_general x2, matrix products, body(): n_attn = dot32(dmix0, qkv_groups[0], NT) + dot32(dmix1, qkv_groups[1], NT)  21.5 us
    dot_general x2, matrix products, mlp_part(): grad_down = dot32(active, dy, TN).astype(BF16)  16.6 us
    unnamed x225, local copies, waits for them, and re-layouts  13.2 us
  transfers between devices with their start and end apart: 98, of which 47 were waited for; matrix products, arithmetic and copies ran while one was open for 36% of the time, Pallas kernels for 17%

profile of v1, /device:TPU:0, one launch (start us, length us, event | category | flops | bytes accessed | tf_op | source)
XLA Modules:
  0.0 559.7 jit_solution(7301787920408267975)
XLA Ops:
  14.0 5.9 %fusion.10 = (f32[2048,128]{1,0:T(8,128)}, f32[2048,128]{1,0:T(8,128)}, f32[2048,128]{1,0:T(8,128)}) fusion(f32[128]{0:T(128)S(1)} %mul.80, f32[2048]{0:T(1024)S(1)} %bitcast.144, pred[128]{0:T(512)(128)(4,1)S(1)} %get-tuple-element.208, pred[128]{0:T(512)(128)(4,1)S(1)} %get-tuple-element.209, pred[128]{0:T(512)(128)(4,1)S(1)} %broadcast_compare_fusion.1), kind=kLoop, calls=%fused_computation.44 | loop fusion | flops 1310720 | bytes 3154816 | tf_op jit(solution)/shard_map/jit(_where)/select_n | solution.py:306
  50.7 8.7 %collective-permute-done.33 = bf16[512,256]{1,0:T(8,128)(2,1)S(1)} collective-permute-done((bf16[512,256]{1,0:T(8,128)(2,1)S(1)}, bf16[512,256]{1,0:T(8,128)(2,1)S(1)}, u32[]{:S(2)}, u32[]{:S(2)}) %collective-permute-start.33) | collective-permute-done | bytes 262176 | tf_op jit(solution)/shard_map/ppermute | solution.py:200
  70.3 7.1 %collective-permute-done.28 = bf16[256,512]{1,0:T(8,128)(2,1)S(1)} collective-permute-done((bf16[256,512]{1,0:T(8,128)(2,1)S(1)}, bf16[256,512]{1,0:T(8,128)(2,1)S(1)}, u32[]{:S(2)}, u32[]{:S(2)}) %collective-permute-start.28) | collective-permute-done | bytes 262176 | tf_op jit(solution)/shard_map/ppermute | solution.py:200
  91.9 8.7 %collective-permute-done.20 = bf16[256,512]{1,0:T(8,128)(2,1)S(1)} collective-permute-done((bf16[256,512]{1,0:T(8,128)(2,1)S(1)}, bf16[256,512]{1,0:T(8,128)(2,1)S(1)}, u32[]{:S(2)}, u32[]{:S(2)}) %collective-permute-start.20) | collective-permute-done | bytes 262176 | tf_op jit(solution)/shard_map/ppermute | solution.py:197
  105.8 10.0 %collective-permute-done.29 = bf16[256,1024]{1,0:T(8,128)(2,1)S(1)} collective-permute-done((bf16[256,1024]{1,0:T(8,128)(2,1)S(1)}, bf16[256,1024]{1,0:T(8,128)(2,1)S(1)}, u32[]{:S(2)}, u32[]{:S(2)}) %collective-permute-start.29) | collective-permute-done | bytes 524320 | tf_op jit(solution)/shard_map/ppermute | solution.py:197
  129.5 8.7 %collective-permute-done.39 = bf16[1024,384]{0,1:T(8,128)(2,1)} collective-permute-done((bf16[1024,384]{0,1:T(8,128)(2,1)S(1)}, bf16[1024,384]{0,1:T(8,128)(2,1)}, u32[]{:S(2)}, u32[]{:S(2)}) %collective-permute-start.39) | collective-permute-done | bytes 786464 | tf_op jit(solution)/shard_map/ppermute | solution.py:200
  157.2 29.7 %attention.2 = (bf16[2048,256]{1,0:T(8,128)(2,1)}, bf16[2048,768]{1,0:T(8,128)(2,1)}) custom-call(f32[2048,768]{1,0:T(8,128)} %convolution_add_fusion.3.mixed_ref, bf16[2048,256]{1,0:T(8,128)(2,1)} %convolution_convert_fusion.1.dout_ref, f32[2048,128]{1,0:T(8,128)} %get-tuple-element.187.cos_ref, f32[2048,128]{1,0:T(8,128)} %get-tuple-element.186.sa_ref, ...), custom_call_target="tpu_custom_call" | custom-call | flops 12884901888 | bytes 20971520 | tf_op jit(solution)/shard_map/attention/pallas_call | solution.py:103
  186.9 6.7 %convolution_convert_fusion.7 = bf16[1024,768]{0,1:T(8,128)(2,1)} fusion(bf16[2048,1024]{1,0:T(8,128)(2,1)S(1)} %get-tuple-element.53, bf16[2048,768]{1,0:T(8,128)(2,1)} %get-tuple-element.56), kind=kOutput, calls=%fused_computation.40 | convolution fusion | flops 3222011904 | bytes 8912896 | tf_op jit(solution)/shard_map/dot_general | solution.py:412
  194.1 17.1 %mlp_front.3 = (bf16[2048,1024]{1,0:T(8,128)(2,1)}, bf16[2048,1024]{1,0:T(8,128)(2,1)}, f32[1,1024]{1,0:T(1,128)}) custom-call(bf16[2048,1024]{1,0:T(8,128)(2,1)} %get-tuple-element.42.mn_ref, bf16[2048,1024]{1,0:T(8,128)(2,1)} %copy-done.36, bf16[1024,1024]{1,0:T(8,128)(2,1)} %copy-done.22, f32[1,1024]{1,0:T(1,128)} %maximum_convert_fusion.1.bias_ref, ...), custom_call_target="tpu_custom_call" | custom-call | flops 8589934592 | bytes 29360128 | tf_op jit(solution)/shard_map/mlp_front/pallas_call | solution.py:155
  211.2 9.5 %convolution_convert_fusion.2 = bf16[1024,1024]{1,0:T(8,128)(2,1)} fusion(bf16[2048,1024]{1,0:T(8,128)(2,1)} %get-tuple-element.51, bf16[2048,1024]{1,0:T(8,128)(2,1)} %copy-done.36), kind=kOutput, calls=%fused_computation.35 | convolution fusion | flops 4296015872 | bytes 10485760 | tf_op jit(solution)/shard_map/dot_general | solution.py:406
  226.6 17.1 %mlp_front.2 = (bf16[2048,1024]{1,0:T(8,128)(2,1)}, bf16[2048,1024]{1,0:T(8,128)(2,1)}, f32[1,1024]{1,0:T(1,128)}) custom-call(bf16[2048,1024]{1,0:T(8,128)(2,1)} %get-tuple-element.42.mn_ref, bf16[2048,1024]{1,0:T(8,128)(2,1)} %copy-done.36, bf16[1024,1024]{1,0:T(8,128)(2,1)} %copy-done.20, f32[1,1024]{1,0:T(1,128)} %maximum_convert_fusion.bias_ref, ...), custom_call_target="tpu_custom_call" | custom-call | flops 8589934592 | bytes 29360128 | tf_op jit(solution)/shard_map/mlp_front/pallas_call | solution.py:155
  243.7 7.1 %convolution_convert_fusion.4 = bf16[1024,1024]{1,0:T(8,128)(2,1)S(1)} fusion(bf16[2048,1024]{1,0:T(8,128)(2,1)} %get-tuple-element.50, bf16[2048,1024]{1,0:T(8,128)(2,1)S(1)} %copy-done.37), kind=kOutput, calls=%fused_computation.37 | convolution fusion | flops 4296015872 | bytes 10485760 | tf_op jit(solution)/shard_map/dot_general | solution.py:406
  265.3 7.1 %fusion.60 = f32[2048,1024]{1,0:T(8,128)S(1)} fusion(bf16[2048,1024]{1,0:T(8,128)(2,1)} %get-tuple-element.59, bf16[1024,1024]{1,0:T(8,128)(2,1)} %copy-done.22), kind=kOutput, calls=%fused_computation.293 | convolution fusion | flops 4294967296 | bytes 14680064 | tf_op jit(solution)/shard_map/dot_general | solution.py:450
  272.5 6.7 %fusion.59 = f32[2048,1024]{1,0:T(8,128)} fusion(bf16[2048,1024]{1,0:T(8,128)(2,1)S(1)} %copy-done.95, bf16[1024,1024]{1,0:T(8,128)(2,1)S(1)} %copy-done.24), kind=kOutput, calls=%fused_computation.292 | convolution fusion | flops 4294967296 | bytes 14680064 | tf_op jit(solution)/shard_map/dot_general | solution.py:438
  279.2 6.8 %fusion.58 = f32[2048,1024]{1,0:T(8,128)} fusion(bf16[2048,1024]{1,0:T(8,128)(2,1)S(1)} %copy-done.99, bf16[1024,1024]{1,0:T(8,128)(2,1)S(1)} %copy-done.19), kind=kOutput, calls=%fused_computation.291 | convolution fusion | flops 4294967296 | bytes 14680064 | tf_op jit(solution)/shard_map/dot_general | solution.py:437
  286.0 7.4 %convolution_add_fusion = f32[2048,1024]{1,0:T(8,128)} fusion(f32[2048,1024]{1,0:T(8,128)S(1)} %fusion.60, bf16[2048,1024]{1,0:T(8,128)(2,1)S(1)} %copy-done.98, bf16[1024,1024]{1,0:T(8,128)(2,1)S(1)} %copy-done.21), kind=kOutput, calls=%fused_computation.26 | convolution fusion | flops 4297064448 | bytes 23068672 | tf_op jit(solution)/shard_map/dot_general | solution.py:450
  293.4 5.9 %fusion.23 = f32[2048,1024]{1,0:T(8,128)} fusion(bf16[2048,768]{1,0:T(8,128)(2,1)S(1)} %copy-done.12, bf16[1024,384]{0,1:T(8,128)(2,1)S(1)} %copy-done.94, bf16[1024,384]{0,1:T(8,128)(2,1)S(1)} %copy-done.48), kind=kOutput, calls=%fused_computation.66 | convolution fusion | flops 3224371200 | bytes 13107200 | tf_op jit(solution)/shard_map/dot_general | solution.py:451
  357.3 29.7 %attention.3 = (bf16[2048,256]{1,0:T(8,128)(2,1)}, bf16[2048,768]{1,0:T(8,128)(2,1)}) custom-call(f32[2048,768]{1,0:T(8,128)} %convolution_add_fusion.2.mixed_ref, bf16[2048,256]{1,0:T(8,128)(2,1)} %convolution_convert_fusion.dout_ref, f32[2048,128]{1,0:T(8,128)} %get-tuple-element.187.cos_ref, f32[2048,128]{1,0:T(8,128)} %get-tuple-element.186.sa_ref, ...), custom_call_target="tpu_custom_call" | custom-call | flops 12884901888 | bytes 20971520 | tf_op jit(solution)/shard_map/attention/pallas_call | solution.py:103
  398.2 15.7 %fusion.56 = (f32[1024]{0:T(1024)}, f32[1024]{0:T(1024)}, f32[2048,1024]{1,0:T(8,128)}, f32[1024]{0:T(1024)S(1)}, f32[1024]{0:T(1024)}, /*index=5*/f32[2048,1024]{1,0:T(8,128)}) fusion(f32[2048,1024]{1,0:T(8,128)} %convolution_add_fusion, f32[2048]{0:T(1024)S(1)} %copy-done.65, f32[2048]{0:T(1024)S(1)} %copy-done.61, bf16[1024,1024]{1,0:T(8,128)(2,1)} %copy-done.5, ...), kind=kOutput, calls=%fused_computation.289 | convolution fusion | flops 3254775808 | bytes 42508288 | tf_op jit(solution)/shard_map/dot_general | solution.py:451
  417.9 7.4 %add_add_fusion = f32[2048,1024]{1,0:T(8,128)S(1)} fusion(f32[2048,1024]{1,0:T(8,128)} %fusion.58, f32[2048,1024]{1,0:T(8,128)} %fusion.59, bf16[2048,256]{1,0:T(8,128)(2,1)S(1)} %copy-done.34, bf16[2048,256]{1,0:T(8,128)(2,1)S(1)} %copy-done.32, bf16[128,1024]{1,0:T(8,128)(2,1)} %collective-permute-done.42, bf16[128,1024]{1,0:T(8,128)(2,1)} %collective-permute-done.41, ...), kind=kOutput, calls=%fused_computation.8 | convolution fusion | flops 2160066560 | bytes 28311552 | tf_op jit(solution)/shard_map/dot_general | solution.py:439
  437.3 7.7 %collective-permute-done.87 = bf16[1024,256]{1,0:T(8,128)(2,1)S(1)} collective-permute-done((bf16[1024,256]{1,0:T(8,128)(2,1)}, bf16[1024,256]{1,0:T(8,128)(2,1)S(1)}, u32[]{:S(2)}, u32[]{:S(2)}) %collective-permute-start.87) | collective-permute-done | bytes 524320 | tf_op jit(solution)/shard_map/ppermute | solution.py:197
  472.1 11.8 %collective-permute-done.71 = bf16[128,256]{1,0:T(8,128)(2,1)S(1)} collective-permute-done((bf16[128,256]{1,0:T(8,128)(2,1)S(1)}, bf16[128,256]{1,0:T(8,128)(2,1)S(1)}, u32[]{:S(2)}, u32[]{:S(2)}) %collective-permute-start.71) | collective-permute-done | bytes 65568 | tf_op jit(solution)/shard_map/ppermute | solution.py:200
  484.0 6.0 %collective-permute-done.72 = bf16[128,256]{1,0:T(8,128)(2,1)S(1)} collective-permute-done((bf16[128,256]{1,0:T(8,128)(2,1)S(1)}, bf16[128,256]{1,0:T(8,128)(2,1)S(1)}, u32[]{:S(2)}, u32[]{:S(2)}) %collective-permute-start.72) | collective-permute-done | bytes 65568 | tf_op jit(solution)/shard_map/ppermute | solution.py:200
  501.1 9.5 %collective-permute-done.95 = bf16[512,256]{1,0:T(8,128)(2,1)S(1)} collective-permute-done((bf16[512,256]{1,0:T(8,128)(2,1)S(1)}, bf16[512,256]{1,0:T(8,128)(2,1)S(1)}, u32[]{:S(2)}, u32[]{:S(2)}) %collective-permute-start.95) | collective-permute-done | bytes 262176 | tf_op jit(solution)/shard_map/ppermute | solution.py:200
  (620 shorter events, 298.5 us)
Async XLA Ops:
  1.7 29.1 %collective-permute-start.21 = (bf16[512,128]{1,0:T(8,128)(2,1)S(1)}, bf16[512,128]{1,0:T(8,128)(2,1)S(1)}, u32[]{:S(2)}, u32[]{:S(2)}) collective-permute-start(bf16[512,128]{1,0:T(8,128)(2,1)S(1)} %constant_dynamic-slice_fusion.24), channel_id=1, source_target_pairs={{0,4},{4,0},{8,12},{12,8},{16,20},{20,16},{24,28},{28,24},{1,5},{5... | collective-permute-start | bytes 393224 | tf_op jit(solution)/shard_map/ppermute | solution.py:194
  3.1 28.3 %collective-permute-start.15 = (bf16[128,512]{1,0:T(8,128)(2,1)S(1)}, bf16[128,512]{1,0:T(8,128)(2,1)S(1)}, u32[]{:S(2)}, u32[]{:S(2)}) collective-permute-start(bf16[128,512]{1,0:T(8,128)(2,1)S(1)} %constant_dynamic-slice_fusion.27), channel_id=1, source_target_pairs={{0,4},{4,0},{8,12},{12,8},{16,20},{20,16},{24,28},{28,24},{1,5},{5... | collective-permute-start | bytes 393224 | tf_op jit(solution)/shard_map/ppermute | solution.py:194
  5.6 23.4 %collective-permute-start.2 = (bf16[128,3,128]{0,2,1:T(8,128)(2,1)S(1)}, bf16[128,3,128]{0,2,1:T(8,128)(2,1)S(1)}, u32[]{:S(2)}, u32[]{:S(2)}) collective-permute-start(bf16[128,3,128]{0,2,1:T(8,128)(2,1)S(1)} %copy.62), channel_id=1, source_target_pairs={{0,4},{4,0},{8,12},{12,8},{16,20},{20,16},{24,28},{28,24},{1,5},{5... | collective-permute-start | bytes 294920 | tf_op jit(solution)/shard_map/ppermute | solution.py:194
  34.9 24.6 %collective-permute-start.13 = (bf16[128,1024]{1,0:T(8,128)(2,1)S(1)}, bf16[128,1024]{1,0:T(8,128)(2,1)S(1)}, u32[]{:S(2)}, u32[]{:S(2)}) collective-permute-start(bf16[128,1024]{1,0:T(8,128)(2,1)S(1)} %constant_dynamic-update-slice_fusion.44), channel_id=1, source_target_pairs={{0,1},{1,2},{2,3},{3,0},{4,5},{5,6},{6,7},{7,4},{8,9},{9,10},{10,1... | collective-permute-start | bytes 786440 | tf_op jit(solution)/shard_map/ppermute | solution.py:200
  80.3 60.6 %collective-permute-start = (bf16[1024,1024]{1,0:T(8,128)(2,1)S(1)}, bf16[1024,1024]{1,0:T(8,128)(2,1)S(1)}, u32[]{:S(2)}, u32[]{:S(2)}) collective-permute-start(bf16[1024,1024]{1,0:T(8,128)(2,1)S(1)} %copy-done.3), channel_id=1, source_target_pairs={{0,4},{4,0},{8,12},{12,8},{16,20},{20,16},{24,28},{28,24},{1,5},{5... | collective-permute-start | bytes 6291464 | tf_op jit(solution)/shard_map/ppermute | solution.py:194
  80.3 21.6 %collective-permute-start.36 = (bf16[1024,256]{1,0:T(8,128)(2,1)S(1)}, bf16[1024,256]{1,0:T(8,128)(2,1)S(1)}, u32[]{:S(2)}, u32[]{:S(2)}) collective-permute-start(bf16[1024,256]{1,0:T(8,128)(2,1)S(1)} %constant_dynamic-update-slice_fusion.28), channel_id=1, source_target_pairs={{0,16},{4,20},{8,24},{12,28},{16,0},{20,4},{24,8},{28,12},{1,17},{... | collective-permute-start | bytes 1572872 | tf_op jit(solution)/shard_map/ppermute | solution.py:197
  83.6 21.2 %collective-permute-start.7 = (bf16[1024,384]{0,1:T(8,128)(2,1)S(1)}, bf16[1024,384]{0,1:T(8,128)(2,1)S(1)}, u32[]{:S(2)}, u32[]{:S(2)}) collective-permute-start(bf16[1024,384]{0,1:T(8,128)(2,1)S(1)} %constant_dynamic-update-slice_fusion.43), channel_id=1, source_target_pairs={{0,1},{1,2},{2,3},{3,0},{4,5},{5,6},{6,7},{7,4},{8,9},{9,10},{10,1... | collective-permute-start | bytes 2359304 | tf_op jit(solution)/shard_map/ppermute | solution.py:200
  104.8 39.4 %collective-permute-start.1 = (bf16[1024,1024]{1,0:T(8,128)(2,1)S(1)}, bf16[1024,1024]{1,0:T(8,128)(2,1)S(1)}, u32[]{:S(2)}, u32[]{:S(2)}) collective-permute-start(bf16[1024,1024]{1,0:T(8,128)(2,1)S(1)} %copy-done.6), channel_id=1, source_target_pairs={{0,4},{4,0},{8,12},{12,8},{16,20},{20,16},{24,28},{28,24},{1,5},{5... | collective-permute-start | bytes 6291464 | tf_op jit(solution)/shard_map/ppermute | solution.py:194
  115.9 22.4 %collective-permute-start.39 = (bf16[1024,384]{0,1:T(8,128)(2,1)S(1)}, bf16[1024,384]{0,1:T(8,128)(2,1)}, u32[]{:S(2)}, u32[]{:S(2)}) collective-permute-start(bf16[1024,384]{0,1:T(8,128)(2,1)S(1)} %collective-permute-done.7), channel_id=1, source_target_pairs={{0,1},{1,2},{2,3},{3,0},{4,5},{5,6},{6,7},{7,4},{8,9},{9,10},{10,1... | collective-permute-start | bytes 2359304 | tf_op jit(solution)/shard_map/ppermute | solution.py:200
  128.3 171.9 %collective-permute-start.42 = (bf16[128,1024]{1,0:T(8,128)(2,1)}, bf16[128,1024]{1,0:T(8,128)(2,1)}, u32[]{:S(2)}, u32[]{:S(2)}) collective-permute-start(bf16[128,1024]{1,0:T(8,128)(2,1)} %collective-permute-done.41), channel_id=1, source_target_pairs={{0,1},{1,2},{2,3},{3,0},{4,5},{5,6},{6,7},{7,4},{8,9},{9,10},{10,1... | collective-permute-start | bytes 786440 | tf_op jit(solution)/shard_map/ppermute | solution.py:200
  138.2 211.3 %collective-permute-start.40 = (bf16[1024,384]{0,1:T(8,128)(2,1)}, bf16[1024,384]{0,1:T(8,128)(2,1)}, u32[]{:S(2)}, u32[]{:S(2)}) collective-permute-start(bf16[1024,384]{0,1:T(8,128)(2,1)} %collective-permute-done.39), channel_id=1, source_target_pairs={{0,1},{1,2},{2,3},{3,0},{4,5},{5,6},{6,7},{7,4},{8,9},{9,10},{10,1... | collective-permute-start | bytes 2359304 | tf_op jit(solution)/shard_map/ppermute | solution.py:200
  257.1 68.1 %collective-permute-start.91 = (bf16[512,256]{1,0:T(8,128)(2,1)}, bf16[512,256]{1,0:T(8,128)(2,1)}, u32[]{:S(2)}, u32[]{:S(2)}) collective-permute-start(bf16[512,256]{1,0:T(8,128)(2,1)} %get-tuple-element.108), channel_id=1, source_target_pairs={{0,16},{4,20},{8,24},{12,28},{16,0},{20,4},{24,8},{28,12},{1,17},{... | collective-permute-start | bytes 786440 | tf_op jit(solution)/shard_map/ppermute | solution.py:197
  258.2 68.3 %collective-permute-start.93 = (bf16[512,256]{1,0:T(8,128)(2,1)}, bf16[512,256]{1,0:T(8,128)(2,1)}, u32[]{:S(2)}, u32[]{:S(2)}) collective-permute-start(bf16[512,256]{1,0:T(8,128)(2,1)} %get-tuple-element.110), channel_id=1, source_target_pairs={{0,8},{4,12},{8,0},{12,4},{16,24},{20,28},{24,16},{28,20},{1,9},{5... | collective-permute-start | bytes 786440 | tf_op jit(solution)/shard_map/ppermute | solution.py:197
  263.4 43.1 %collective-permute-start.62 = (bf16[128,256]{1,0:T(8,128)(2,1)}, bf16[128,256]{1,0:T(8,128)(2,1)}, u32[]{:S(2)}, u32[]{:S(2)}) collective-permute-start(bf16[128,256]{1,0:T(8,128)(2,1)} %get-tuple-element.158), channel_id=1, source_target_pairs={{0,16},{4,20},{8,24},{12,28},{16,0},{20,4},{24,8},{28,12},{1,17},{... | collective-permute-start | bytes 196616 | tf_op jit(solution)/shard_map/ppermute | solution.py:197
  335.3 131.0 %collective-permute-start.66 = (bf16[128,256]{1,0:T(8,128)(2,1)S(1)}, bf16[128,256]{1,0:T(8,128)(2,1)}, u32[]{:S(2)}, u32[]{:S(2)}) collective-permute-start(bf16[128,256]{1,0:T(8,128)(2,1)S(1)} %split.109), channel_id=1, source_target_pairs={{0,1},{1,2},{2,3},{3,0},{4,5},{5,6},{6,7},{7,4},{8,9},{9,10},{10,1... | collective-permute-start | bytes 196616 | tf_op jit(solution)/shard_map/ppermute | solution.py:200
  341.5 92.0 %collective-permute-start.92 = (bf16[1024,256]{1,0:T(8,128)(2,1)}, bf16[1024,256]{1,0:T(8,128)(2,1)}, u32[]{:S(2)}, u32[]{:S(2)}) collective-permute-start(bf16[1024,256]{1,0:T(8,128)(2,1)} %pad_maximum_fusion.13), channel_id=1, source_target_pairs={{0,8},{4,12},{8,0},{12,4},{16,24},{20,28},{24,16},{28,20},{1,9},{5... | collective-permute-start | bytes 1572872 | tf_op jit(solution)/shard_map/ppermute | solution.py:197
  347.9 86.7 %collective-permute-start.94 = (bf16[1024,256]{1,0:T(8,128)(2,1)}, bf16[1024,256]{1,0:T(8,128)(2,1)}, u32[]{:S(2)}, u32[]{:S(2)}) collective-permute-start(bf16[1024,256]{1,0:T(8,128)(2,1)} %pad_maximum_fusion.14), channel_id=1, source_target_pairs={{0,16},{4,20},{8,24},{12,28},{16,0},{20,4},{24,8},{28,12},{1,17},{... | collective-permute-start | bytes 1572872 | tf_op jit(solution)/shard_map/ppermute | solution.py:197
  395.2 35.2 %collective-permute-start.67 = (bf16[128,256]{1,0:T(8,128)(2,1)}, bf16[128,256]{1,0:T(8,128)(2,1)}, u32[]{:S(2)}, u32[]{:S(2)}) collective-permute-start(bf16[128,256]{1,0:T(8,128)(2,1)} %get-tuple-element.152), channel_id=1, source_target_pairs={{0,16},{4,20},{8,24},{12,28},{16,0},{20,4},{24,8},{28,12},{1,17},{... | collective-permute-start | bytes 196616 | tf_op jit(solution)/shard_map/ppermute | solution.py:197
  396.4 35.2 %collective-permute-start.69 = (bf16[128,256]{1,0:T(8,128)(2,1)}, bf16[128,256]{1,0:T(8,128)(2,1)}, u32[]{:S(2)}, u32[]{:S(2)}) collective-permute-start(bf16[128,256]{1,0:T(8,128)(2,1)} %get-tuple-element.154), channel_id=1, source_target_pairs={{0,8},{4,12},{8,0},{12,4},{16,24},{20,28},{24,16},{28,20},{1,9},{5... | collective-permute-start | bytes 196616 | tf_op jit(solution)/shard_map/ppermute | solution.py:197
  452.0 49.0 %collective-permute-start.54 = (bf16[256,3,128]{0,2,1:T(8,128)(2,1)S(1)}, bf16[256,3,128]{0,2,1:T(8,128)(2,1)S(1)}, u32[]{:S(2)}, u32[]{:S(2)}) collective-permute-start(bf16[256,3,128]{0,2,1:T(8,128)(2,1)S(1)} %copy-done.59), channel_id=1, source_target_pairs={{0,1},{1,2},{2,3},{3,0},{4,5},{5,6},{6,7},{7,4},{8,9},{9,10},{10,1... | collective-permute-start | bytes 589832 | tf_op jit(solution)/shard_map/ppermute | solution.py:200
  465.3 67.5 %collective-permute-start.44 = (bf16[1024,1024]{1,0:T(8,128)(2,1)S(1)}, bf16[1024,1024]{1,0:T(8,128)(2,1)S(1)}, u32[]{:S(2)}, u32[]{:S(2)}) collective-permute-start(bf16[1024,1024]{1,0:T(8,128)(2,1)S(1)} %copy-done.25), channel_id=1, source_target_pairs={{0,4},{4,0},{8,12},{12,8},{16,20},{20,16},{24,28},{28,24},{1,5},{5... | collective-permute-start | bytes 6291464 | tf_op jit(solution)/shard_map/ppermute | solution.py:194
  466.2 25.2 %collective-permute-start.90 = (bf16[512,256]{1,0:T(8,128)(2,1)S(1)}, bf16[512,256]{1,0:T(8,128)(2,1)S(1)}, u32[]{:S(2)}, u32[]{:S(2)}) collective-permute-start(bf16[512,256]{1,0:T(8,128)(2,1)S(1)} %split.107), channel_id=1, source_target_pairs={{0,1},{1,2},{2,3},{3,0},{4,5},{5,6},{6,7},{7,4},{8,9},{9,10},{10,1... | collective-permute-start | bytes 786440 | tf_op jit(solution)/shard_map/ppermute | solution.py:200
  467.2 24.7 %collective-permute-start.78 = (bf16[256,512]{1,0:T(8,128)(2,1)S(1)}, bf16[256,512]{1,0:T(8,128)(2,1)S(1)}, u32[]{:S(2)}, u32[]{:S(2)}) collective-permute-start(bf16[256,512]{1,0:T(8,128)(2,1)S(1)} %split.108), channel_id=1, source_target_pairs={{0,1},{1,2},{2,3},{3,0},{4,5},{5,6},{6,7},{7,4},{8,9},{9,10},{10,1... | collective-permute-start | bytes 786440 | tf_op jit(solution)/shard_map/ppermute | solution.py:200
  493.2 58.2 %collective-permute-start.43 = (bf16[1024,1024]{1,0:T(8,128)(2,1)}, bf16[1024,1024]{1,0:T(8,128)(2,1)}, u32[]{:S(2)}, u32[]{:S(2)}) collective-permute-start(bf16[1024,1024]{1,0:T(8,128)(2,1)} %slice.433), channel_id=1, source_target_pairs={{0,4},{4,0},{8,12},{12,8},{16,20},{20,16},{24,28},{28,24},{1,5},{5... | collective-permute-start | bytes 6291464 | tf_op jit(solution)/shard_map/ppermute | solution.py:194
  (179 other events, 2597.9 us)

commit v2 on v1

v2 whole, which is shorter than its diff:
```python
from functools import partial
import math

import jax
import jax.numpy as jnp
from jax import lax
from jax.experimental import pallas as pl
from jax.experimental.pallas import tpu as pltpu
from jax.sharding import PartitionSpec as P

HD = 64
ROT = 16
EPS = 1e-05
MASKED = 1e30
F32 = jnp.float32
BF16 = jnp.bfloat16
VMEM_BYTES = 56 * 1024 * 1024
NT = (((1,), (1,)), ((), ()))
TN = (((0,), (0,)), ((), ()))
NN = (((1,), (0,)), ((), ()))

dot32 = partial(lax.dot_general, preferred_element_type=F32)


def whole_spec(value):
    return pl.BlockSpec(value.shape, lambda *_: (0,) * value.ndim)


def put_rows(into, pieces, place):
    for ref, key in pieces:
        rows = ref.shape[0]
        if rows == into.shape[0]:
            into[...] = ref[...]
        else:
            into[pl.ds(pl.multiple_of((place ^ key) * rows, rows), rows), :] = ref[...]


def prepare_kernel(x_own, x_other, dy_own, dy_other, gain_ref, an_ref, mn_ref, dy_ref, ant_ref, mnt_ref, dyt_ref):
    step = pl.program_id(0)
    half = pl.num_programs(0) // 2

    def work(x_ref, grad_ref):
        xhat, _ = row_norm(x_ref[...].astype(F32))
        an = (xhat * gain_ref[0:1, :] + gain_ref[1:2, :]).astype(BF16)
        mn = (xhat * gain_ref[2:3, :] + gain_ref[3:4, :]).astype(BF16)
        dy = grad_ref[...]
        an_ref[...], mn_ref[...], dy_ref[...] = an, mn, dy
        ant_ref[...], mnt_ref[...], dyt_ref[...] = an.T, mn.T, dy.T

    @pl.when(step < half)
    def _():
        work(x_own, dy_own)

    @pl.when(step >= half)
    def _():
        work(x_other, dy_other)


def prepare(x_own, x_other, dy_own, dy_other, gains):
    rows, depth = x_own.shape
    br = min(256, rows)
    half = rows // br
    own = pl.BlockSpec((br, depth), lambda i: (jnp.minimum(i, half - 1), 0))
    other = pl.BlockSpec((br, depth), lambda i: (jnp.maximum(i - half, 0), 0))
    tall = pl.BlockSpec((br, depth), lambda i: (i, 0))
    wide = pl.BlockSpec((depth, br), lambda i: (0, i))
    return pl.pallas_call(
        prepare_kernel,
        grid=(2 * half,),
        in_specs=[own, other, own, other, whole_spec(gains)],
        out_specs=[tall] * 3 + [wide] * 3,
        out_shape=[jax.ShapeDtypeStruct((2 * rows, depth), BF16)] * 3
        + [jax.ShapeDtypeStruct((depth, 2 * rows), BF16)] * 3,
        compiler_params=pltpu.CompilerParams(vmem_limit_bytes=VMEM_BYTES),
        cost_estimate=pl.CostEstimate(
            flops=40 * rows * depth, bytes_accessed=32 * rows * depth, transcendentals=2 * rows
        ),
        name="prepare",
    )(x_own, x_other, dy_own, dy_other, gains)


def attention_kernel(place_ref, an_ref, dy_ref, bias_ref, cos_ref, sa_ref, sb_ref, qf_ref, kf_ref, *refs, keys, bq):
    length = an_ref.shape[0]
    width = 2 * HD
    piece_refs, refs = refs[: sum(map(len, keys))], refs[sum(map(len, keys)) :]
    att_ref, dmix_ref, qkv_ref, out_ref, packed, dk_scr, dv_scr = refs
    at = 0
    for j, pair_keys in enumerate(keys):
        pieces = list(zip(piece_refs[at : at + len(pair_keys)], pair_keys))
        at += len(pair_keys)

        @pl.when((pl.program_id(0) == j) & (pl.program_id(1) == 0))
        def _():
            put_rows(packed, pieces, place_ref[0])
            qkv_ref[...] = packed[:, : 3 * width]
            out_ref[...] = packed[:, 3 * width :]

    mixed = dot32(an_ref[...], packed[:, : 3 * width], NN) + bias_ref[...]
    cos, sa, sb = cos_ref[...], sa_ref[...], sb_ref[...]
    scale = 1.0 / math.sqrt(HD)
    half = ROT // 2

    def turn(v, c, a, b, sign):
        side = pltpu.roll(v, width - half, 1) * a + pltpu.roll(v, half, 1) * b
        return v * c + side if sign > 0 else v * c - side

    q = turn(mixed[:, 0:width], cos, sa, sb, 1).astype(BF16)
    k = turn(mixed[:, width : 2 * width], cos, sa, sb, 1).astype(BF16)
    v = mixed[:, 2 * width : 3 * width].astype(BF16)
    do = dot32(dy_ref[...], packed[:, 3 * width :], NN).astype(BF16)
    lane = lax.broadcasted_iota(jnp.int32, (length, width), 1)
    zero = jnp.zeros((), BF16)
    qs = (q.astype(F32) * scale).astype(BF16)
    qf = qf_ref[...]
    kaug = jnp.concatenate([k, kf_ref[...]], axis=1)
    heads = []
    for h in range(2):
        m = (lane // HD) == h
        qm = jnp.where(m, qs, zero)
        heads.append(
            (
                jnp.concatenate([qm, qf], axis=1),
                qm,
                jnp.where(m, k, zero),
                jnp.where(m, v, zero),
                jnp.where(m, do, zero),
            )
        )
    causal = lax.broadcasted_iota(jnp.int32, (bq, bq), 1) <= lax.broadcasted_iota(jnp.int32, (bq, bq), 0)
    blocks = length // bq
    for i in range(blocks):
        r0 = i * bq
        w = r0 + bq
        att = dq = dkp = dvp = None
        for qaug, qm, km, vm, dom in heads:
            s = dot32(qaug[r0:w], kaug[:w], NT)
            diagonal = jnp.where(causal, s[:, r0:], -MASKED)
            s = diagonal if i == 0 else jnp.concatenate([s[:, :r0], diagonal], axis=1)
            e = jnp.exp(s - jnp.max(s, axis=1, keepdims=True))
            p = e * (1.0 / jnp.sum(e, axis=1, keepdims=True))
            pb = p.astype(BF16)
            o = dot32(pb, vm[:w], NN)
            dp = dot32(dom[r0:w], v[:w], NT)
            delta = jnp.sum(p * dp, axis=1, keepdims=True)
            ds = (p * (dp - delta)).astype(BF16)
            x = dot32(ds, km[:w], NN)
            a = dot32(pb, dom[r0:w], TN)
            b = dot32(ds, qm[r0:w], TN)
            if att is None:
                att, dq, dvp, dkp = o, x, a, b
            else:
                att, dq, dvp, dkp = att + o, dq + x, dvp + a, dkp + b
        att_ref[r0:w, :] = att.astype(BF16)
        dmix_ref[r0:w, 0:width] = turn(dq * scale, cos[r0:w], sa[r0:w], sb[r0:w], -1).astype(BF16)
        if i > 0:
            dk_scr[:r0] += dkp[:r0]
            dv_scr[:r0] += dvp[:r0]
        dk_scr[r0:w] = dkp[r0:]
        dv_scr[r0:w] = dvp[r0:]
    dmix_ref[:, width : 2 * width] = turn(dk_scr[...], cos, sa, sb, -1).astype(BF16)
    dmix_ref[:, 2 * width : 3 * width] = dv_scr[...].astype(BF16)


def attention(pairs, place, an, dy, bias, tables, length):
    rows, depth = an.shape
    width = 2 * HD
    seqs = rows // length
    count = len(pairs)
    row = pl.BlockSpec((length, depth), lambda j, s, p: (s, 0))
    table = pl.BlockSpec((length, width), lambda j, s, p: (s, 0))
    pieces = [piece for pair in pairs for piece in pair.values()]
    units = seqs * count
    return pl.pallas_call(
        partial(attention_kernel, keys=[list(pair) for pair in pairs], bq=min(512, length)),
        grid_spec=pltpu.PrefetchScalarGridSpec(
            num_scalar_prefetch=1,
            grid=(count, seqs),
            in_specs=[row, row, pl.BlockSpec((1, 3 * width), lambda j, s, p: (0, j))]
            + [table] * 5
            + [whole_spec(v) for v in pieces],
            out_specs=[
                pl.BlockSpec((length, width), lambda j, s, p: (s, j)),
                pl.BlockSpec((length, 3 * width), lambda j, s, p: (s, j)),
                pl.BlockSpec((depth, 3 * width), lambda j, s, p: (0, j)),
                pl.BlockSpec((depth, width), lambda j, s, p: (0, j)),
            ],
            scratch_shapes=[
                pltpu.VMEM((depth, 4 * width), BF16),
                pltpu.VMEM((length, width), F32),
                pltpu.VMEM((length, width), F32),
            ],
        ),
        out_shape=[
            jax.ShapeDtypeStruct((rows, count * width), BF16),
            jax.ShapeDtypeStruct((rows, count * 3 * width), BF16),
            jax.ShapeDtypeStruct((depth, count * 3 * width), BF16),
            jax.ShapeDtypeStruct((depth, count * width), BF16),
        ],
        compiler_params=pltpu.CompilerParams(vmem_limit_bytes=VMEM_BYTES),
        cost_estimate=pl.CostEstimate(
            flops=units * (32 * length * length * width + 8 * length * depth * width),
            bytes_accessed=units * length * (depth * 4 + width * 40),
            transcendentals=units * 2 * length * length,
        ),
        name="attention",
    )(place, an, dy, bias, *tables, *pieces)


def mlp_kernel(place_ref, mn_ref, dy_ref, bias_ref, *refs, keys):
    piece_refs, refs = refs[: sum(map(len, keys))], refs[sum(map(len, keys)) :]
    act_ref, dgate_ref, sum_ref, up_ref, down_ref, packed = refs
    units = up_ref.shape[1]
    at = 0
    for j, slot_keys in enumerate(keys):
        pieces = list(zip(piece_refs[at : at + len(slot_keys)], slot_keys))
        at += len(slot_keys)

        @pl.when((pl.program_id(0) == j) & (pl.program_id(1) == 0))
        def _():
            put_rows(packed, pieces, place_ref[0])
            up_ref[...] = packed[:, :units]
            down_ref[...] = packed[:, units:]

    gate = dot32(mn_ref[...], packed[:, :units], NN) + bias_ref[...]
    dact = dot32(dy_ref[...], packed[:, units:], NN)
    cdf = 0.5 + 0.5 * lax.erf(gate * math.sqrt(0.5))
    pdf = jnp.exp(gate * gate * -0.5) * (1.0 / math.sqrt(2.0 * math.pi))
    act_ref[...] = (gate * cdf).astype(BF16)
    dgate = (dact * (cdf + gate * pdf)).astype(BF16)
    dgate_ref[...] = dgate
    part = jnp.sum(dgate.astype(F32), axis=0, keepdims=True)

    @pl.when(pl.program_id(1) == 0)
    def _():
        sum_ref[...] = part

    @pl.when(pl.program_id(1) > 0)
    def _():
        sum_ref[...] += part


def mlp_front(slots, place, mn, dy, bias):
    rows, depth = mn.shape
    units = slots[0][0].shape[1] // 2
    count = len(slots)
    br = min(512, rows)
    row = pl.BlockSpec((br, depth), lambda c, r, p: (r, 0))
    tile = pl.BlockSpec((br, units), lambda c, r, p: (r, c))
    top = pl.BlockSpec((1, units), lambda c, r, p: (0, c))
    tall = pl.BlockSpec((depth, units), lambda c, r, p: (0, c))
    pieces = [piece for slot in slots for piece in slot.values()]
    return pl.pallas_call(
        partial(mlp_kernel, keys=[list(slot) for slot in slots]),
        grid_spec=pltpu.PrefetchScalarGridSpec(
            num_scalar_prefetch=1,
            grid=(count, rows // br),
            in_specs=[row, row, top] + [whole_spec(v) for v in pieces],
            out_specs=[tile, tile, top, tall, tall],
            scratch_shapes=[pltpu.VMEM((depth, 2 * units), BF16)],
        ),
        out_shape=[
            jax.ShapeDtypeStruct((rows, count * units), BF16),
            jax.ShapeDtypeStruct((rows, count * units), BF16),
            jax.ShapeDtypeStruct((1, count * units), F32),
            jax.ShapeDtypeStruct((depth, count * units), BF16),
            jax.ShapeDtypeStruct((depth, count * units), BF16),
        ],
        compiler_params=pltpu.CompilerParams(vmem_limit_bytes=VMEM_BYTES),
        cost_estimate=pl.CostEstimate(
            flops=4 * rows * depth * count * units,
            bytes_accessed=count * (rows * depth * 4 + units * depth * 8 + rows * units * 4),
            transcendentals=2 * rows * count * units,
        ),
        name="mlp_front",
    )(place, mn, dy, bias, *pieces)


def grads_kernel(place_ref, left_a, left_b, right_a, right_b, *outs, count, keys):
    a = dot32(left_a[...], right_a[...], NN)
    b = dot32(left_b[...], right_b[...], NN)
    wa, wb = a.shape[1] // count, b.shape[1] // count
    for n, _ in enumerate(keys):

        @pl.when(pl.program_id(0) == n)
        def _():
            for j in range(count):
                out = outs[j * len(keys) + n]
                out[:, :wa] = a[:, j * wa : (j + 1) * wa].astype(out.dtype)
                out[:, wa:] = b[:, j * wb : (j + 1) * wb].astype(out.dtype)


def weight_grads(place, places, left_a, right_a, left_b, right_b, count):
    depth, rows = left_a.shape
    keys = (3, 1, 2, 0) if places == 4 else (0,)
    size = depth // len(keys)

    def left_at(i, p):
        key = keys[0]
        for n in range(1, len(keys)):
            key = jnp.where(i == n, keys[n], key)
        return (p[0] ^ key, 0)

    left = pl.BlockSpec((size, rows), left_at)
    width = (right_a.shape[1] + right_b.shape[1]) // count
    out = pl.BlockSpec((size, width), lambda i, p: (0, 0))
    found = pl.pallas_call(
        partial(grads_kernel, count=count, keys=keys),
        grid_spec=pltpu.PrefetchScalarGridSpec(
            num_scalar_prefetch=1,
            grid=(len(keys),),
            in_specs=[left, left, whole_spec(right_a), whole_spec(right_b)],
            out_specs=[out] * (count * len(keys)),
        ),
        out_shape=[jax.ShapeDtypeStruct((size, width), BF16)] * (count * len(keys)),
        compiler_params=pltpu.CompilerParams(vmem_limit_bytes=VMEM_BYTES),
        cost_estimate=pl.CostEstimate(
            flops=2 * rows * depth * count * width,
            bytes_accessed=4 * rows * depth + 2 * count * width * (rows + depth),
            transcendentals=0,
        ),
        name="weight_grads",
    )(place, left_a, left_b, right_a, right_b)
    return [dict(zip(keys, found[j * len(keys) : (j + 1) * len(keys)])) for j in range(count)]


def row_norm(x):
    centre = x - jnp.mean(x, axis=-1, keepdims=True)
    rstd = lax.rsqrt(jnp.mean(centre * centre, axis=-1, keepdims=True) + EPS)
    return centre * rstd, rstd


def pull_kernel(*refs):
    dg0, up0, dg1, up1, dm0, qkv0, dm1, qkv1, x_ref, gain_ref = refs[:10]
    out_ref, sum_ref = refs[-2:]
    n_mlp = dot32(dg0[...], up0[...], NT) + dot32(dg1[...], up1[...], NT)
    n_attn = dot32(dm0[...], qkv0[...], NT) + dot32(dm1[...], qkv1[...], NT)
    xhat, rstd = row_norm(x_ref[...].astype(F32))
    u = n_attn * gain_ref[0:1, :] + n_mlp * gain_ref[2:3, :]
    parts = [jnp.sum(v, axis=0, keepdims=True) for v in (n_attn * xhat, n_attn, n_mlp * xhat, n_mlp)]
    part = jnp.concatenate(parts + [jnp.zeros((4, u.shape[1]), F32)], axis=0)

    @pl.when(pl.program_id(0) == 0)
    def _():
        sum_ref[...] = part

    @pl.when(pl.program_id(0) > 0)
    def _():
        sum_ref[...] += part

    out_ref[...] = u.astype(out_ref.dtype)


def pull_back(terms, x, gains, first_row, dtype):
    rows, depth = x.shape
    br = min(256, rows)
    first = first_row // br
    block = lambda v: pl.BlockSpec((br, v.shape[1]), lambda i: (i + first, 0))
    specs, args = [], []
    for grad, weight in terms:
        specs += [block(grad), whole_spec(weight)]
        args += [grad, weight]
    tile = pl.BlockSpec((br, depth), lambda i: (i, 0))
    width = sum(grad.shape[1] for grad, _ in terms)
    return pl.pallas_call(
        pull_kernel,
        grid=(rows // br,),
        in_specs=specs + [tile, whole_spec(gains)],
        out_specs=[tile, pl.BlockSpec((8, depth), lambda i: (0, 0))],
        out_shape=[jax.ShapeDtypeStruct((rows, depth), dtype), jax.ShapeDtypeStruct((8, depth), F32)],
        compiler_params=pltpu.CompilerParams(vmem_limit_bytes=VMEM_BYTES),
        cost_estimate=pl.CostEstimate(
            flops=2 * rows * width * depth,
            bytes_accessed=2 * width * (rows + depth) + rows * depth * 8,
            transcendentals=rows,
        ),
        name="pull_back",
    )(*args, x, gains)


def out_kernel(*refs, own):
    att0, out0, att1, out1, act0, down0, act1, down1 = refs[:8]
    y = dot32(act0[...], down0[...], NT) + dot32(act1[...], down1[...], NT)
    y = y + dot32(att0[...], out0[...], NT) + dot32(att1[...], out1[...], NT)
    if not own:
        refs[-1][...] = y.astype(BF16)
        return
    x_ref, other_ref, bias_ref, dy_ref, pull_ref, other_pull_ref, y_ref, grad_ref = refs[8:]
    x = x_ref[...].astype(F32)
    y_ref[...] = (y + x + other_ref[...].astype(F32) + bias_ref[...]).astype(BF16)
    xhat, rstd = row_norm(x)
    u = pull_ref[...] + other_pull_ref[...].astype(F32)
    u = u - jnp.mean(u, axis=-1, keepdims=True) - xhat * jnp.mean(u * xhat, axis=-1, keepdims=True)
    grad_ref[...] = dy_ref[...].astype(F32) + rstd * u


def branch_out(terms, rows, last=None):
    own = last is not None
    depth = terms[0][1].shape[0]
    br = min(256, rows)
    first = 0 if own else rows // br
    tile = pl.BlockSpec((br, depth), lambda i: (i, 0))
    specs, args = [], []
    for value, weight in terms:
        specs += [pl.BlockSpec((br, value.shape[1]), lambda i: (i + first, 0)), whole_spec(weight)]
        args += [value, weight]
    if own:
        specs += [whole_spec(v) if v.shape[0] == 1 else tile for v in last]
        args += last
    width = sum(value.shape[1] for value, _ in terms)
    shapes = [jax.ShapeDtypeStruct((rows, depth), BF16)] + [jax.ShapeDtypeStruct((rows, depth), F32)] * own
    return pl.pallas_call(
        partial(out_kernel, own=own),
        grid=(rows // br,),
        in_specs=specs,
        out_specs=[tile] * len(shapes),
        out_shape=shapes,
        compiler_params=pltpu.CompilerParams(vmem_limit_bytes=VMEM_BYTES),
        cost_estimate=pl.CostEstimate(
            flops=2 * rows * width * depth,
            bytes_accessed=2 * width * (rows + depth) + rows * depth * (18 if own else 2),
            transcendentals=0,
        ),
        name="branch_out",
    )(*args)


class Links:
    def __init__(self):
        self.fsdp = lax.axis_size("fsdp")
        self.tp = lax.axis_size("tp")
        index = lax.axis_index("fsdp")
        self.core = index % 2
        self.place = index // 2
        self.lane = lax.axis_index("tp")
        self.places = self.fsdp // 2
        self.cores = [list(range(c, self.fsdp, 2)) for c in range(2)]
        self.bits = [1 << b for b in range((self.places - 1).bit_length())]

    def swap(self, value):
        return lax.ppermute(value, "fsdp", [(i, i ^ 1) for i in range(self.fsdp)])

    def hop(self, value, bit):
        return lax.ppermute(value, "fsdp", [(i, i ^ (2 * bit)) for i in range(self.fsdp)])

    def ring(self, value):
        return lax.ppermute(value, "tp", [(i, (i + 1) % self.tp) for i in range(self.tp)])

    def far_bit(self, slot):
        return 1 if slot % 2 == 0 else 2

    def near_places(self, piece):
        return {0: piece, 1: self.hop(piece, 1), 2: self.hop(piece, 2)}

    def far_place(self, pieces, slot):
        bit = self.far_bit(slot)
        return {**pieces, 3: self.hop(pieces[3 - bit], bit)}

    def scatter_far(self, blocks, slot):
        return self.hop(blocks[3], 3 - self.far_bit(slot))

    def scatter_near(self, blocks, far, slot):
        bit = self.far_bit(slot)
        near = {1: blocks[1], 2: blocks[2]}
        near[bit] = (near[bit].astype(F32) + far.astype(F32)).astype(BF16)
        return self.hop(near[1], 1), self.hop(near[2], 2)

    def gather_other(self, piece):
        return {0: lax.all_gather(piece, "fsdp", axis=0, tiled=True, axis_index_groups=self.cores)}

    def scatter_other(self, value):
        return lax.psum_scatter(
            value, "fsdp", scatter_dimension=0, tiled=True, axis_index_groups=self.cores
        )

    def scatter_lanes(self, slots):
        total = None
        for step in range(1, self.tp):
            total = slots[step]() if total is None else total + slots[step]()
            total = self.ring(total.astype(BF16)).astype(F32)
        return slots[0]() if total is None else total + slots[0]()

    def total(self, value):
        for bit in [1] + [2 * b for b in self.bits]:
            value = value + lax.ppermute(value, "fsdp", [(i, i ^ bit) for i in range(self.fsdp)])
        bit = 1
        while bit < self.tp:
            value = value + lax.ppermute(value, "tp", [(i, i ^ bit) for i in range(self.tp)])
            bit *= 2
        return value


def pick(value, index, axis):
    return lax.dynamic_index_in_dim(value, index, axis, keepdims=False)


def pair_rows(links, mine, other):
    got = links.swap(other)
    first = jnp.where(links.core == 0, mine, got)
    second = jnp.where(links.core == 0, got, mine)
    return jnp.concatenate([first, second], axis=0)


def unpair_rows(links, block):
    half = block.shape[0] // 2
    mine = lax.dynamic_slice_in_dim(block, links.core * half, half, 0)
    got = links.swap(lax.dynamic_slice_in_dim(block, (1 - links.core) * half, half, 0))
    return jnp.where(links.core == 0, mine, got), jnp.where(links.core == 0, got, mine)


sync = lax.optimization_barrier


def tables_of(segment_rows):
    seqs, length = segment_rows.shape
    width = 2 * HD
    starts = jnp.sum((segment_rows[:, None, :] < segment_rows[:, :, None]).astype(jnp.int32), axis=-1)
    places = (jnp.arange(length, dtype=jnp.int32)[None] - starts).reshape(-1).astype(F32)
    inverse_freq = jnp.power(10000.0, -jnp.arange(0, ROT, 2, dtype=F32) / ROT)
    angles = places[:, None] * jnp.tile(inverse_freq, width // (ROT // 2))[None, :]
    lane = jnp.arange(width, dtype=jnp.int32)[None, :]
    turn = lane % HD
    cos = jnp.where(turn < ROT, jnp.cos(angles), 1.0)
    sine = jnp.sin(angles)
    sa = jnp.where(turn < ROT // 2, -sine, 0.0)
    sb = jnp.where((turn >= ROT // 2) & (turn < ROT), sine, 0.0)
    same = segment_rows.reshape(-1, 1) == lane
    key_mark = jnp.where(same, 1.0, 0.0).astype(BF16)
    query_mark = jnp.where(same | (lane >= 8), 0.0, -MASKED).astype(BF16)
    return cos, sa, sb, query_mark, key_mark


def body(
    tokens,
    segments,
    attn_gain,
    attn_shift,
    mlp_gain,
    mlp_shift,
    qkv_weight,
    qkv_bias,
    out_weight,
    out_bias,
    up_weight,
    up_bias,
    down_weight,
    down_bias,
    cotangent,
):
    links = Links()
    tp = links.tp
    rows, depth = tokens.shape
    length = segments.shape[1]
    head_cols = qkv_weight.shape[2] // 2
    unit_cols = up_weight.shape[1] // 2

    def halves(shard, axis):
        size = shard.shape[axis] // 2
        return [lax.dynamic_slice_in_dim(shard, c * size, size, axis) for c in (links.core, 1 - links.core)]

    qkv_halves = [v.reshape(v.shape[0], -1) for v in halves(qkv_weight, 2)]
    out_halves = [v.T for v in halves(out_weight, 0)]
    up_halves = halves(up_weight, 1)
    down_halves = [v.T for v in halves(down_weight, 0)]
    attn_slots = [pair_rows(links, *[jnp.concatenate(v, axis=1) for v in zip(qkv_halves, out_halves)])]
    mlp_slots = [pair_rows(links, *[jnp.concatenate(v, axis=1) for v in zip(up_halves, down_halves)])]
    qkv_cols = 3 * head_cols

    half = tp // 2
    per = max(1, 2 * HD // head_cols)

    by_hops = links.places == 4 and per == 1
    place = jnp.full((1,), links.place if by_hops else 0, jnp.int32)

    def join_pair(slots):
        if per == 1:
            return slots[0]
        lead = slots[0].shape[0]
        return jnp.concatenate([v.reshape(lead, 4, head_cols) for v in slots], axis=2).reshape(lead, -1)

    def join_qkv(slots):
        if per == 1:
            return slots[0]
        lead = slots[0].shape[0]
        return jnp.concatenate([v.reshape(lead, 3, head_cols) for v in slots], axis=2).reshape(lead, -1)

    def split_pair(value, parts):
        if per == 1:
            return [value]
        lead = value.shape[0]
        blocks = value.reshape(lead, parts, per, head_cols)
        return [blocks[:, :, j].reshape(lead, -1) for j in range(per)]

    groups = [list(range(0, half)), list(range(half, tp))]

    lane_of = [(links.lane - s) % tp for s in range(tp)]
    qkv_bias_lanes = pick(qkv_bias.reshape(3, tp, 2, head_cols), links.core, 2)
    up_bias_lanes = pick(up_bias.reshape(tp, 2, unit_cols), links.core, 1)
    qkv_bias_groups = [
        jnp.concatenate(
            [
                join_qkv([pick(qkv_bias_lanes, lane_of[s], 1).reshape(1, -1) for s in g[i : i + per]])
                for i in range(0, half, per)
            ],
            axis=1,
        ).astype(F32)
        for g in groups
    ]
    up_bias_groups = [
        jnp.concatenate([pick(up_bias_lanes, lane_of[s], 0) for s in g]).astype(F32)[None] for g in groups
    ]

    gains = jnp.stack([v.astype(F32) for v in (attn_gain, attn_shift, mlp_gain, mlp_shift)])
    own_segments = lax.dynamic_slice_in_dim(segments, links.lane * rows // length, rows // length, 0)
    tables = tables_of(jnp.concatenate([own_segments, links.swap(own_segments)], axis=0))
    x_other = links.swap(tokens)
    normed = prepare(tokens, x_other, cotangent, links.swap(cotangent), gains)

    def start_gather(slots):
        return [links.near_places(v) if by_hops else links.gather_other(v) for v in slots]

    def end_gather(states):
        return [links.far_place(v, s) for s, v in enumerate(states)] if by_hops else states

    def pairs_of(states):
        if per == 1:
            return states
        return [{0: join_pair([v[0] for v in states[i : i + per]])} for i in range(0, half, per)]

    def attention_part(g, states, an, dy):
        return attention(pairs_of(states), place, an, dy, qkv_bias_groups[g], tables, length)

    def attention_grads(attended, dmixed, ant, dyt):
        blocks = weight_grads(place, links.places if by_hops else 1, ant, dmixed, dyt, attended, half // per)
        return blocks if per == 1 else [{0: v} for b in blocks for v in split_pair(b[0], 4)]

    def mlp_grads(active, dgate, mnt, dyt):
        return weight_grads(place, links.places if by_hops else 1, mnt, dgate, dyt, active, half)

    def start_scatter(slots):
        return slots, [links.scatter_far(v, s) for s, v in enumerate(slots)] if by_hops else []

    def next_scatter(state):
        slots, far = state
        if not by_hops:
            return [links.scatter_other(v[0]) for v in slots]
        return [(v[0], links.scatter_near(v, f, s)) for s, (v, f) in enumerate(zip(slots, far))]

    def end_scatter(states):
        def term(state):
            if not by_hops:
                return state.astype(F32)
            own, near = state
            return own.astype(F32) + near[0].astype(F32) + near[1].astype(F32)

        return [partial(term, state) for state in states]

    for s in range(1, half):
        attn_slots.append(links.ring(attn_slots[-1]))
        mlp_slots.append(links.ring(mlp_slots[-1]))
    gather_a = start_gather(attn_slots)
    gather_a, tables, normed = sync((gather_a, tables, normed))
    gather_a = end_gather(gather_a)
    gather_a, mlp_slots, attn_slots, normed = sync((gather_a, mlp_slots, attn_slots, normed))
    an, mn, dy2, ant, mnt, dyt = normed

    gather_b = start_gather(mlp_slots)
    for s in range(half, tp):
        mlp_slots.append(links.ring(mlp_slots[-1]))
        attn_slots.append(links.ring(attn_slots[-1]))
    att0, dmix0, qkv0, out0 = attention_part(0, gather_a, an, dy2)
    gather_b, att0, dmix0, mn = sync((gather_b, att0, dmix0, mn))
    gather_b = end_gather(gather_b)
    grad_a0 = attention_grads(att0, dmix0, ant, dyt)
    gather_b, grad_a0, mn, mlp_slots = sync((gather_b, grad_a0, mn, mlp_slots))

    gather_c = start_gather(mlp_slots[half:])
    act0, dgate0, gate_sum0, up0, down0 = mlp_front(gather_b, place, mn, dy2, up_bias_groups[0])
    gather_c, act0, dgate0 = sync((gather_c, act0, dgate0))
    gather_c = end_gather(gather_c)
    grad_m0 = mlp_grads(act0, dgate0, mnt, dyt)
    gather_c, grad_m0, mn, attn_slots = sync((gather_c, grad_m0, mn, attn_slots))

    gather_d = start_gather(attn_slots[half:])
    scatter_b = start_scatter(grad_m0)
    act1, dgate1, gate_sum1, up1, down1 = mlp_front(gather_c, place, mn, dy2, up_bias_groups[1])
    gather_d, scatter_b, act1, dgate1 = sync((gather_d, scatter_b, act1, dgate1))
    gather_d = end_gather(gather_d)
    scatter_b = next_scatter(scatter_b)
    grad_m1 = mlp_grads(act1, dgate1, mnt, dyt)
    gather_d, grad_m1, an = sync((gather_d, grad_m1, an))

    scatter_c = start_scatter(grad_m1)
    scatter_a = start_scatter(grad_a0)
    att1, dmix1, qkv1, out1 = attention_part(1, gather_d, an, dy2)
    scatter_b, scatter_c, scatter_a, att1, dmix1 = sync((scatter_b, scatter_c, scatter_a, att1, dmix1))
    sum_b = end_scatter(scatter_b)
    scatter_c = next_scatter(scatter_c)
    scatter_a = next_scatter(scatter_a)
    grad_a1 = attention_grads(att1, dmix1, ant, dyt)
    scatter_d = start_scatter(grad_a1)
    out_terms = ((att0, out0), (att1, out1), (act0, down0), (act1, down1))
    (sent_out,) = branch_out(out_terms, rows)
    other_out = links.swap(sent_out)
    scatter_d, sent_out, dgate1 = sync((scatter_d, sent_out, dgate1))
    scatter_d = next_scatter(scatter_d)
    terms = ((dgate0, up0), (dgate1, up1), (dmix0, qkv0), (dmix1, qkv1))
    sent_pull, sums_other = pull_back(terms, x_other, gains, rows, BF16)
    other_pull = links.swap(sent_pull)
    scatter_c, scatter_a, sums_other, act0 = sync((scatter_c, scatter_a, sums_other, act0))
    sum_c = end_scatter(scatter_c)
    sum_a = end_scatter(scatter_a)
    pulled, sums_own = pull_back(terms, tokens, gains, 0, F32)
    scatter_d, pulled, att0 = sync((scatter_d, pulled, att0))
    sum_d = end_scatter(scatter_d)
    end_bias = (out_bias.astype(F32) + down_bias.astype(F32))[None]
    out_terms = ((att0, out0), (att1, out1), (act0, down0), (act1, down1))
    output, input_grad = branch_out(
        out_terms, rows, [tokens, other_out, end_bias, cotangent, pulled, other_pull]
    )

    mlp_own = unpair_rows(links, links.scatter_lanes(sum_b + sum_c))
    attn_own = unpair_rows(links, links.scatter_lanes(sum_a + sum_d))
    up_grad = jnp.concatenate([v[:, :unit_cols] for v in mlp_own], axis=1)
    down_grad = jnp.concatenate([v[:, unit_cols:] for v in mlp_own], axis=1).T
    qkv_grad = jnp.concatenate([v[:, :qkv_cols].reshape(-1, 3, head_cols) for v in attn_own], axis=2)
    out_grad = jnp.concatenate([v[:, qkv_cols:] for v in attn_own], axis=1).T

    def spread(values):
        lead, cols = values[0].shape
        full = jnp.zeros((lead, tp, 2, cols), F32)
        for s, value in enumerate(values):
            full = lax.dynamic_update_slice(full, value.reshape(lead, 1, 1, cols), (0, lane_of[s], links.core, 0))
        return full.reshape(-1)

    qkv_sums = [jnp.sum(d.astype(F32), axis=0, keepdims=True) for d in (dmix0, dmix1)]
    pair_sums = [v for d in qkv_sums for v in jnp.split(d, half // per, axis=1)]
    qkv_bias_part = spread([v.reshape(3, head_cols) for d in pair_sums for v in split_pair(d, 3)])
    up_bias_part = spread([v for part in (gate_sum0, gate_sum1) for v in jnp.split(part, half, axis=1)])
    bias_part = jnp.sum(cotangent.astype(F32), axis=0)
    pieces = [
        *(sums_own + sums_other)[:4],
        qkv_bias_part,
        bias_part,
        up_bias_part,
    ]
    sizes = [v.shape[0] for v in pieces]
    summed = links.total(jnp.concatenate(pieces).reshape(-1, 128)).reshape(-1)
    sums = []
    at = 0
    for size in sizes:
        sums.append(summed[at : at + size])
        at += size
    return (
        output,
        input_grad,
        sums[0],
        sums[1],
        sums[2],
        sums[3],
        qkv_grad,
        sums[4].reshape(qkv_bias.shape),
        out_grad,
        sums[5],
        up_grad,
        sums[6],
        down_grad,
        sums[5],
    )


def solution(mesh):
    placed = (
        P(("fsdp", "tp"), None),
        P("fsdp", None),
        P(),
        P(),
        P(),
        P(),
        P("fsdp", None, "tp"),
        P(),
        P("tp", "fsdp"),
        P(),
        P("fsdp", "tp"),
        P(),
        P("tp", "fsdp"),
        P(),
        P(("fsdp", "tp"), None),
    )
    return jax.shard_map(
        body,
        mesh=mesh,
        in_specs=placed,
        out_specs=(
            P(("fsdp", "tp"), None),
            P(("fsdp", "tp"), None),
            P(),
            P(),
            P(),
            P(),
            P("fsdp", None, "tp"),
            P(),
            P("tp", "fsdp"),
            P(),
            P("fsdp", "tp"),
            P(),
            P("tp", "fsdp"),
            P(),
        ),
        check_vma=False,
    )
```

time: 567 us -> 430 us (0.76)
  Pallas kernels: 93.5 us -> 247 us
  matrix products: 116 us -> 0 us
  waiting for transfers between devices: 174 us -> 66.2 us
  other arithmetic: 58.1 us -> 27.1 us
  local copies, waits for them, and re-layouts: 37.4 us -> 13.1 us
  starting transfers between devices: 77.4 us -> 68 us
    pallas_call x4 -> x13, Pallas kernels: 93.5 us -> 247 us  [the longest x2 89.8 us: attention(): pl.pallas_call(partial(attention_kernel, keys=[list(pair) for pair in pai...]
    dot_general x19 -> x0, matrix products: 116 us -> none  [the longest x2 21.5 us: body(): n_attn = dot32(dmix0, qkv_groups[0], NT) + dot32(dmix1, qkv_groups[1], NT)]
    ppermute x56 -> x48, waiting for transfers between devices: 74.8 us -> 14.1 us  [hop(): lax.ppermute(value, 'fsdp', [(i, i ^ 2 * bit) for i in range(self.fsdp)])]
    ppermute x24 -> x12, waiting for transfers between devices: 90.4 us -> 30.6 us  [ring(): lax.ppermute(value, 'tp', [(i, (i + 1) % self.tp) for i in range(self.tp)])]
    convert_element_type x18 -> x10, other arithmetic: 19.4 us -> 4.62 us  [the longest x8 3.46 us: scatter_near(): near[bit] = (near[bit].astype(F32) + far.astype(F32)).astype(BF16)]
    ppermute x2, waiting for transfers between devices: 3.13 us -> 16.3 us  [total(): lax.ppermute(value, 'tp', [(i, i ^ bit) for i in range(self.tp)])]
    slice x24 -> x8, local copies, waits for them, and re-layouts: 13 us -> 0.38 us  [the longest x4 0.28 us: body(): v[:, :qkv_cols].reshape(-1, 3, head_cols)]
    concatenate x26 -> x6, other arithmetic: 11.7 us -> 0.95 us  [the longest x1 0.83 us: body(): up_grad = jnp.concatenate([v[:, :unit_cols] for v in mlp_own], axis=1)]
  transfers between devices with their start and end apart: 98 -> 74, of which waited for: 47 -> 14; matrix products, arithmetic and copies ran while one was open for 36% -> 9% of each run, Pallas kernels for 17% -> 53%
where the time goes in v2:
time: 430 us; the launch traced here: 424 us
  Pallas kernels  247 us (57%)
  starting transfers between devices  68 us (16%)
  waiting for transfers between devices  66.2 us (15%)
  other arithmetic  27.1 us (6%)
  local copies, waits for them, and re-layouts  13.1 us (3%)
    pallas_call x2, Pallas kernels, attention(): pl.pallas_call(partial(attention_kernel, keys=[list(pair) for pair in pai...  89.8 us
    pallas_call x4, Pallas kernels, weight_grads(): pl.pallas_call(partial(grads_kernel, count=count, keys=keys), grid_spec=p...  51.7 us
    ppermute x48, starting transfers between devices, hop(): lax.ppermute(value, 'fsdp', [(i, i ^ 2 * bit) for i in range(self.fsdp)])  51.1 us
    pallas_call x2, Pallas kernels, mlp_front(): pl.pallas_call(partial(mlp_kernel, keys=[list(slot) for slot in slots]),...  37.4 us
    ppermute x12, waiting for transfers between devices, ring(): lax.ppermute(value, 'tp', [(i, (i + 1) % self.tp) for i in range(self.tp)])  30.6 us
    pallas_call x2, Pallas kernels, pull_back(): pl.pallas_call(pull_kernel, grid=(rows // br,), in_specs=specs + [tile, w...  29.4 us
    pallas_call x2, Pallas kernels, branch_out(): pl.pallas_call(partial(out_kernel, own=own), grid=(rows // br,), in_specs...  24.5 us
    ppermute x2, waiting for transfers between devices, total(): lax.ppermute(value, 'tp', [(i, i ^ bit) for i in range(self.tp)])  16.3 us
  transfers between devices with their start and end apart: 74, of which 14 were waited for; matrix products, arithmetic and copies ran while one was open for 9% of the time, Pallas kernels for 53%

profile of v2, /device:TPU:0, one launch (start us, length us, event | category | flops | bytes accessed | tf_op | source)
XLA Modules:
  0.0 423.9 jit_solution(11168963605563778207)
XLA Ops:
  10.8 5.9 %fusion = (f32[2048,128]{1,0:T(8,128)}, f32[2048,128]{1,0:T(8,128)}, f32[2048,128]{1,0:T(8,128)}) fusion(f32[128]{0:T(128)S(1)} %mul.50, f32[2048]{0:T(1024)S(1)} %bitcast.109, pred[128]{0:T(512)(128)(4,1)S(1)} %get-tuple-element.586, pred[128]{0:T(512)(128)(4,1)S(1)} %get-tuple-element.587, pred[128]{0:T(512)(128)(4,1)S(1)} %broadcast_compare_fusion.1), kind=kLoop, calls=%fused_computation.6 | loop fusion | flops 1310720 | bytes 3154816 | tf_op jit(solution)/shard_map/jit(_where)/select_n | solution.py:525
  22.6 5.9 %collective-permute-done.3.refs_4_ = bf16[256,512]{1,0:T(8,128)(2,1)} collective-permute-done((bf16[256,512]{1,0:T(8,128)(2,1)S(1)}, bf16[256,512]{1,0:T(8,128)(2,1)}, u32[]{:S(2)}, u32[]{:S(2)}) %collective-permute-start.3) | collective-permute-done | bytes 262176 | tf_op jit(solution)/shard_map/ppermute | solution.py:446
  32.8 14.3 %prepare.1 = (bf16[2048,1024]{1,0:T(8,128)(2,1)}, bf16[2048,1024]{1,0:T(8,128)(2,1)}, bf16[2048,1024]{1,0:T(8,128)(2,1)}, bf16[1024,2048]{1,0:T(8,128)(2,1)}, bf...) custom-call(bf16[1024,1024]{1,0:T(8,128)(2,1)} %refs_8_.3, bf16[1024,1024]{1,0:T(8,128)(2,1)} %copy-done.3, ...), custom_call_target="tpu_custom_call" | custom-call | flops 41943040 | bytes 33554432 | tf_op jit(solution)/shard_map/prepare/pallas_call | solution.py:67
  49.1 5.5 %collective-permute-done.10.refs_7_ = bf16[256,512]{1,0:T(8,128)(2,1)S(1)} collective-permute-done((bf16[256,512]{1,0:T(8,128)(2,1)S(1)}, bf16[256,512]{1,0:T(8,128)(2,1)S(1)}, u32[]{:S(2)}, u32[]{:S(2)}) %collective-permute-start.10) | collective-permute-done | bytes 262176 | tf_op jit(solution)/shard_map/ppermute | solution.py:443
  63.7 44.7 %attention.2 = (bf16[2048,256]{1,0:T(8,128)(2,1)}, bf16[2048,768]{1,0:T(8,128)(2,1)}, bf16[1024,768]{1,0:T(8,128)(2,1)}, bf16[1024,256]{1,0:T(8,128)(2,1)}) custom-call(s32[1]{0:T(128)} %bitcast.place_ref, bf16[2048,1024]{1,0:T(8,128)(2,1)} %get-tuple-element.402.an_ref, bf16[2048,1024]{1,0:T(8,128)(2,1)} %get-tuple-element.276.dy_ref, ...), custom_call_target="tpu_custom_call" | custom-call | flops 21474836480 | bytes 37748736 | tf_op jit(solution)/shard_map/attention/pallas_call | solution.py:173
  116.0 9.8 %weight_grads.4 = (bf16[256,512]{1,0:T(8,128)(2,1)}, bf16[256,512]{1,0:T(8,128)(2,1)}, bf16[256,512]{1,0:T(8,128)(2,1)}, bf16[256,512]{1,0:T(8,128)(2,1)}, bf16[...) custom-call(s32[1]{0:T(128)} %bitcast.place_ref, ...), custom_call_target="tpu_custom_call" | custom-call | flops 4294967296 | bytes 14680064 | tf_op jit(solution)/shard_map/weight_grads/pallas_call | solution.py:306
  131.1 18.7 %mlp_front.2 = (bf16[2048,1024]{1,0:T(8,128)(2,1)}, bf16[2048,1024]{1,0:T(8,128)(2,1)}, f32[1,1024]{1,0:T(1,128)}, bf16[1024,1024]{1,0:T(8,128)(2,1)}, bf16[1024,1024]{1,0:T(8,128)(2,1)}) custom-call(s32[1]{0:T(128)} %bitcast.place_ref, bf16[2048,1024]{1,0:T(8,128)(2,1)} %get-tuple-element.351.mn_ref, bf16[2048,1024]{1,0:T(8,128)(2,1)} %get-tuple-element.276.dy_ref, ...), custom_call_target="tpu_custom_call" | custom-call | flops 8589934592 | bytes 33554432 | tf_op jit(solution)/shard_map/mlp_front/pallas_call | solution.py:252
  152.5 15.9 %weight_grads.5 = (bf16[256,1024]{1,0:T(8,128)(2,1)}, bf16[256,1024]{1,0:T(8,128)(2,1)}, bf16[256,1024]{1,0:T(8,128)(2,1)}, bf16[256,1024]{1,0:T(8,128)(2,1)}, b...) custom-call(s32[1]{0:T(128)} %bitcast.place_ref, ...), custom_call_target="tpu_custom_call" | custom-call | flops 8589934592 | bytes 20971520 | tf_op jit(solution)/shard_map/weight_grads/pallas_call | solution.py:306
  174.3 3.5 collective-permute-done.29.refs_1_
  179.0 18.7 %mlp_front.3 = (bf16[2048,1024]{1,0:T(8,128)(2,1)}, bf16[2048,1024]{1,0:T(8,128)(2,1)}, f32[1,1024]{1,0:T(1,128)}, bf16[1024,1024]{1,0:T(8,128)(2,1)}, bf16[1024,1024]{1,0:T(8,128)(2,1)}) custom-call(s32[1]{0:T(128)} %bitcast.place_ref, bf16[2048,1024]{1,0:T(8,128)(2,1)} %get-tuple-element.351.mn_ref, bf16[2048,1024]{1,0:T(8,128)(2,1)} %get-tuple-element.276.dy_ref, ...), custom_call_target="tpu_custom_call" | custom-call | flops 8589934592 | bytes 33554432 | tf_op jit(solution)/shard_map/mlp_front/pallas_call | solution.py:252
  204.5 16.1 %weight_grads.6 = (bf16[256,1024]{1,0:T(8,128)(2,1)}, bf16[256,1024]{1,0:T(8,128)(2,1)}, bf16[256,1024]{1,0:T(8,128)(2,1)}, bf16[256,1024]{1,0:T(8,128)(2,1)}, b...) custom-call(s32[1]{0:T(128)} %bitcast.place_ref, ...), custom_call_target="tpu_custom_call" | custom-call | flops 8589934592 | bytes 20971520 | tf_op jit(solution)/shard_map/weight_grads/pallas_call | solution.py:306
  225.9 45.1 %attention.3 = (bf16[2048,256]{1,0:T(8,128)(2,1)}, bf16[2048,768]{1,0:T(8,128)(2,1)}, bf16[1024,768]{1,0:T(8,128)(2,1)}, bf16[1024,256]{1,0:T(8,128)(2,1)}) custom-call(s32[1]{0:T(128)} %bitcast.place_ref, bf16[2048,1024]{1,0:T(8,128)(2,1)} %get-tuple-element.402.an_ref, bf16[2048,1024]{1,0:T(8,128)(2,1)} %get-tuple-element.276.dy_ref, ...), custom_call_target="tpu_custom_call" | custom-call | flops 21474836480 | bytes 37748736 | tf_op jit(solution)/shard_map/attention/pallas_call | solution.py:173
  273.7 9.9 %weight_grads.7 = (bf16[256,512]{1,0:T(8,128)(2,1)}, bf16[256,512]{1,0:T(8,128)(2,1)}, bf16[256,512]{1,0:T(8,128)(2,1)}, bf16[256,512]{1,0:T(8,128)(2,1)}, bf16[...) custom-call(s32[1]{0:T(128)} %bitcast.place_ref, ...), custom_call_target="tpu_custom_call" | custom-call | flops 4294967296 | bytes 14680064 | tf_op jit(solution)/shard_map/weight_grads/pallas_call | solution.py:306
  291.6 10.3 %branch_out.2 = bf16[1024,1024]{1,0:T(8,128)(2,1)} custom-call(bf16[2048,256]{1,0:T(8,128)(2,1)} %get-tuple-element.441.right_b.refs_0_, bf16[1024,256]{1,0:T(8,128)(2,1)} %get-tuple-element.423.refs_1_, bf16[2048,256]{1,0:T(8,128)(2,1)} %get-tuple-element.414.right_b.refs_2_, bf16[1024,256]{1,0:T(8,128)(2,1)} %get-tuple-element.424.refs_3_, ...), custom_call_target="tpu_custom_call" | custom-call | flops 5368709120 | bytes 12582912 | tf_op jit(solution)/shard_map/branch_out/pallas_call | solution.py:411
  304.8 14.9 %pull_back.2 = (f32[1024,1024]{1,0:T(8,128)}, f32[8,1024]{1,0:T(8,128)}) custom-call(bf16[2048,1024]{1,0:T(8,128)(2,1)} %get-tuple-element.330.right_a.refs_0_, bf16[1024,1024]{1,0:T(8,128)(2,1)} %get-tuple-element.435.refs_1_, bf16[2048,1024]{1,0:T(8,128)(2,1)} %get-tuple-element.436.right_a.refs_2_, bf16[1024,1024]{1,0:T(8,128)(2,1)} %get-tuple-element.437.refs_3_, ...), custom_call_target="tpu_custom_call" | custom-call | flops 7516192768 | bytes 23068672 | tf_op jit(solution)/shard_map/pull_back/pallas_call | solution.py:364
  322.4 14.6 %pull_back.3 = (bf16[1024,1024]{1,0:T(8,128)(2,1)}, f32[8,1024]{1,0:T(8,128)}) custom-call(bf16[2048,1024]{1,0:T(8,128)(2,1)} %get-tuple-element.330.right_a.refs_0_, bf16[1024,1024]{1,0:T(8,128)(2,1)} %get-tuple-element.435.refs_1_, bf16[2048,1024]{1,0:T(8,128)(2,1)} %get-tuple-element.436.right_a.refs_2_, bf16[1024,1024]{1,0:T(8,128)(2,1)} %get-tuple-element.437.refs_3_, ...), custom_call_target="tpu_custom_call" | custom-call | flops 7516192768 | bytes 23068672 | tf_op jit(solution)/shard_map/pull_back/pallas_call | solution.py:364
  345.4 5.2 %collective-permute-done.62 = f32[96,128]{1,0:T(8,128)S(1)} collective-permute-done((f32[96,128]{1,0:T(8,128)S(1)}, f32[96,128]{1,0:T(8,128)S(1)}, u32[]{:S(2)}, u32[]{:S(2)}) %collective-permute-start.62) | collective-permute-done | bytes 49184 | tf_op jit(solution)/shard_map/ppermute | solution.py:484
  355.3 3.5 collective-permute-done.49
  359.7 3.4 collective-permute-done.66
  363.3 12.0 %collective-permute-done.64 = f32[96,128]{1,0:T(8,128)S(1)} collective-permute-done((f32[96,128]{1,0:T(8,128)S(1)}, f32[96,128]{1,0:T(8,128)S(1)}, u32[]{:S(2)}, u32[]{:S(2)}) %collective-permute-start.64) | collective-permute-done | bytes 49184 | tf_op jit(solution)/shard_map/ppermute | solution.py:487
  377.1 4.4 %collective-permute-done.65 = f32[96,128]{1,0:T(8,128)S(1)} collective-permute-done((f32[96,128]{1,0:T(8,128)S(1)}, f32[96,128]{1,0:T(8,128)S(1)}, u32[]{:S(2)}, u32[]{:S(2)}) %collective-permute-start.65) | collective-permute-done | bytes 49184 | tf_op jit(solution)/shard_map/ppermute | solution.py:487
  383.0 9.6 %collective-permute-done.68 = bf16[256,512]{1,0:T(8,128)(2,1)S(1)} collective-permute-done((bf16[256,512]{1,0:T(8,128)(2,1)S(1)}, bf16[256,512]{1,0:T(8,128)(2,1)S(1)}, u32[]{:S(2)}, u32[]{:S(2)}) %collective-permute-start.68) | collective-permute-done | bytes 262176 | tf_op jit(solution)/shard_map/ppermute | solution.py:446
  394.4 8.5 %collective-permute-done.72 = bf16[256,1024]{1,0:T(8,128)(2,1)S(1)} collective-permute-done((bf16[256,1024]{1,0:T(8,128)(2,1)S(1)}, bf16[256,1024]{1,0:T(8,128)(2,1)S(1)}, u32[]{:S(2)}, u32[]{:S(2)}) %collective-permute-start.72) | collective-permute-done | bytes 524320 | tf_op jit(solution)/shard_map/ppermute | solution.py:446
  408.8 14.2 %branch_out.3 = (bf16[1024,1024]{1,0:T(8,128)(2,1)}, f32[1024,1024]{1,0:T(8,128)}) custom-call(bf16[2048,256]{1,0:T(8,128)(2,1)} %get-tuple-element.441.right_b.refs_0_, bf16[1024,256]{1,0:T(8,128)(2,1)} %get-tuple-element.423.refs_1_, bf16[2048,256]{1,0:T(8,128)(2,1)} %get-tuple-element.414.right_b.refs_2_, bf16[1024,256]{1,0:T(8,128)(2,1)} %get-tuple-element.424.refs_3_, ...), custom_call_target="tpu_custom_call" | custom-call | flops 5368709120 | bytes 29360128 | tf_op jit(solution)/shard_map/branch_out/pallas_call | solution.py:411
  (387 shorter events, 107.2 us)
Async XLA Ops:
  19.5 27.6 %collective-permute-start.1 = (bf16[256,512]{1,0:T(8,128)(2,1)S(1)}, bf16[256,512]{1,0:T(8,128)(2,1)S(1)}, u32[]{:S(2)}, u32[]{:S(2)}) collective-permute-start(bf16[256,512]{1,0:T(8,128)(2,1)S(1)} %pad_maximum_fusion.3.refs_0_), channel_id=1, source_target_pairs={{0,8},{4,12},{8,0},{12,4},{16,24},{20,28},{24,16},{28,20},{1,9},{5... | collective-permute-start | bytes 786440 | tf_op jit(solution)/shard_map/ppermute | solution.py:443
  21.0 26.1 %collective-permute-start.2 = (bf16[256,512]{1,0:T(8,128)(2,1)S(1)}, bf16[256,512]{1,0:T(8,128)(2,1)S(1)}, u32[]{:S(2)}, u32[]{:S(2)}) collective-permute-start(bf16[256,512]{1,0:T(8,128)(2,1)S(1)} %pad_maximum_fusion.3.refs_0_), channel_id=1, source_target_pairs={{0,16},{4,20},{8,24},{12,28},{16,0},{20,4},{24,8},{28,12},{1,17},{... | collective-permute-start | bytes 786440 | tf_op jit(solution)/shard_map/ppermute | solution.py:443
  56.7 51.8 %collective-permute-start.13 = (bf16[256,1024]{1,0:T(8,128)(2,1)S(1)}, bf16[256,1024]{1,0:T(8,128)(2,1)S(1)}, u32[]{:S(2)}, u32[]{:S(2)}) collective-permute-start(bf16[256,1024]{1,0:T(8,128)(2,1)S(1)} %pad_maximum_fusion.refs_0_), channel_id=1, source_target_pairs={{0,8},{4,12},{8,0},{12,4},{16,24},{20,28},{24,16},{28,20},{1,9},{5... | collective-permute-start | bytes 1572872 | tf_op jit(solution)/shard_map/ppermute | solution.py:443
  58.1 51.7 %collective-permute-start.14 = (bf16[256,1024]{1,0:T(8,128)(2,1)S(1)}, bf16[256,1024]{1,0:T(8,128)(2,1)S(1)}, u32[]{:S(2)}, u32[]{:S(2)}) collective-permute-start(bf16[256,1024]{1,0:T(8,128)(2,1)S(1)} %pad_maximum_fusion.refs_0_), channel_id=1, source_target_pairs={{0,16},{4,20},{8,24},{12,28},{16,0},{20,4},{24,8},{28,12},{1,17},{... | collective-permute-start | bytes 1572872 | tf_op jit(solution)/shard_map/ppermute | solution.py:443
  58.8 51.0 %collective-permute-start.15 = (bf16[256,1024]{1,0:T(8,128)(2,1)S(1)}, bf16[256,1024]{1,0:T(8,128)(2,1)S(1)}, u32[]{:S(2)}, u32[]{:S(2)}) collective-permute-start(bf16[256,1024]{1,0:T(8,128)(2,1)S(1)} %collective-permute-done.12.refs_4_), channel_id=1, source_target_pairs={{0,8},{4,12},{8,0},{12,4},{16,24},{20,28},{24,16},{28,20},{1,9},{5... | collective-permute-start | bytes 1572872 | tf_op jit(solution)/shard_map/ppermute | solution.py:443
  60.3 49.5 %collective-permute-start.16 = (bf16[256,1024]{1,0:T(8,128)(2,1)S(1)}, bf16[256,1024]{1,0:T(8,128)(2,1)S(1)}, u32[]{:S(2)}, u32[]{:S(2)}) collective-permute-start(bf16[256,1024]{1,0:T(8,128)(2,1)S(1)} %collective-permute-done.12.refs_4_), channel_id=1, source_target_pairs={{0,16},{4,20},{8,24},{12,28},{16,0},{20,4},{24,8},{28,12},{1,17},{... | collective-permute-start | bytes 1572872 | tf_op jit(solution)/shard_map/ppermute | solution.py:443
  63.2 48.8 %collective-permute-start.19 = (bf16[256,1024]{1,0:T(8,128)(2,1)S(1)}, bf16[256,1024]{1,0:T(8,128)(2,1)S(1)}, u32[]{:S(2)}, u32[]{:S(2)}) collective-permute-start(bf16[256,1024]{1,0:T(8,128)(2,1)S(1)} %collective-permute-done.12.refs_4_), channel_id=1, source_target_pairs={{0,1},{1,2},{2,3},{3,0},{4,5},{5,6},{6,7},{7,4},{8,9},{9,10},{10,1... | collective-permute-start | bytes 1572872 | tf_op jit(solution)/shard_map/ppermute | solution.py:446
  108.5 60.0 %collective-permute-start.28 = (bf16[256,512]{1,0:T(8,128)(2,1)S(1)}, bf16[256,512]{1,0:T(8,128)(2,1)}, u32[]{:S(2)}, u32[]{:S(2)}) collective-permute-start(bf16[256,512]{1,0:T(8,128)(2,1)S(1)} %collective-permute-done.27.refs_0_), channel_id=1, source_target_pairs={{0,1},{1,2},{2,3},{3,0},{4,5},{5,6},{6,7},{7,4},{8,9},{9,10},{10,1... | collective-permute-start | bytes 786440 | tf_op jit(solution)/shard_map/ppermute | solution.py:446
  169.9 28.6 %collective-permute-start.30 = (bf16[256,512]{1,0:T(8,128)(2,1)S(1)}, bf16[256,512]{1,0:T(8,128)(2,1)}, u32[]{:S(2)}, u32[]{:S(2)}) collective-permute-start(bf16[256,512]{1,0:T(8,128)(2,1)S(1)} %collective-permute-done.27.refs_0_), channel_id=1, source_target_pairs={{0,16},{4,20},{8,24},{12,28},{16,0},{20,4},{24,8},{28,12},{1,17},{... | collective-permute-start | bytes 786440 | tf_op jit(solution)/shard_map/ppermute | solution.py:443
  171.5 28.6 %collective-permute-start.31 = (bf16[256,512]{1,0:T(8,128)(2,1)}, bf16[256,512]{1,0:T(8,128)(2,1)}, u32[]{:S(2)}, u32[]{:S(2)}) collective-permute-start(bf16[256,512]{1,0:T(8,128)(2,1)} %collective-permute-done.28.refs_4_), channel_id=1, source_target_pairs={{0,8},{4,12},{8,0},{12,4},{16,24},{20,28},{24,16},{28,20},{1,9},{5... | collective-permute-start | bytes 786440 | tf_op jit(solution)/shard_map/ppermute | solution.py:443
  172.3 28.6 %collective-permute-start.32 = (bf16[256,512]{1,0:T(8,128)(2,1)}, bf16[256,512]{1,0:T(8,128)(2,1)}, u32[]{:S(2)}, u32[]{:S(2)}) collective-permute-start(bf16[256,512]{1,0:T(8,128)(2,1)} %collective-permute-done.28.refs_4_), channel_id=1, source_target_pairs={{0,16},{4,20},{8,24},{12,28},{16,0},{20,4},{24,8},{28,12},{1,17},{... | collective-permute-start | bytes 786440 | tf_op jit(solution)/shard_map/ppermute | solution.py:443
  172.9 28.0 %collective-permute-start.33 = (bf16[256,1024]{1,0:T(8,128)(2,1)}, bf16[256,1024]{1,0:T(8,128)(2,1)S(1)}, u32[]{:S(2)}, u32[]{:S(2)}) collective-permute-start(bf16[256,1024]{1,0:T(8,128)(2,1)} %get-tuple-element.346), channel_id=1, source_target_pairs={{0,16},{4,20},{8,24},{12,28},{16,0},{20,4},{24,8},{28,12},{1,17},{... | collective-permute-start | bytes 1572872 | tf_op jit(solution)/shard_map/ppermute | solution.py:443
  220.9 50.1 %collective-permute-start.35 = (bf16[256,1024]{1,0:T(8,128)(2,1)S(1)}, bf16[256,1024]{1,0:T(8,128)(2,1)S(1)}, u32[]{:S(2)}, u32[]{:S(2)}) collective-permute-start(bf16[256,1024]{1,0:T(8,128)(2,1)S(1)} %add_convert_fusion.6), channel_id=1, source_target_pairs={{0,8},{4,12},{8,0},{12,4},{16,24},{20,28},{24,16},{28,20},{1,9},{5... | collective-permute-start | bytes 1572872 | tf_op jit(solution)/shard_map/ppermute | solution.py:443
  221.8 49.2 %collective-permute-start.36 = (bf16[256,1024]{1,0:T(8,128)(2,1)S(1)}, bf16[256,1024]{1,0:T(8,128)(2,1)S(1)}, u32[]{:S(2)}, u32[]{:S(2)}) collective-permute-start(bf16[256,1024]{1,0:T(8,128)(2,1)S(1)} %copy-done.35), channel_id=1, source_target_pairs={{0,16},{4,20},{8,24},{12,28},{16,0},{20,4},{24,8},{28,12},{1,17},{... | collective-permute-start | bytes 1572872 | tf_op jit(solution)/shard_map/ppermute | solution.py:443
  222.4 48.6 %collective-permute-start.37 = (bf16[256,1024]{1,0:T(8,128)(2,1)S(1)}, bf16[256,1024]{1,0:T(8,128)(2,1)S(1)}, u32[]{:S(2)}, u32[]{:S(2)}) collective-permute-start(bf16[256,1024]{1,0:T(8,128)(2,1)S(1)} %copy-done.34), channel_id=1, source_target_pairs={{0,8},{4,12},{8,0},{12,4},{16,24},{20,28},{24,16},{28,20},{1,9},{5... | collective-permute-start | bytes 1572872 | tf_op jit(solution)/shard_map/ppermute | solution.py:443
  223.6 47.5 %collective-permute-start.41 = (bf16[256,1024]{1,0:T(8,128)(2,1)}, bf16[256,1024]{1,0:T(8,128)(2,1)S(1)}, u32[]{:S(2)}, u32[]{:S(2)}) collective-permute-start(bf16[256,1024]{1,0:T(8,128)(2,1)} %get-tuple-element.389), channel_id=1, source_target_pairs={{0,16},{4,20},{8,24},{12,28},{16,0},{20,4},{24,8},{28,12},{1,17},{... | collective-permute-start | bytes 1572872 | tf_op jit(solution)/shard_map/ppermute | solution.py:443
  225.1 46.0 %collective-permute-start.42 = (bf16[256,1024]{1,0:T(8,128)(2,1)}, bf16[256,1024]{1,0:T(8,128)(2,1)S(1)}, u32[]{:S(2)}, u32[]{:S(2)}) collective-permute-start(bf16[256,1024]{1,0:T(8,128)(2,1)} %get-tuple-element.393), channel_id=1, source_target_pairs={{0,8},{4,12},{8,0},{12,4},{16,24},{20,28},{24,16},{28,20},{1,9},{5... | collective-permute-start | bytes 1572872 | tf_op jit(solution)/shard_map/ppermute | solution.py:443
  286.1 33.6 %collective-permute-start.58 = (bf16[256,512]{1,0:T(8,128)(2,1)}, bf16[256,512]{1,0:T(8,128)(2,1)}, u32[]{:S(2)}, u32[]{:S(2)}) collective-permute-start(bf16[256,512]{1,0:T(8,128)(2,1)} %add_convert_fusion.10), channel_id=1, source_target_pairs={{0,16},{4,20},{8,24},{12,28},{16,0},{20,4},{24,8},{28,12},{1,17},{... | collective-permute-start | bytes 786440 | tf_op jit(solution)/shard_map/ppermute | solution.py:443
  288.4 31.9 %collective-permute-start.55 = (bf16[256,512]{1,0:T(8,128)(2,1)}, bf16[256,512]{1,0:T(8,128)(2,1)}, u32[]{:S(2)}, u32[]{:S(2)}) collective-permute-start(bf16[256,512]{1,0:T(8,128)(2,1)} %add_convert_fusion.11), channel_id=1, source_target_pairs={{0,8},{4,12},{8,0},{12,4},{16,24},{20,28},{24,16},{28,20},{1,9},{5... | collective-permute-start | bytes 786440 | tf_op jit(solution)/shard_map/ppermute | solution.py:443
  289.4 49.7 %collective-permute-start.54 = (bf16[256,1024]{1,0:T(8,128)(2,1)S(1)}, bf16[256,1024]{1,0:T(8,128)(2,1)S(1)}, u32[]{:S(2)}, u32[]{:S(2)}) collective-permute-start(bf16[256,1024]{1,0:T(8,128)(2,1)S(1)} %add_convert_fusion.3), channel_id=1, source_target_pairs={{0,16},{4,20},{8,24},{12,28},{16,0},{20,4},{24,8},{28,12},{1,17},{... | collective-permute-start | bytes 1572872 | tf_op jit(solution)/shard_map/ppermute | solution.py:443
  302.1 37.6 %collective-permute-start.51 = (bf16[256,1024]{1,0:T(8,128)(2,1)S(1)}, bf16[256,1024]{1,0:T(8,128)(2,1)S(1)}, u32[]{:S(2)}, u32[]{:S(2)}) collective-permute-start(bf16[256,1024]{1,0:T(8,128)(2,1)S(1)} %add_convert_fusion.4), channel_id=1, source_target_pairs={{0,8},{4,12},{8,0},{12,4},{16,24},{20,28},{24,16},{28,20},{1,9},{5... | collective-permute-start | bytes 1572872 | tf_op jit(solution)/shard_map/ppermute | solution.py:443
  354.9 26.8 %collective-permute-start.71 = (bf16[256,1024]{1,0:T(8,128)(2,1)S(1)}, bf16[256,1024]{1,0:T(8,128)(2,1)S(1)}, u32[]{:S(2)}, u32[]{:S(2)}) collective-permute-start(bf16[256,1024]{1,0:T(8,128)(2,1)S(1)} %add_convert_fusion.1), channel_id=1, source_target_pairs={{0,1},{1,2},{2,3},{3,0},{4,5},{5,6},{6,7},{7,4},{8,9},{9,10},{10,1... | collective-permute-start | bytes 1572872 | tf_op jit(solution)/shard_map/ppermute | solution.py:446
  376.5 32.3 %collective-permute-start.59 = (bf16[1024,1024]{1,0:T(8,128)(2,1)}, bf16[1024,1024]{1,0:T(8,128)(2,1)}, u32[]{:S(2)}, u32[]{:S(2)}) collective-permute-start(bf16[1024,1024]{1,0:T(8,128)(2,1)} %branch_out.2), channel_id=1, source_target_pairs={{0,4},{4,0},{8,12},{12,8},{16,20},{20,16},{24,28},{28,24},{1,5},{5... | collective-permute-start | bytes 6291464 | tf_op jit(solution)/shard_map/ppermute | solution.py:440
  376.6 32.3 %collective-permute-start.60 = (bf16[1024,1024]{1,0:T(8,128)(2,1)}, bf16[1024,1024]{1,0:T(8,128)(2,1)}, u32[]{:S(2)}, u32[]{:S(2)}) collective-permute-start(bf16[1024,1024]{1,0:T(8,128)(2,1)} %get-tuple-element.461), channel_id=1, source_target_pairs={{0,4},{4,0},{8,12},{12,8},{16,20},{20,16},{24,28},{28,24},{1,5},{5... | collective-permute-start | bytes 6291464 | tf_op jit(solution)/shard_map/ppermute | solution.py:440
  (115 other events, 2005.1 us)

commit v3 on v2

v3 whole, which is shorter than its diff:
```python
from functools import partial
import math

import jax
import jax.numpy as jnp
from jax import lax
from jax.experimental import pallas as pl
from jax.experimental.pallas import tpu as pltpu
from jax.sharding import PartitionSpec as P

HD = 64
ROT = 16
EPS = 1e-05
MASKED = 1e30
F32 = jnp.float32
BF16 = jnp.bfloat16
VMEM_BYTES = 56 * 1024 * 1024
NT = (((1,), (1,)), ((), ()))
TN = (((0,), (0,)), ((), ()))
NN = (((1,), (0,)), ((), ()))

dot32 = partial(lax.dot_general, preferred_element_type=F32)


def whole_spec(value):
    return pl.BlockSpec(value.shape, lambda *_: (0,) * value.ndim)


def place_rows(piece, key, place_ref, whole):
    rows = piece.shape[0]
    if rows == whole.shape[0]:
        return slice(None)
    return pl.ds(pl.multiple_of((place_ref[0] ^ key) * rows, rows), rows)


def prepare_kernel(x_own, x_other, dy_own, dy_other, gain_ref, an_ref, mn_ref, dy_ref):
    step = pl.program_id(0)
    half = pl.num_programs(0) // 2

    def work(x_ref, grad_ref):
        xhat, _ = row_norm(x_ref[...].astype(F32))
        an = (xhat * gain_ref[0:1, :] + gain_ref[1:2, :]).astype(BF16)
        mn = (xhat * gain_ref[2:3, :] + gain_ref[3:4, :]).astype(BF16)
        dy = grad_ref[...]
        an_ref[...], mn_ref[...], dy_ref[...] = an, mn, dy

    @pl.when(step < half)
    def _():
        work(x_own, dy_own)

    @pl.when(step >= half)
    def _():
        work(x_other, dy_other)


def prepare(x_own, x_other, dy_own, dy_other, gains):
    rows, depth = x_own.shape
    br = min(512, rows)
    half = rows // br
    own = pl.BlockSpec((br, depth), lambda i: (jnp.minimum(i, half - 1), 0))
    other = pl.BlockSpec((br, depth), lambda i: (jnp.maximum(i - half, 0), 0))
    tall = pl.BlockSpec((br, depth), lambda i: (i, 0))
    return pl.pallas_call(
        prepare_kernel,
        grid=(2 * half,),
        in_specs=[own, other, own, other, whole_spec(gains)],
        out_specs=[tall] * 3,
        out_shape=[jax.ShapeDtypeStruct((2 * rows, depth), BF16)] * 3,
        compiler_params=pltpu.CompilerParams(vmem_limit_bytes=VMEM_BYTES),
        cost_estimate=pl.CostEstimate(
            flops=40 * rows * depth, bytes_accessed=32 * rows * depth, transcendentals=2 * rows
        ),
        name="prepare",
    )(x_own, x_other, dy_own, dy_other, gains)


def attention_kernel(place_ref, an_ref, dy_ref, bias_ref, cos_ref, sa_ref, sb_ref, qf_ref, kf_ref, *refs, keys, bq):
    length = an_ref.shape[0]
    width = 2 * HD
    count = len(keys)
    piece_refs, refs = refs[: sum(map(len, keys))], refs[sum(map(len, keys)) :]
    att_ref, dmix_ref, sum_ref, qkv_ref, out_ref, mixed_scr, do_scr, dk_scr, dv_scr = refs
    seq, pair = pl.program_id(0), pl.program_id(1)

    @pl.when((seq == 0) & (pair == 0))
    def _():
        at = 0
        for j, pair_keys in enumerate(keys):
            for ref, (key, lead) in zip(piece_refs[at : at + len(pair_keys)], pair_keys):
                into = place_rows(ref, key, place_ref, qkv_ref)
                qkv_ref[into, j * 3 * width : (j + 1) * 3 * width] = ref[:, lead : lead + 3 * width]
                out_ref[into, j * width : (j + 1) * width] = ref[:, lead + 3 * width : lead + 4 * width]
            at += len(pair_keys)

    @pl.when(pair == 0)
    def _():
        step = min(256, length)
        for r in range(0, length, step):
            mixed = dot32(an_ref[r : r + step, :], qkv_ref[...], NN) + bias_ref[...]
            do = dot32(dy_ref[r : r + step, :], out_ref[...], NN).astype(BF16)
            for j in range(count):
                mixed_scr[j, r : r + step, :] = mixed[:, j * 3 * width : (j + 1) * 3 * width]
                do_scr[j, r : r + step, :] = do[:, j * width : (j + 1) * width]

    mixed = mixed_scr.at[pair]
    cos, sa, sb = cos_ref[...], sa_ref[...], sb_ref[...]
    scale = 1.0 / math.sqrt(HD)
    half = ROT // 2

    def turn(v, c, a, b, sign):
        side = pltpu.roll(v, width - half, 1) * a + pltpu.roll(v, half, 1) * b
        return v * c + side if sign > 0 else v * c - side

    q = turn(mixed[:, 0:width], cos, sa, sb, 1).astype(BF16)
    k = turn(mixed[:, width : 2 * width], cos, sa, sb, 1).astype(BF16)
    v = mixed[:, 2 * width : 3 * width].astype(BF16)
    do = do_scr[pair]
    lane = lax.broadcasted_iota(jnp.int32, (length, width), 1)
    zero = jnp.zeros((), BF16)
    qs = (q.astype(F32) * scale).astype(BF16)
    qf = qf_ref[...]
    kaug = jnp.concatenate([k, kf_ref[...]], axis=1)
    heads = []
    for h in range(2):
        m = (lane // HD) == h
        qm = jnp.where(m, qs, zero)
        heads.append(
            (
                jnp.concatenate([qm, qf], axis=1),
                qm,
                jnp.where(m, k, zero),
                jnp.where(m, v, zero),
                jnp.where(m, do, zero),
            )
        )
    causal = lax.broadcasted_iota(jnp.int32, (bq, bq), 1) <= lax.broadcasted_iota(jnp.int32, (bq, bq), 0)
    blocks = length // bq
    for i in range(blocks):
        r0 = i * bq
        w = r0 + bq
        att = dq = dkp = dvp = None
        for qaug, qm, km, vm, dom in heads:
            s = dot32(qaug[r0:w], kaug[:w], NT)
            diagonal = jnp.where(causal, s[:, r0:], -MASKED)
            s = diagonal if i == 0 else jnp.concatenate([s[:, :r0], diagonal], axis=1)
            e = jnp.exp(s - jnp.max(s, axis=1, keepdims=True))
            p = e * (1.0 / jnp.sum(e, axis=1, keepdims=True))
            pb = p.astype(BF16)
            o = dot32(pb, vm[:w], NN)
            dp = dot32(dom[r0:w], v[:w], NT)
            delta = jnp.sum(p * dp, axis=1, keepdims=True)
            ds = (p * (dp - delta)).astype(BF16)
            x = dot32(ds, km[:w], NN)
            a = dot32(pb, dom[r0:w], TN)
            b = dot32(ds, qm[r0:w], TN)
            if att is None:
                att, dq, dvp, dkp = o, x, a, b
            else:
                att, dq, dvp, dkp = att + o, dq + x, dvp + a, dkp + b
        att_ref[r0:w, :] = att.astype(BF16)
        dmix_ref[r0:w, 0:width] = turn(dq * scale, cos[r0:w], sa[r0:w], sb[r0:w], -1).astype(BF16)
        if i > 0:
            dk_scr[:r0] += dkp[:r0]
            dv_scr[:r0] += dvp[:r0]
        dk_scr[r0:w] = dkp[r0:]
        dv_scr[r0:w] = dvp[r0:]
    dmix_ref[:, width : 2 * width] = turn(dk_scr[...], cos, sa, sb, -1).astype(BF16)
    dmix_ref[:, 2 * width : 3 * width] = dv_scr[...].astype(BF16)
    part = jnp.sum(dmix_ref[...].astype(F32), axis=0, keepdims=True)

    @pl.when(seq == 0)
    def _():
        sum_ref[pair] = part

    @pl.when(seq > 0)
    def _():
        sum_ref[pair] += part


def attention(pairs, place, an, dy, bias, tables, length):
    rows, depth = an.shape
    width = 2 * HD
    seqs = rows // length
    count = len(pairs)
    row = pl.BlockSpec((length, depth), lambda s, j, p: (s, 0))
    table = pl.BlockSpec((length, width), lambda s, j, p: (s, 0))
    pieces = [piece for pair in pairs for piece, _, _ in pair]
    units = seqs * count
    shapes = [
        jax.ShapeDtypeStruct((rows, count * width), BF16),
        jax.ShapeDtypeStruct((rows, count * 3 * width), BF16),
        jax.ShapeDtypeStruct((count, 1, 3 * width), F32),
        jax.ShapeDtypeStruct((depth, count * 3 * width), BF16),
        jax.ShapeDtypeStruct((depth, count * width), BF16),
    ]
    return pl.pallas_call(
        partial(attention_kernel, keys=[[v[1:] for v in pair] for pair in pairs], bq=min(512, length)),
        grid_spec=pltpu.PrefetchScalarGridSpec(
            num_scalar_prefetch=1,
            grid=(seqs, count),
            in_specs=[row, row, whole_spec(bias)] + [table] * 5 + [whole_spec(v) for v in pieces],
            out_specs=[
                pl.BlockSpec((length, width), lambda s, j, p: (s, j)),
                pl.BlockSpec((length, 3 * width), lambda s, j, p: (s, j)),
            ]
            + [whole_spec(v) for v in shapes[2:]],
            scratch_shapes=[
                pltpu.VMEM((count, length, 3 * width), F32),
                pltpu.VMEM((count, length, width), BF16),
                pltpu.VMEM((length, width), F32),
                pltpu.VMEM((length, width), F32),
            ],
        ),
        out_shape=shapes,
        compiler_params=pltpu.CompilerParams(vmem_limit_bytes=VMEM_BYTES),
        cost_estimate=pl.CostEstimate(
            flops=units * (32 * length * length * width + 8 * length * depth * width),
            bytes_accessed=units * length * (depth * 4 + width * 40),
            transcendentals=units * 2 * length * length,
        ),
        name="attention",
    )(place, an, dy, bias, *tables, *pieces)


def mlp_kernel(place_ref, mn_ref, dy_ref, bias_ref, *refs, keys):
    piece_refs, refs = refs[: sum(map(len, keys))], refs[sum(map(len, keys)) :]
    act_ref, dgate_ref, sum_ref, up_ref, down_ref = refs
    units = up_ref.shape[1] // len(keys)
    step = pl.program_id(0)

    @pl.when(step == 0)
    def _():
        at = 0
        for j, slot_keys in enumerate(keys):
            for ref, (key, lead) in zip(piece_refs[at : at + len(slot_keys)], slot_keys):
                into = place_rows(ref, key, place_ref, up_ref)
                up_ref[into, j * units : (j + 1) * units] = ref[:, lead : lead + units]
                down_ref[into, j * units : (j + 1) * units] = ref[:, lead + units : lead + 2 * units]
            at += len(slot_keys)

    part = []
    for c in range(0, up_ref.shape[1], units):
        col = slice(c, c + units)
        gate = dot32(mn_ref[...], up_ref[:, col], NN) + bias_ref[:, col]
        dact = dot32(dy_ref[...], down_ref[:, col], NN)
        e = jnp.exp(gate * gate * -0.5)
        pdf = e * (1.0 / math.sqrt(2.0 * math.pi))
        cdf = 0.5 + 0.5 * lax.erf(gate * math.sqrt(0.5))
        act_ref[:, col] = (gate * cdf).astype(BF16)
        dgate = (dact * (cdf + gate * pdf)).astype(BF16)
        dgate_ref[:, col] = dgate
        part.append(jnp.sum(dgate.astype(F32), axis=0, keepdims=True))
    part = jnp.concatenate(part, axis=1)

    @pl.when(step == 0)
    def _():
        sum_ref[...] = part

    @pl.when(step > 0)
    def _():
        sum_ref[...] += part


def mlp_front(slots, place, mn, dy, bias):
    rows, depth = mn.shape
    units = bias.shape[1] // len(slots)
    count = len(slots)
    br = min(512, rows)
    row = pl.BlockSpec((br, depth), lambda r, p: (r, 0))
    tile = pl.BlockSpec((br, count * units), lambda r, p: (r, 0))
    pieces = [piece for slot in slots for piece, _, _ in slot]
    shapes = [
        jax.ShapeDtypeStruct((rows, count * units), BF16),
        jax.ShapeDtypeStruct((rows, count * units), BF16),
        jax.ShapeDtypeStruct((1, count * units), F32),
        jax.ShapeDtypeStruct((depth, count * units), BF16),
        jax.ShapeDtypeStruct((depth, count * units), BF16),
    ]
    return pl.pallas_call(
        partial(mlp_kernel, keys=[[v[1:] for v in slot] for slot in slots]),
        grid_spec=pltpu.PrefetchScalarGridSpec(
            num_scalar_prefetch=1,
            grid=(rows // br,),
            in_specs=[row, row, whole_spec(bias)] + [whole_spec(v) for v in pieces],
            out_specs=[tile, tile] + [whole_spec(v) for v in shapes[2:]],
        ),
        out_shape=shapes,
        compiler_params=pltpu.CompilerParams(vmem_limit_bytes=VMEM_BYTES),
        cost_estimate=pl.CostEstimate(
            flops=4 * rows * depth * count * units,
            bytes_accessed=rows * depth * 4 + count * (units * depth * 8 + rows * units * 4),
            transcendentals=2 * rows * count * units,
        ),
        name="mlp_front",
    )(place, mn, dy, bias, *pieces)


def grads_kernel(place_ref, left_a, left_b, right_a, right_b, *refs, count, keys):
    outs, (sum_a, sum_b) = refs[:-2], refs[-2:]
    step = pl.program_id(0)

    @pl.when(step == 0)
    def _():
        sum_a[...] = dot32(left_a[...], right_a[...], TN)
        sum_b[...] = dot32(left_b[...], right_b[...], TN)

    @pl.when(step > 0)
    def _():
        sum_a[...] += dot32(left_a[...], right_a[...], TN)
        sum_b[...] += dot32(left_b[...], right_b[...], TN)

    @pl.when(step == pl.num_programs(0) - 1)
    def _():
        wa, wb = right_a.shape[1] // count, right_b.shape[1] // count
        width = wa + wb
        for j in range(count):
            for n, key in enumerate(keys):
                out = outs[j] if key == 3 else outs[n + count - 1 if len(keys) > 1 else 0]
                at = place_rows(out, key, place_ref, sum_a)
                first = 0 if key == 3 else j * width
                out[:, first : first + wa] = sum_a[at, j * wa : (j + 1) * wa].astype(BF16)
                out[:, first + wa : first + width] = sum_b[at, j * wb : (j + 1) * wb].astype(BF16)


def weight_grads(place, places, left_a, right_a, left_b, right_b, count):
    rows, depth = left_a.shape
    keys = (3, 1, 2, 0) if places == 4 else (0,)
    size = depth // len(keys)
    br = min(512, rows)
    wa, wb = right_a.shape[1], right_b.shape[1]
    block = lambda v: pl.BlockSpec((br, v.shape[1]), lambda i, p: (i, 0))
    far = jax.ShapeDtypeStruct((size, (wa + wb) // count), BF16)
    near = jax.ShapeDtypeStruct((size, wa + wb), BF16)
    shapes = [far] * count + [near] * 3 if places == 4 else [near]
    found = pl.pallas_call(
        partial(grads_kernel, count=count, keys=keys),
        grid_spec=pltpu.PrefetchScalarGridSpec(
            num_scalar_prefetch=1,
            grid=(rows // br,),
            in_specs=[block(v) for v in (left_a, left_b, right_a, right_b)],
            out_specs=[whole_spec(v) for v in shapes],
            scratch_shapes=[pltpu.VMEM((depth, wa), F32), pltpu.VMEM((depth, wb), F32)],
        ),
        out_shape=shapes,
        compiler_params=pltpu.CompilerParams(vmem_limit_bytes=VMEM_BYTES),
        cost_estimate=pl.CostEstimate(
            flops=2 * rows * depth * (wa + wb),
            bytes_accessed=4 * rows * depth + 2 * (wa + wb) * (rows + depth),
            transcendentals=0,
        ),
        name="weight_grads",
    )(place, left_a, left_b, right_a, right_b)
    return found


def row_norm(x):
    centre = x - jnp.mean(x, axis=-1, keepdims=True)
    rstd = lax.rsqrt(jnp.mean(centre * centre, axis=-1, keepdims=True) + EPS)
    return centre * rstd, rstd


def pull_kernel(*refs):
    dg0, up0, dg1, up1, dm0, qkv0, dm1, qkv1, x_ref, gain_ref = refs[:10]
    out_ref, sum_ref = refs[-2:]
    n_mlp = dot32(dg0[...], up0[...], NT) + dot32(dg1[...], up1[...], NT)
    n_attn = dot32(dm0[...], qkv0[...], NT) + dot32(dm1[...], qkv1[...], NT)
    xhat, rstd = row_norm(x_ref[...].astype(F32))
    u = n_attn * gain_ref[0:1, :] + n_mlp * gain_ref[2:3, :]
    parts = [jnp.sum(v, axis=0, keepdims=True) for v in (n_attn * xhat, n_attn, n_mlp * xhat, n_mlp)]
    part = jnp.concatenate(parts + [jnp.zeros((4, u.shape[1]), F32)], axis=0)

    @pl.when(pl.program_id(0) == 0)
    def _():
        sum_ref[...] = part

    @pl.when(pl.program_id(0) > 0)
    def _():
        sum_ref[...] += part

    out_ref[...] = u.astype(out_ref.dtype)


def pull_back(terms, x, gains, first_row, dtype):
    rows, depth = x.shape
    br = min(256, rows)
    first = first_row // br
    block = lambda v: pl.BlockSpec((br, v.shape[1]), lambda i: (i + first, 0))
    specs, args = [], []
    for grad, weight in terms:
        specs += [block(grad), whole_spec(weight)]
        args += [grad, weight]
    tile = pl.BlockSpec((br, depth), lambda i: (i, 0))
    width = sum(grad.shape[1] for grad, _ in terms)
    return pl.pallas_call(
        pull_kernel,
        grid=(rows // br,),
        in_specs=specs + [tile, whole_spec(gains)],
        out_specs=[tile, pl.BlockSpec((8, depth), lambda i: (0, 0))],
        out_shape=[jax.ShapeDtypeStruct((rows, depth), dtype), jax.ShapeDtypeStruct((8, depth), F32)],
        compiler_params=pltpu.CompilerParams(vmem_limit_bytes=VMEM_BYTES),
        cost_estimate=pl.CostEstimate(
            flops=2 * rows * width * depth,
            bytes_accessed=2 * width * (rows + depth) + rows * depth * 8,
            transcendentals=rows,
        ),
        name="pull_back",
    )(*args, x, gains)


def out_kernel(*refs, own):
    att0, out0, att1, out1, act0, down0, act1, down1 = refs[:8]
    y = dot32(act0[...], down0[...], NT) + dot32(act1[...], down1[...], NT)
    y = y + dot32(att0[...], out0[...], NT) + dot32(att1[...], out1[...], NT)
    if not own:
        refs[-1][...] = y.astype(BF16)
        return
    x_ref, other_ref, bias_ref, dy_ref, pull_ref, other_pull_ref, y_ref, grad_ref = refs[8:]
    x = x_ref[...].astype(F32)
    y_ref[...] = (y + x + other_ref[...].astype(F32) + bias_ref[...]).astype(BF16)
    xhat, rstd = row_norm(x)
    u = pull_ref[...] + other_pull_ref[...].astype(F32)
    u = u - jnp.mean(u, axis=-1, keepdims=True) - xhat * jnp.mean(u * xhat, axis=-1, keepdims=True)
    grad_ref[...] = dy_ref[...].astype(F32) + rstd * u


def branch_out(terms, rows, last=None):
    own = last is not None
    depth = terms[0][1].shape[0]
    br = min(256, rows)
    first = 0 if own else rows // br
    tile = pl.BlockSpec((br, depth), lambda i: (i, 0))
    specs, args = [], []
    for value, weight in terms:
        specs += [pl.BlockSpec((br, value.shape[1]), lambda i: (i + first, 0)), whole_spec(weight)]
        args += [value, weight]
    if own:
        specs += [whole_spec(v) if v.shape[0] == 1 else tile for v in last]
        args += last
    width = sum(value.shape[1] for value, _ in terms)
    shapes = [jax.ShapeDtypeStruct((rows, depth), BF16)] + [jax.ShapeDtypeStruct((rows, depth), F32)] * own
    return pl.pallas_call(
        partial(out_kernel, own=own),
        grid=(rows // br,),
        in_specs=specs,
        out_specs=[tile] * len(shapes),
        out_shape=shapes,
        compiler_params=pltpu.CompilerParams(vmem_limit_bytes=VMEM_BYTES),
        cost_estimate=pl.CostEstimate(
            flops=2 * rows * width * depth,
            bytes_accessed=2 * width * (rows + depth) + rows * depth * (18 if own else 2),
            transcendentals=0,
        ),
        name="branch_out",
    )(*args)


class Links:
    def __init__(self):
        self.fsdp = lax.axis_size("fsdp")
        self.tp = lax.axis_size("tp")
        index = lax.axis_index("fsdp")
        self.core = index % 2
        self.place = index // 2
        self.lane = lax.axis_index("tp")
        self.places = self.fsdp // 2
        self.cores = [list(range(c, self.fsdp, 2)) for c in range(2)]
        self.bits = [1 << b for b in range((self.places - 1).bit_length())]

    def swap(self, value):
        return lax.ppermute(value, "fsdp", [(i, i ^ 1) for i in range(self.fsdp)])

    def hop(self, value, bit):
        return lax.ppermute(value, "fsdp", [(i, i ^ (2 * bit)) for i in range(self.fsdp)])

    def ring(self, value):
        return lax.ppermute(value, "tp", [(i, (i + 1) % self.tp) for i in range(self.tp)])


    def near_places(self, piece):
        return self.hop(piece, 1), self.hop(piece, 2)

    def far_parts(self, near):
        cut = near[0].shape[1] // 2
        return near[1][:, :cut], near[0][:, cut:]

    def far_place(self, parts):
        return self.hop(parts[0], 1), self.hop(parts[1], 2)

    def scatter_far(self, far):
        return self.hop(far[0], 2), self.hop(far[1], 1)

    def add_far(self, one, two, far):
        cut = one.shape[1] // 2
        first = (one[:, :cut].astype(F32) + far[0].astype(F32)).astype(BF16)
        second = (two[:, cut:].astype(F32) + far[1].astype(F32)).astype(BF16)
        return lax.dynamic_update_slice(one, first, (0, 0)), lax.dynamic_update_slice(two, second, (0, cut))

    def scatter_near(self, one, two):
        return self.hop(one, 1), self.hop(two, 2)

    def gather_other(self, piece):
        return lax.all_gather(piece, "fsdp", axis=0, tiled=True, axis_index_groups=self.cores)

    def scatter_other(self, value):
        return lax.psum_scatter(
            value, "fsdp", scatter_dimension=0, tiled=True, axis_index_groups=self.cores
        )

    def ring_sum(self, total, terms):
        for term in terms:
            total = term if total is None else total + term
            total = self.ring(total.astype(BF16)).astype(F32)
        return total

    def sum_steps(self):
        steps = [("fsdp", self.fsdp, 1 << b) for b in range((self.fsdp - 1).bit_length())]
        return steps + [("tp", self.tp, 1 << b) for b in range((self.tp - 1).bit_length())]

    def sum_step(self, value, step):
        name, size, bit = step
        return value + lax.ppermute(value, name, [(i, i ^ bit) for i in range(size)])


def pick(value, index, axis):
    return lax.dynamic_index_in_dim(value, index, axis, keepdims=False)


def pair_rows(links, mine, other):
    got = links.swap(other)
    first = jnp.where(links.core == 0, mine, got)
    second = jnp.where(links.core == 0, got, mine)
    return jnp.concatenate([first, second], axis=0)


def unpair_rows(links, block):
    half = block.shape[0] // 2
    mine = lax.dynamic_slice_in_dim(block, links.core * half, half, 0)
    got = links.swap(lax.dynamic_slice_in_dim(block, (1 - links.core) * half, half, 0))
    return jnp.where(links.core == 0, mine, got), jnp.where(links.core == 0, got, mine)


sync = lax.optimization_barrier


def tables_of(segment_rows):
    seqs, length = segment_rows.shape
    width = 2 * HD
    starts = jnp.sum((segment_rows[:, None, :] < segment_rows[:, :, None]).astype(jnp.int32), axis=-1)
    places = (jnp.arange(length, dtype=jnp.int32)[None] - starts).reshape(-1).astype(F32)
    inverse_freq = jnp.power(10000.0, -jnp.arange(0, ROT, 2, dtype=F32) / ROT)
    angles = places[:, None] * jnp.tile(inverse_freq, width // (ROT // 2))[None, :]
    lane = jnp.arange(width, dtype=jnp.int32)[None, :]
    turn = lane % HD
    cos = jnp.where(turn < ROT, jnp.cos(angles), 1.0)
    sine = jnp.sin(angles)
    sa = jnp.where(turn < ROT // 2, -sine, 0.0)
    sb = jnp.where((turn >= ROT // 2) & (turn < ROT), sine, 0.0)
    same = segment_rows.reshape(-1, 1) == lane
    key_mark = jnp.where(same, 1.0, 0.0).astype(BF16)
    query_mark = jnp.where(same | (lane >= 8), 0.0, -MASKED).astype(BF16)
    return cos, sa, sb, query_mark, key_mark


def body(
    tokens,
    segments,
    attn_gain,
    attn_shift,
    mlp_gain,
    mlp_shift,
    qkv_weight,
    qkv_bias,
    out_weight,
    out_bias,
    up_weight,
    up_bias,
    down_weight,
    down_bias,
    cotangent,
):
    links = Links()
    tp = links.tp
    rows, depth = tokens.shape
    length = segments.shape[1]
    head_cols = qkv_weight.shape[2] // 2
    unit_cols = up_weight.shape[1] // 2

    def halves(shard, axis):
        size = shard.shape[axis] // 2
        return [lax.dynamic_slice_in_dim(shard, c * size, size, axis) for c in (links.core, 1 - links.core)]

    qkv_halves = [v.reshape(v.shape[0], -1) for v in halves(qkv_weight, 2)]
    out_halves = [v.T for v in halves(out_weight, 0)]
    up_halves = halves(up_weight, 1)
    down_halves = [v.T for v in halves(down_weight, 0)]
    attn_slots = [pair_rows(links, *[jnp.concatenate(v, axis=1) for v in zip(qkv_halves, out_halves)])]
    mlp_slots = [pair_rows(links, *[jnp.concatenate(v, axis=1) for v in zip(up_halves, down_halves)])]
    qkv_cols = 3 * head_cols

    half = tp // 2
    per = max(1, 2 * HD // head_cols)

    by_hops = links.places == 4 and per == 1
    place = jnp.full((1,), links.place if by_hops else 0, jnp.int32)

    def join_pair(slots):
        if per == 1:
            return slots[0]
        lead = slots[0].shape[0]
        return jnp.concatenate([v.reshape(lead, 4, head_cols) for v in slots], axis=2).reshape(lead, -1)

    def join_qkv(slots):
        if per == 1:
            return slots[0]
        lead = slots[0].shape[0]
        return jnp.concatenate([v.reshape(lead, 3, head_cols) for v in slots], axis=2).reshape(lead, -1)

    def split_pair(value, parts):
        if per == 1:
            return [value]
        lead = value.shape[0]
        blocks = value.reshape(lead, parts, per, head_cols)
        return [blocks[:, :, j].reshape(lead, -1) for j in range(per)]

    groups = [list(range(0, half)), list(range(half, tp))]

    lane_of = [(links.lane - s) % tp for s in range(tp)]
    qkv_bias_lanes = pick(qkv_bias.reshape(3, tp, 2, head_cols), links.core, 2)
    up_bias_lanes = pick(up_bias.reshape(tp, 2, unit_cols), links.core, 1)
    qkv_bias_groups = [
        jnp.concatenate(
            [
                join_qkv([pick(qkv_bias_lanes, lane_of[s], 1).reshape(1, -1) for s in g[i : i + per]])
                for i in range(0, half, per)
            ],
            axis=1,
        ).astype(F32)
        for g in groups
    ]
    up_bias_groups = [
        jnp.concatenate([pick(up_bias_lanes, lane_of[s], 0) for s in g]).astype(F32)[None] for g in groups
    ]

    gains = jnp.stack([v.astype(F32) for v in (attn_gain, attn_shift, mlp_gain, mlp_shift)])
    x_other, dy_other = links.swap(tokens), links.swap(cotangent)

    def group_piece(slots):
        return jnp.concatenate(slots, axis=1)

    def near(piece):
        return links.near_places(piece) if by_hops else links.gather_other(piece)

    def far_parts(got):
        return links.far_parts(got) if by_hops else ()

    def far(parts):
        return links.far_place(parts) if by_hops else ()

    def pieces_of(piece, got, last, width):
        if not by_hops:
            return [[(got, 0, j * width)] for j in range(half)]
        return [[(piece, 0, j * width), (got[0], 1, j * width), (got[1], 2, j * width), (last[j], 3, 0)] for j in (0, 1)]

    def pairs_of(slots):
        if per == 1:
            return slots
        columns = [v[0][0][:, v[0][2] : v[0][2] + 4 * head_cols] for v in slots]
        return [[(join_pair(columns[i : i + per]), 0, 0)] for i in range(0, half, per)]

    def attention_part(g, slots, an, dy):
        return attention(pairs_of(slots), place, an, dy, qkv_bias_groups[g], tables, length)

    def attention_grads(attended, dmixed):
        found = weight_grads(place, links.places if by_hops else 1, an, dmixed, dy2, attended, half // per)
        if per == 1:
            return found
        pairs = jnp.split(found[0], half // per, axis=1)
        return [jnp.concatenate([v for pair in pairs for v in split_pair(pair, 4)], axis=1)]

    def mlp_grads(active, dgate):
        return weight_grads(place, links.places if by_hops else 1, mn, dgate, dy2, active, half)

    def sum_far(blocks):
        return links.scatter_far(blocks[:2]) if by_hops else links.scatter_other(blocks[0])

    def add_far(blocks, got):
        return links.add_far(blocks[2], blocks[3], got) if by_hops else got

    def sum_near(sent):
        return links.scatter_near(*sent) if by_hops else sent

    def place_sum(blocks, got):
        if by_hops:
            got = blocks[4].astype(F32) + got[0].astype(F32) + got[1].astype(F32)
        return jnp.split(got.astype(F32), half, axis=1)

    def small_sums():
        def spread(values):
            lead, cols = values[0].shape
            full = jnp.zeros((lead, tp, 2, cols), F32)
            for s, value in enumerate(values):
                full = lax.dynamic_update_slice(full, value.reshape(lead, 1, 1, cols), (0, lane_of[s], links.core, 0))
            return full.reshape(-1)

        pair_sums = [v[i] for v in (qkv_sum0, qkv_sum1) for i in range(half // per)]
        qkv_bias_part = spread([v.reshape(3, head_cols) for d in pair_sums for v in split_pair(d, 3)])
        up_bias_part = spread([v for part in (gate_sum0, gate_sum1) for v in jnp.split(part, half, axis=1)])
        bias_part = jnp.sum(cotangent.astype(F32), axis=0)
        pieces = [
            *(sums_own + sums_other)[:4],
            qkv_bias_part,
            bias_part,
            up_bias_part,
        ]
        return jnp.concatenate(pieces).reshape(-1, 128)

    sizes = [depth] * 4 + [qkv_bias.size, depth, up_bias.size]

    attn_cols, mlp_cols = 4 * head_cols, 2 * unit_cols
    ring = links.ring
    own_segments = lax.dynamic_slice_in_dim(segments, links.lane * rows // length, rows // length, 0)
    pair_segments = jnp.concatenate([own_segments, links.swap(own_segments)], axis=0)
    attn_slots, pair_segments = sync((attn_slots, pair_segments))
    for s in range(1, half):
        attn_slots.append(ring(attn_slots[-1]))
    if by_hops:
        got = [links.near_places(attn_slots[0])]
        tables = tables_of(pair_segments)
        attn_slots, tables, x_other, dy_other = sync((attn_slots, tables, x_other, dy_other))
        got.append(links.near_places(attn_slots[1]))
        last = [links.hop(got[0][1], 1)]
        mlp_slots.append(ring(mlp_slots[0]))
        normed = prepare(tokens, x_other, cotangent, dy_other, gains)
        got, last, normed = sync((got, last, normed))
        last.append(links.hop(got[1][0], 2))
        group_a = [[(attn_slots[j], 0, 0), (got[j][0], 1, 0), (got[j][1], 2, 0), (last[j], 3, 0)] for j in (0, 1)]
    else:
        tables = tables_of(pair_segments)
        normed = prepare(tokens, x_other, cotangent, dy_other, gains)
        for s in range(1, half):
            mlp_slots.append(ring(mlp_slots[-1]))
        group_a = pieces_of(None, near(group_piece(attn_slots)), None, attn_cols)
    arrays = [[v[0] for v in slot] for slot in group_a]
    arrays, mlp_slots, attn_slots, normed = sync((arrays, mlp_slots, attn_slots, normed))
    group_a = [[(v, *w[1:]) for v, w in zip(vs, slot)] for vs, slot in zip(arrays, group_a)]
    an, mn, dy2 = normed
    piece_b = group_piece(mlp_slots)
    piece_b, an, attn_slots = sync((piece_b, an, attn_slots))

    def ring_on(slots, count):
        for _ in range(count):
            slots.append(ring(slots[-1]))
        return slots

    near_b = near(piece_b)
    mlp_slots = ring_on(mlp_slots, 1)
    attn_slots = ring_on(attn_slots, 1)
    att0, dmix0, qkv_sum0, qkv0, out0 = attention_part(0, group_a, an, dy2)
    near_b, mlp_slots, attn_slots, att0, dmix0 = sync((near_b, mlp_slots, attn_slots, att0, dmix0))
    parts_b = far_parts(near_b)
    parts_b, mlp_slots, attn_slots, att0 = sync((parts_b, mlp_slots, attn_slots, att0))

    far_b = far(parts_b)
    mlp_slots = ring_on(mlp_slots, half - 1)
    attn_slots = ring_on(attn_slots, half - 1)
    grad_a0 = attention_grads(att0, dmix0)
    far_b, mlp_slots, attn_slots, grad_a0 = sync((far_b, mlp_slots, attn_slots, grad_a0))
    piece_c = group_piece(mlp_slots[half:])
    piece_c, mn = sync((piece_c, mn))

    near_c = near(piece_c)
    group_b = pieces_of(piece_b, near_b, far_b, mlp_cols)
    act0, dgate0, gate_sum0, up0, down0 = mlp_front(group_b, place, mn, dy2, up_bias_groups[0])
    near_c, act0 = sync((near_c, act0))
    parts_c = far_parts(near_c)
    parts_c, act0 = sync((parts_c, act0))

    far_c = far(parts_c)
    far_a = sum_far(grad_a0)
    grad_b = mlp_grads(act0, dgate0)
    far_c, far_a, grad_b = sync((far_c, far_a, grad_b))
    piece_d = group_piece(attn_slots[half:])
    sent_a = add_far(grad_a0, far_a)
    piece_d, sent_a, mn = sync((piece_d, sent_a, mn))

    near_d = near(piece_d)
    near_a = sum_near(sent_a)
    group_c = pieces_of(piece_c, near_c, far_c, mlp_cols)
    act1, dgate1, gate_sum1, up1, down1 = mlp_front(group_c, place, mn, dy2, up_bias_groups[1])
    near_d, near_a, act1 = sync((near_d, near_a, act1))
    parts_d = far_parts(near_d)
    parts_d, act1 = sync((parts_d, act1))

    far_d = far(parts_d)
    back_b = sum_far(grad_b)
    grad_c = mlp_grads(act1, dgate1)
    far_d, back_b, grad_c = sync((far_d, back_b, grad_c))
    sent_b = add_far(grad_b, back_b)
    sum_a = place_sum(grad_a0, near_a)
    sent_b, sum_a, an = sync((sent_b, sum_a, an))

    back_near_b = sum_near(sent_b)
    back_c = sum_far(grad_c)
    ring_a = links.ring_sum(None, sum_a[1:])
    group_d = pieces_of(piece_d, near_d, far_d, attn_cols)
    att1, dmix1, qkv_sum1, qkv1, out1 = attention_part(1, group_d, an, dy2)
    back_near_b, back_c, ring_a, att1 = sync((back_near_b, back_c, ring_a, att1))
    sent_c = add_far(grad_c, back_c)
    sum_b = place_sum(grad_b, back_near_b)
    sent_c, sum_b, att1 = sync((sent_c, sum_b, att1))

    back_near_c = sum_near(sent_c)
    ring_m = links.ring_sum(None, sum_b[1:])
    grad_d = attention_grads(att1, dmix1)
    ring_m, grad_d, dgate1 = sync((ring_m, grad_d, dgate1))

    back_d = sum_far(grad_d)
    terms = ((dgate0, up0), (dgate1, up1), (dmix0, qkv0), (dmix1, qkv1))
    sent_pull, sums_other = pull_back(terms, x_other, gains, rows, BF16)
    back_near_c, back_d, sent_pull = sync((back_near_c, back_d, sent_pull))
    sum_c = place_sum(grad_c, back_near_c)
    sent_d = add_far(grad_d, back_d)
    term_m = ring_m + sum_c[0]
    sum_c, sent_d, term_m, dgate1 = sync((sum_c, sent_d, term_m, dgate1))

    near_e = sum_near(sent_d)
    ring_m = links.ring_sum(None, [term_m] + sum_c[1:-1])
    other_pull = links.swap(sent_pull)
    terms = ((dgate0, up0), (dgate1, up1), (dmix0, qkv0), (dmix1, qkv1))
    pulled, sums_own = pull_back(terms, tokens, gains, 0, F32)
    near_e, ring_m, other_pull, pulled = sync((near_e, ring_m, other_pull, pulled))
    sum_d = place_sum(grad_d, near_e)
    term_m = ring_m + sum_c[-1]
    term_a = ring_a + sum_d[0]
    small = small_sums()
    sum_d, term_m, term_a, small, att1 = sync((sum_d, term_m, term_a, small, att1))

    steps = links.sum_steps()
    ring_m = links.ring_sum(None, [term_m])
    ring_a = links.ring_sum(None, [term_a] + sum_d[1:-1])
    small = links.sum_step(small, steps[0])
    out_terms = ((att0, out0), (att1, out1), (act0, down0), (act1, down1))
    (sent_out,) = branch_out(out_terms, rows)
    ring_m, ring_a, small, sent_out = sync((ring_m, ring_a, small, sent_out))
    term_a = ring_a + sum_d[-1]
    sum_m = ring_m + sum_b[0]
    term_a, sum_m, small, sent_out = sync((term_a, sum_m, small, sent_out))

    other_out = links.swap(sent_out)
    ring_a = links.ring_sum(None, [term_a])
    mlp_own = unpair_rows(links, sum_m)
    small = links.sum_step(small, steps[1])
    other_out, small, att1, mlp_own, ring_a = sync((other_out, small, att1, mlp_own, ring_a))

    sum_e = ring_a + sum_a[0]
    sum_e, small, att1 = sync((sum_e, small, att1))
    attn_own = unpair_rows(links, sum_e)
    small = links.sum_step(small, steps[2])
    end_bias = (out_bias.astype(F32) + down_bias.astype(F32))[None]
    out_terms = ((att0, out0), (att1, out1), (act0, down0), (act1, down1))
    output, input_grad = branch_out(
        out_terms, rows, [tokens, other_out, end_bias, cotangent, pulled, other_pull]
    )
    small, attn_own, output, input_grad = sync((small, attn_own, output, input_grad))
    for step in steps[3:]:
        small = links.sum_step(small, step)
    up_grad = jnp.concatenate([v[:, :unit_cols] for v in mlp_own], axis=1)
    down_grad = jnp.concatenate([v[:, unit_cols:] for v in mlp_own], axis=1).T
    qkv_grad = jnp.concatenate([v[:, :qkv_cols].reshape(-1, 3, head_cols) for v in attn_own], axis=2)
    out_grad = jnp.concatenate([v[:, qkv_cols:] for v in attn_own], axis=1).T

    summed = small.reshape(-1)
    sums = []
    at = 0
    for size in sizes:
        sums.append(summed[at : at + size])
        at += size
    return (
        output,
        input_grad,
        sums[0],
        sums[1],
        sums[2],
        sums[3],
        qkv_grad,
        sums[4].reshape(qkv_bias.shape),
        out_grad,
        sums[5],
        up_grad,
        sums[6],
        down_grad,
        sums[5],
    )


def solution(mesh):
    placed = (
        P(("fsdp", "tp"), None),
        P("fsdp", None),
        P(),
        P(),
        P(),
        P(),
        P("fsdp", None, "tp"),
        P(),
        P("tp", "fsdp"),
        P(),
        P("fsdp", "tp"),
        P(),
        P("tp", "fsdp"),
        P(),
        P(("fsdp", "tp"), None),
    )
    return jax.shard_map(
        body,
        mesh=mesh,
        in_specs=placed,
        out_specs=(
            P(("fsdp", "tp"), None),
            P(("fsdp", "tp"), None),
            P(),
            P(),
            P(),
            P(),
            P("fsdp", None, "tp"),
            P(),
            P("tp", "fsdp"),
            P(),
            P("fsdp", "tp"),
            P(),
            P("tp", "fsdp"),
            P(),
        ),
        check_vma=False,
    )
```

time: 430 us -> 376 us (0.87)
  waiting for transfers between devices: 66.2 us -> 35.3 us
  Pallas kernels: 247 us -> 223 us
  local copies, waits for them, and re-layouts: 13.1 us -> 25.3 us
  starting transfers between devices: 68 us -> 56.5 us
    ppermute x48 -> x34, starting transfers between devices: 51.1 us -> 35.3 us  [hop(): lax.ppermute(value, 'fsdp', [(i, i ^ 2 * bit) for i in range(self.fsdp)])]
    pallas_call x4, Pallas kernels: 127 us -> 112 us  [the longest x2 74 us: attention(): pl.pallas_call(partial(attention_kernel, keys=[[v[1:] for v in pair] for...]
    ppermute x12, waiting for transfers between devices: 30.6 us -> 16.2 us  [ring(): lax.ppermute(value, 'tp', [(i, (i + 1) % self.tp) for i in range(self.tp)])]
    ppermute x5, waiting for transfers between devices: 21.6 us -> 9.44 us  [sum_step(): lax.ppermute(value, name, [(i, i ^ bit) for i in range(size)])]
    dynamic_update_slice x0 -> x8, other arithmetic: none -> 8.99 us  [the longest x4 6.57 us: add_far(): lax.dynamic_update_slice(two, second, (0, cut))]
    convert_element_type x14 -> x6, other arithmetic: 6.96 us -> 0.47 us  [ring_sum(): total = self.ring(total.astype(BF16)).astype(F32)]
    unnamed x150 -> x126, local copies, waits for them, and re-layouts: 4.93 us -> 11.3 us
    ppermute x12, starting transfers between devices: 10.4 us -> 16.6 us  [ring(): lax.ppermute(value, 'tp', [(i, (i + 1) % self.tp) for i in range(self.tp)])]
  transfers between devices with their start and end apart: 74 -> 60, of which waited for: 14 -> 8; matrix products, arithmetic and copies ran while one was open for 9% -> 9% of each run, Pallas kernels for 53% -> 60%
where the time goes in v3:
time: 376 us; the launch traced here: 370 us
  Pallas kernels  223 us (59%)
  starting transfers between devices  56.5 us (15%)
  waiting for transfers between devices  35.3 us (9%)
  other arithmetic  27.4 us (7%)
  local copies, waits for them, and re-layouts  25.3 us (7%)
    pallas_call x2, Pallas kernels, attention(): pl.pallas_call(partial(attention_kernel, keys=[[v[1:] for v in pair] for...  74 us
    pallas_call x4, Pallas kernels, weight_grads(): pl.pallas_call(partial(grads_kernel, count=count, keys=keys), grid_spec=p...  47.3 us
    pallas_call x2, Pallas kernels, mlp_front(): pl.pallas_call(partial(mlp_kernel, keys=[[v[1:] for v in slot] for slot i...  37.8 us
    ppermute x34, starting transfers between devices, hop(): lax.ppermute(value, 'fsdp', [(i, i ^ 2 * bit) for i in range(self.fsdp)])  35.3 us
    pallas_call x2, Pallas kernels, pull_back(): pl.pallas_call(pull_kernel, grid=(rows // br,), in_specs=specs + [tile, w...  29.4 us
    pallas_call x2, Pallas kernels, branch_out(): pl.pallas_call(partial(out_kernel, own=own), grid=(rows // br,), in_specs...  24.4 us
    ppermute x12, starting transfers between devices, ring(): lax.ppermute(value, 'tp', [(i, (i + 1) % self.tp) for i in range(self.tp)])  16.6 us
    ppermute x12, waiting for transfers between devices, ring(): lax.ppermute(value, 'tp', [(i, (i + 1) % self.tp) for i in range(self.tp)])  16.2 us
  transfers between devices with their start and end apart: 60, of which 8 were waited for; matrix products, arithmetic and copies ran while one was open for 9% of the time, Pallas kernels for 60%

profile of v3, /device:TPU:0, one launch (start us, length us, event | category | flops | bytes accessed | tf_op | source)
XLA Modules:
  0.0 369.9 jit_solution(7801055236824856283)
XLA Ops:
  8.8 2.7 collective-permute-start.2
  14.2 5.9 %fusion = (f32[2048,128]{1,0:T(8,128)}, f32[2048,128]{1,0:T(8,128)}, f32[2048,128]{1,0:T(8,128)}) fusion(f32[128]{0:T(128)S(1)} %mul.50, f32[2048]{0:T(1024)S(1)} %bitcast.107, pred[128]{0:T(512)(128)(4,1)S(1)} %get-tuple-element.526, pred[128]{0:T(512)(128)(4,1)S(1)} %get-tuple-element.527, pred[128]{0:T(512)(128)(4,1)S(1)} %broadcast_compare_fusion.1), kind=kLoop, calls=%fused_computation.6 | loop fusion | flops 1310720 | bytes 3154816 | tf_op jit(solution)/shard_map/jit(_where)/select_n | solution.py:557
  27.3 9.9 %prepare.1 = (bf16[2048,1024]{1,0:T(8,128)(2,1)}, bf16[2048,1024]{1,0:T(8,128)(2,1)}, bf16[2048,1024]{1,0:T(8,128)(2,1)}) custom-call(bf16[1024,1024]{1,0:T(8,128)(2,1)} %refs_8_.3, bf16[1024,1024]{1,0:T(8,128)(2,1)} %copy-done.7, bf16[1024,1024]{1,0:T(8,128)(2,1)} %refs_11_.1, bf16[1024,1024]{1,0:T(8,128)(2,1)} %collective-permute-done.4.dy_other, ...), custom_call_target="tpu_custom_call" | custom-call | flops 41943040 | bytes 33554432 | tf_op jit(solution)/shard_map/prepare/pallas_call | solution.py:63
  37.2 3.5 collective-permute-done.7.refs_5_
  42.9 6.0 %collective-permute-done.10.refs_7_ = bf16[256,512]{1,0:T(8,128)(2,1)S(1)} collective-permute-done((bf16[256,512]{1,0:T(8,128)(2,1)}, bf16[256,512]{1,0:T(8,128)(2,1)S(1)}, u32[]{:S(2)}, u32[]{:S(2)}) %collective-permute-start.10) | collective-permute-done | bytes 262176 | tf_op jit(solution)/shard_map/ppermute | solution.py:473
  54.4 36.7 %attention.2 = (bf16[2048,256]{1,0:T(8,128)(2,1)}, bf16[2048,768]{1,0:T(8,128)(2,1)}, f32[2,1,384]{2,1,0:T(1,128)}, bf16[1024,768]{1,0:T(8,128)(2,1)}, bf16[1024,256]{1,0:T(8,128)(2,1)}) custom-call(s32[1]{0:T(128)} %bitcast.6.place_ref, bf16[2048,1024]{1,0:T(8,128)(2,1)} %get-tuple-element.342.an_ref.left_a, ...), custom_call_target="tpu_custom_call" | custom-call | flops 21474836480 | bytes 37748736 | tf_op jit(solution)/shard_map/attention/pallas_call | solution.py:196
  95.8 9.3 %weight_grads.4 = (bf16[256,512]{1,0:T(8,128)(2,1)}, bf16[256,512]{1,0:T(8,128)(2,1)}, bf16[256,1024]{1,0:T(8,128)(2,1)}, bf16[256,1024]{1,0:T(8,128)(2,1)}, bf16[256,1024]{1,0:T(8,128)(2,1)}) custom-call(s32[1]{0:T(128)} %bitcast.6.place_ref, bf16[2048,1024]{1,0:T(8,128)(2,1)} %get-tuple-element.342.an_ref.left_a, ...), custom_call_target="tpu_custom_call" | custom-call | flops 4294967296 | bytes 14680064 | tf_op jit(solution)/shard_map/weight_grads/pallas_call | solution.py:335
  105.1 6.5 %collective-permute-done.20 = bf16[256,512]{1,0:T(8,128)(2,1)S(1)} collective-permute-done((bf16[256,512]{1,0:T(8,128)(2,1)S(1)}, bf16[256,512]{1,0:T(8,128)(2,1)S(1)}, u32[]{:S(2)}, u32[]{:S(2)}) %collective-permute-start.20) | collective-permute-done | bytes 262176 | tf_op jit(solution)/shard_map/ppermute | solution.py:476
  115.8 18.9 %mlp_front.2 = (bf16[2048,1024]{1,0:T(8,128)(2,1)}, bf16[2048,1024]{1,0:T(8,128)(2,1)}, f32[1,1024]{1,0:T(1,128)}, bf16[1024,1024]{1,0:T(8,128)(2,1)}, bf16[1024,1024]{1,0:T(8,128)(2,1)}) custom-call(s32[1]{0:T(128)} %bitcast.6.place_ref, bf16[2048,1024]{1,0:T(8,128)(2,1)} %get-tuple-element.311.mn_ref.left_a, ...), custom_call_target="tpu_custom_call" | custom-call | flops 8589934592 | bytes 25165824 | tf_op jit(solution)/shard_map/mlp_front/pallas_call | solution.py:279
  140.2 14.3 %weight_grads.5 = (bf16[256,1024]{1,0:T(8,128)(2,1)}, bf16[256,1024]{1,0:T(8,128)(2,1)}, bf16[256,2048]{1,0:T(8,128)(2,1)}, bf16[256,2048]{1,0:T(8,128)(2,1)}, bf16[256,2048]{1,0:T(8,128)(2,1)}) custom-call(s32[1]{0:T(128)} %bitcast.6.place_ref, bf16[2048,1024]{1,0:T(8,128)(2,1)} %get-tuple-element.311.mn_ref.left_a, ...), custom_call_target="tpu_custom_call" | custom-call | flops 8589934592 | bytes 20971520 | tf_op jit(solution)/shard_map/weight_grads/pallas_call | solution.py:335
  160.8 18.9 %mlp_front.3 = (bf16[2048,1024]{1,0:T(8,128)(2,1)}, bf16[2048,1024]{1,0:T(8,128)(2,1)}, f32[1,1024]{1,0:T(1,128)}, bf16[1024,1024]{1,0:T(8,128)(2,1)}, bf16[1024,1024]{1,0:T(8,128)(2,1)}) custom-call(s32[1]{0:T(128)} %bitcast.6.place_ref, bf16[2048,1024]{1,0:T(8,128)(2,1)} %get-tuple-element.311.mn_ref.left_a, ...), custom_call_target="tpu_custom_call" | custom-call | flops 8589934592 | bytes 25165824 | tf_op jit(solution)/shard_map/mlp_front/pallas_call | solution.py:279
  187.1 14.3 %weight_grads.6 = (bf16[256,1024]{1,0:T(8,128)(2,1)}, bf16[256,1024]{1,0:T(8,128)(2,1)}, bf16[256,2048]{1,0:T(8,128)(2,1)}, bf16[256,2048]{1,0:T(8,128)(2,1)}, bf16[256,2048]{1,0:T(8,128)(2,1)}) custom-call(s32[1]{0:T(128)} %bitcast.6.place_ref, bf16[2048,1024]{1,0:T(8,128)(2,1)} %get-tuple-element.311.mn_ref.left_a, ...), custom_call_target="tpu_custom_call" | custom-call | flops 8589934592 | bytes 20971520 | tf_op jit(solution)/shard_map/weight_grads/pallas_call | solution.py:335
  201.8 2.7 fusion.6
  209.1 37.3 %attention.3 = (bf16[2048,256]{1,0:T(8,128)(2,1)}, bf16[2048,768]{1,0:T(8,128)(2,1)}, f32[2,1,384]{2,1,0:T(1,128)}, bf16[1024,768]{1,0:T(8,128)(2,1)}, bf16[1024,256]{1,0:T(8,128)(2,1)}) custom-call(s32[1]{0:T(128)} %bitcast.6.place_ref, bf16[2048,1024]{1,0:T(8,128)(2,1)} %get-tuple-element.342.an_ref.left_a, ...), custom_call_target="tpu_custom_call" | custom-call | flops 21474836480 | bytes 37748736 | tf_op jit(solution)/shard_map/attention/pallas_call | solution.py:196
  253.1 9.4 %weight_grads.7 = (bf16[256,512]{1,0:T(8,128)(2,1)}, bf16[256,512]{1,0:T(8,128)(2,1)}, bf16[256,1024]{1,0:T(8,128)(2,1)}, bf16[256,1024]{1,0:T(8,128)(2,1)}, bf16[256,1024]{1,0:T(8,128)(2,1)}) custom-call(s32[1]{0:T(128)} %bitcast.6.place_ref, bf16[2048,1024]{1,0:T(8,128)(2,1)} %get-tuple-element.342.an_ref.left_a, ...), custom_call_target="tpu_custom_call" | custom-call | flops 4294967296 | bytes 14680064 | tf_op jit(solution)/shard_map/weight_grads/pallas_call | solution.py:335
  264.6 14.6 %pull_back.2 = (bf16[1024,1024]{1,0:T(8,128)(2,1)}, f32[8,1024]{1,0:T(8,128)}) custom-call(bf16[2048,1024]{1,0:T(8,128)(2,1)} %get-tuple-element.298.right_a.refs_0_, bf16[1024,1024]{1,0:T(8,128)(2,1)} %get-tuple-element.367.refs_1_, bf16[2048,1024]{1,0:T(8,128)(2,1)} %get-tuple-element.384.right_a.refs_2_, bf16[1024,1024]{1,0:T(8,128)(2,1)} %get-tuple-element.369.refs_3_, ...), custom_call_target="tpu_custom_call" | custom-call | flops 7516192768 | bytes 23068672 | tf_op jit(solution)/shard_map/pull_back/pallas_call | solution.py:394
  289.1 14.8 %pull_back.3 = (f32[1024,1024]{1,0:T(8,128)}, f32[8,1024]{1,0:T(8,128)}) custom-call(bf16[2048,1024]{1,0:T(8,128)(2,1)} %get-tuple-element.298.right_a.refs_0_, bf16[1024,1024]{1,0:T(8,128)(2,1)} %get-tuple-element.367.refs_1_, bf16[2048,1024]{1,0:T(8,128)(2,1)} %get-tuple-element.384.right_a.refs_2_, bf16[1024,1024]{1,0:T(8,128)(2,1)} %get-tuple-element.369.refs_3_, ...), custom_call_target="tpu_custom_call" | custom-call | flops 7516192768 | bytes 23068672 | tf_op jit(solution)/shard_map/pull_back/pallas_call | solution.py:394
  307.2 3.4 collective-permute-start.49
  311.7 10.2 %branch_out.2 = bf16[1024,1024]{1,0:T(8,128)(2,1)} custom-call(bf16[2048,256]{1,0:T(8,128)(2,1)} %get-tuple-element.274.right_b.refs_0_, bf16[1024,256]{1,0:T(8,128)(2,1)} %get-tuple-element.400.refs_1_, bf16[2048,256]{1,0:T(8,128)(2,1)} %get-tuple-element.421.right_b.refs_2_, bf16[1024,256]{1,0:T(8,128)(2,1)} %get-tuple-element.402.refs_3_, ...), custom_call_target="tpu_custom_call" | custom-call | flops 5368709120 | bytes 12582912 | tf_op jit(solution)/shard_map/branch_out/pallas_call | solution.py:441
  321.9 5.2 %collective-permute-done.50 = bf16[256,512]{1,0:T(8,128)(2,1)S(1)} collective-permute-done((bf16[256,512]{1,0:T(8,128)(2,1)S(1)}, bf16[256,512]{1,0:T(8,128)(2,1)S(1)}, u32[]{:S(2)}, u32[]{:S(2)}) %collective-permute-start.50) | collective-permute-done | bytes 262176 | tf_op jit(solution)/shard_map/ppermute | solution.py:476
  335.4 4.5 %collective-permute-done.55 = bf16[256,512]{1,0:T(8,128)(2,1)S(1)} collective-permute-done((bf16[256,512]{1,0:T(8,128)(2,1)S(1)}, bf16[256,512]{1,0:T(8,128)(2,1)S(1)}, u32[]{:S(2)}, u32[]{:S(2)}) %collective-permute-start.55) | collective-permute-done | bytes 262176 | tf_op jit(solution)/shard_map/ppermute | solution.py:476
  341.4 14.2 %branch_out.3 = (bf16[1024,1024]{1,0:T(8,128)(2,1)}, f32[1024,1024]{1,0:T(8,128)}) custom-call(bf16[2048,256]{1,0:T(8,128)(2,1)} %get-tuple-element.274.right_b.refs_0_, bf16[1024,256]{1,0:T(8,128)(2,1)} %get-tuple-element.400.refs_1_, bf16[2048,256]{1,0:T(8,128)(2,1)} %get-tuple-element.421.right_b.refs_2_, bf16[1024,256]{1,0:T(8,128)(2,1)} %get-tuple-element.402.refs_3_, ...), custom_call_target="tpu_custom_call" | custom-call | flops 5368709120 | bytes 29360128 | tf_op jit(solution)/shard_map/branch_out/pallas_call | solution.py:441
  358.1 4.0 %collective-permute-done.58 = f32[96,128]{1,0:T(8,128)S(1)} collective-permute-done((f32[96,128]{1,0:T(8,128)S(1)}, f32[96,128]{1,0:T(8,128)S(1)}, u32[]{:S(2)}, u32[]{:S(2)}) %collective-permute-start.58) | collective-permute-done | bytes 49184 | tf_op jit(solution)/shard_map/ppermute | solution.py:521
  364.0 3.2 collective-permute-done.59
  (358 shorter events, 97.0 us)
Async XLA Ops:
  3.7 19.9 %collective-permute-start.3 = (bf16[1024,1024]{1,0:T(8,128)(2,1)}, bf16[1024,1024]{1,0:T(8,128)(2,1)S(1)}, u32[]{:S(2)}, u32[]{:S(2)}) collective-permute-start(bf16[1024,1024]{1,0:T(8,128)(2,1)} %refs_8_.3), channel_id=1, source_target_pairs={{0,4},{4,0},{8,12},{12,8},{16,20},{20,16},{24,28},{28,24},{1,5},{5... | collective-permute-start | bytes 6291464 | tf_op jit(solution)/shard_map/ppermute | solution.py:470
  49.0 42.1 %collective-permute-start.13 = (bf16[256,2048]{1,0:T(8,128)(2,1)S(1)}, bf16[256,2048]{1,0:T(8,128)(2,1)S(1)}, u32[]{:S(2)}, u32[]{:S(2)}) collective-permute-start(bf16[256,2048]{1,0:T(8,128)(2,1)S(1)} %pad_maximum_fusion.refs_0_.refs_4_), channel_id=1, source_target_pairs={{0,8},{4,12},{8,0},{12,4},{16,24},{20,28},{24,16},{28,20},{1,9},{5... | collective-permute-start | bytes 3145736 | tf_op jit(solution)/shard_map/ppermute | solution.py:473
  50.6 40.6 %collective-permute-start.14 = (bf16[256,2048]{1,0:T(8,128)(2,1)S(1)}, bf16[256,2048]{1,0:T(8,128)(2,1)S(1)}, u32[]{:S(2)}, u32[]{:S(2)}) collective-permute-start(bf16[256,2048]{1,0:T(8,128)(2,1)S(1)} %pad_maximum_fusion.refs_0_.refs_4_), channel_id=1, source_target_pairs={{0,16},{4,20},{8,24},{12,28},{16,0},{20,4},{24,8},{28,12},{1,17},{... | collective-permute-start | bytes 3145736 | tf_op jit(solution)/shard_map/ppermute | solution.py:473
  51.1 40.0 %collective-permute-start.15 = (bf16[256,1024]{1,0:T(8,128)(2,1)S(1)}, bf16[256,1024]{1,0:T(8,128)(2,1)S(1)}, u32[]{:S(2)}, u32[]{:S(2)}) collective-permute-start(bf16[256,1024]{1,0:T(8,128)(2,1)S(1)} %collective-permute-done.12), channel_id=1, source_target_pairs={{0,1},{1,2},{2,3},{3,0},{4,5},{5,6},{6,7},{7,4},{8,9},{9,10},{10,1... | collective-permute-start | bytes 1572872 | tf_op jit(solution)/shard_map/ppermute | solution.py:476
  52.7 38.4 %collective-permute-start.16 = (bf16[256,512]{1,0:T(8,128)(2,1)S(1)}, bf16[256,512]{1,0:T(8,128)(2,1)S(1)}, u32[]{:S(2)}, u32[]{:S(2)}) collective-permute-start(bf16[256,512]{1,0:T(8,128)(2,1)S(1)} %copy-done.45), channel_id=1, source_target_pairs={{0,1},{1,2},{2,3},{3,0},{4,5},{5,6},{6,7},{7,4},{8,9},{9,10},{10,1... | collective-permute-start | bytes 786440 | tf_op jit(solution)/shard_map/ppermute | solution.py:476
  91.2 20.3 %collective-permute-start.17 = (bf16[256,1024]{1,0:T(8,128)(2,1)S(1)}, bf16[256,1024]{1,0:T(8,128)(2,1)}, u32[]{:S(2)}, u32[]{:S(2)}) collective-permute-start(bf16[256,1024]{1,0:T(8,128)(2,1)S(1)} %slice.123), channel_id=1, source_target_pairs={{0,8},{4,12},{8,0},{12,4},{16,24},{20,28},{24,16},{28,20},{1,9},{5... | collective-permute-start | bytes 1572872 | tf_op jit(solution)/shard_map/ppermute | solution.py:473
  111.7 24.1 %collective-permute-start.21 = (bf16[256,2048]{1,0:T(8,128)(2,1)S(1)}, bf16[256,2048]{1,0:T(8,128)(2,1)}, u32[]{:S(2)}, u32[]{:S(2)}) collective-permute-start(bf16[256,2048]{1,0:T(8,128)(2,1)S(1)} %pad_maximum_fusion.1.refs_0_.refs_4_), channel_id=1, source_target_pairs={{0,8},{4,12},{8,0},{12,4},{16,24},{20,28},{24,16},{28,20},{1,9},{5... | collective-permute-start | bytes 3145736 | tf_op jit(solution)/shard_map/ppermute | solution.py:473
  112.7 23.2 %collective-permute-start.22 = (bf16[256,2048]{1,0:T(8,128)(2,1)S(1)}, bf16[256,2048]{1,0:T(8,128)(2,1)}, u32[]{:S(2)}, u32[]{:S(2)}) collective-permute-start(bf16[256,2048]{1,0:T(8,128)(2,1)S(1)} %pad_maximum_fusion.1.refs_0_.refs_4_), channel_id=1, source_target_pairs={{0,16},{4,20},{8,24},{12,28},{16,0},{20,4},{24,8},{28,12},{1,17},{... | collective-permute-start | bytes 3145736 | tf_op jit(solution)/shard_map/ppermute | solution.py:473
  113.2 41.3 %collective-permute-start.25 = (bf16[256,512]{1,0:T(8,128)(2,1)}, bf16[256,512]{1,0:T(8,128)(2,1)S(1)}, u32[]{:S(2)}, u32[]{:S(2)}) collective-permute-start(bf16[256,512]{1,0:T(8,128)(2,1)} %get-tuple-element.296), channel_id=1, source_target_pairs={{0,16},{4,20},{8,24},{12,28},{16,0},{20,4},{24,8},{28,12},{1,17},{... | collective-permute-start | bytes 786440 | tf_op jit(solution)/shard_map/ppermute | solution.py:473
  114.7 39.8 %collective-permute-start.26 = (bf16[256,512]{1,0:T(8,128)(2,1)}, bf16[256,512]{1,0:T(8,128)(2,1)S(1)}, u32[]{:S(2)}, u32[]{:S(2)}) collective-permute-start(bf16[256,512]{1,0:T(8,128)(2,1)} %get-tuple-element.297), channel_id=1, source_target_pairs={{0,8},{4,12},{8,0},{12,4},{16,24},{20,28},{24,16},{28,20},{1,9},{5... | collective-permute-start | bytes 786440 | tf_op jit(solution)/shard_map/ppermute | solution.py:473
  156.6 25.7 %collective-permute-start.27 = (bf16[256,1024]{1,0:T(8,128)(2,1)S(1)}, bf16[256,1024]{1,0:T(8,128)(2,1)}, u32[]{:S(2)}, u32[]{:S(2)}) collective-permute-start(bf16[256,1024]{1,0:T(8,128)(2,1)S(1)} %pad_maximum_fusion.3.refs_0_.refs_4_), channel_id=1, source_target_pairs={{0,8},{4,12},{8,0},{12,4},{16,24},{20,28},{24,16},{28,20},{1,9},{5... | collective-permute-start | bytes 1572872 | tf_op jit(solution)/shard_map/ppermute | solution.py:473
  157.4 25.7 %collective-permute-start.28 = (bf16[256,1024]{1,0:T(8,128)(2,1)S(1)}, bf16[256,1024]{1,0:T(8,128)(2,1)}, u32[]{:S(2)}, u32[]{:S(2)}) collective-permute-start(bf16[256,1024]{1,0:T(8,128)(2,1)S(1)} %pad_maximum_fusion.3.refs_0_.refs_4_), channel_id=1, source_target_pairs={{0,16},{4,20},{8,24},{12,28},{16,0},{20,4},{24,8},{28,12},{1,17},{... | collective-permute-start | bytes 1572872 | tf_op jit(solution)/shard_map/ppermute | solution.py:473
  158.8 24.3 %collective-permute-start.29 = (bf16[256,1024]{1,0:T(8,128)(2,1)S(1)}, bf16[256,1024]{1,0:T(8,128)(2,1)S(1)}, u32[]{:S(2)}, u32[]{:S(2)}) collective-permute-start(bf16[256,1024]{1,0:T(8,128)(2,1)S(1)} %fusion.9), channel_id=1, source_target_pairs={{0,8},{4,12},{8,0},{12,4},{16,24},{20,28},{24,16},{28,20},{1,9},{5... | collective-permute-start | bytes 1572872 | tf_op jit(solution)/shard_map/ppermute | solution.py:473
  160.0 23.1 %collective-permute-start.30 = (bf16[256,1024]{1,0:T(8,128)(2,1)}, bf16[256,1024]{1,0:T(8,128)(2,1)S(1)}, u32[]{:S(2)}, u32[]{:S(2)}) collective-permute-start(bf16[256,1024]{1,0:T(8,128)(2,1)} %fusion.10), channel_id=1, source_target_pairs={{0,16},{4,20},{8,24},{12,28},{16,0},{20,4},{24,8},{28,12},{1,17},{... | collective-permute-start | bytes 1572872 | tf_op jit(solution)/shard_map/ppermute | solution.py:473
  180.9 20.8 %collective-permute-start.33 = (bf16[256,1024]{1,0:T(8,128)(2,1)}, bf16[256,1024]{1,0:T(8,128)(2,1)S(1)}, u32[]{:S(2)}, u32[]{:S(2)}) collective-permute-start(bf16[256,1024]{1,0:T(8,128)(2,1)} %get-tuple-element.320), channel_id=1, source_target_pairs={{0,16},{4,20},{8,24},{12,28},{16,0},{20,4},{24,8},{28,12},{1,17},{... | collective-permute-start | bytes 1572872 | tf_op jit(solution)/shard_map/ppermute | solution.py:473
  204.7 41.7 %collective-permute-start.35 = (bf16[256,2048]{1,0:T(8,128)(2,1)S(1)}, bf16[256,2048]{1,0:T(8,128)(2,1)S(1)}, u32[]{:S(2)}, u32[]{:S(2)}) collective-permute-start(bf16[256,2048]{1,0:T(8,128)(2,1)S(1)} %fusion.5), channel_id=1, source_target_pairs={{0,8},{4,12},{8,0},{12,4},{16,24},{20,28},{24,16},{28,20},{1,9},{5... | collective-permute-start | bytes 3145736 | tf_op jit(solution)/shard_map/ppermute | solution.py:473
  205.5 41.0 %collective-permute-start.36 = (bf16[256,2048]{1,0:T(8,128)(2,1)}, bf16[256,2048]{1,0:T(8,128)(2,1)S(1)}, u32[]{:S(2)}, u32[]{:S(2)}) collective-permute-start(bf16[256,2048]{1,0:T(8,128)(2,1)} %fusion.6), channel_id=1, source_target_pairs={{0,16},{4,20},{8,24},{12,28},{16,0},{20,4},{24,8},{28,12},{1,17},{... | collective-permute-start | bytes 3145736 | tf_op jit(solution)/shard_map/ppermute | solution.py:473
  206.9 39.5 %collective-permute-start.39 = (bf16[256,512]{1,0:T(8,128)(2,1)S(1)}, bf16[256,512]{1,0:T(8,128)(2,1)S(1)}, u32[]{:S(2)}, u32[]{:S(2)}) collective-permute-start(bf16[256,512]{1,0:T(8,128)(2,1)S(1)} %split.49), channel_id=1, source_target_pairs={{0,1},{1,2},{2,3},{3,0},{4,5},{5,6},{6,7},{7,4},{8,9},{9,10},{10,1... | collective-permute-start | bytes 786440 | tf_op jit(solution)/shard_map/ppermute | solution.py:476
  207.1 39.4 %collective-permute-start.37 = (bf16[256,1024]{1,0:T(8,128)(2,1)}, bf16[256,1024]{1,0:T(8,128)(2,1)S(1)}, u32[]{:S(2)}, u32[]{:S(2)}) collective-permute-start(bf16[256,1024]{1,0:T(8,128)(2,1)} %get-tuple-element.339), channel_id=1, source_target_pairs={{0,16},{4,20},{8,24},{12,28},{16,0},{20,4},{24,8},{28,12},{1,17},{... | collective-permute-start | bytes 1572872 | tf_op jit(solution)/shard_map/ppermute | solution.py:473
  207.7 38.7 %collective-permute-start.38 = (bf16[256,1024]{1,0:T(8,128)(2,1)}, bf16[256,1024]{1,0:T(8,128)(2,1)S(1)}, u32[]{:S(2)}, u32[]{:S(2)}) collective-permute-start(bf16[256,1024]{1,0:T(8,128)(2,1)} %get-tuple-element.340), channel_id=1, source_target_pairs={{0,8},{4,12},{8,0},{12,4},{16,24},{20,28},{24,16},{28,20},{1,9},{5... | collective-permute-start | bytes 1572872 | tf_op jit(solution)/shard_map/ppermute | solution.py:473
  250.9 28.3 %collective-permute-start.41 = (bf16[256,2048]{1,0:T(8,128)(2,1)}, bf16[256,2048]{1,0:T(8,128)(2,1)S(1)}, u32[]{:S(2)}, u32[]{:S(2)}) collective-permute-start(bf16[256,2048]{1,0:T(8,128)(2,1)} %copy-done.21), channel_id=1, source_target_pairs={{0,8},{4,12},{8,0},{12,4},{16,24},{20,28},{24,16},{28,20},{1,9},{5... | collective-permute-start | bytes 3145736 | tf_op jit(solution)/shard_map/ppermute | solution.py:473
  251.7 27.5 %collective-permute-start.42 = (bf16[256,2048]{1,0:T(8,128)(2,1)}, bf16[256,2048]{1,0:T(8,128)(2,1)S(1)}, u32[]{:S(2)}, u32[]{:S(2)}) collective-permute-start(bf16[256,2048]{1,0:T(8,128)(2,1)} %copy-done.23), channel_id=1, source_target_pairs={{0,16},{4,20},{8,24},{12,28},{16,0},{20,4},{24,8},{28,12},{1,17},{... | collective-permute-start | bytes 3145736 | tf_op jit(solution)/shard_map/ppermute | solution.py:473
  279.2 25.8 %collective-permute-start.48 = (bf16[1024,1024]{1,0:T(8,128)(2,1)}, bf16[1024,1024]{1,0:T(8,128)(2,1)S(1)}, u32[]{:S(2)}, u32[]{:S(2)}) collective-permute-start(bf16[1024,1024]{1,0:T(8,128)(2,1)} %get-tuple-element.383), channel_id=1, source_target_pairs={{0,4},{4,0},{8,12},{12,8},{16,20},{20,16},{24,28},{28,24},{1,5},{5... | collective-permute-start | bytes 6291464 | tf_op jit(solution)/shard_map/ppermute | solution.py:470
  307.2 19.9 %collective-permute-start.49 = (bf16[256,1024]{1,0:T(8,128)(2,1)S(1)}, bf16[256,1024]{1,0:T(8,128)(2,1)S(1)}, u32[]{:S(2)}, u32[]{:S(2)}) collective-permute-start(bf16[256,1024]{1,0:T(8,128)(2,1)S(1)} %add.253), channel_id=1, source_target_pairs={{0,1},{1,2},{2,3},{3,0},{4,5},{5,6},{6,7},{7,4},{8,9},{9,10},{10,1... | collective-permute-start | bytes 1572872 | tf_op jit(solution)/shard_map/ppermute | solution.py:476
  (93 other events, 916.3 us)

commit v4 on v3

--- a/solution.py
+++ b/solution.py
@@ -74,23 +74,21 @@
     )(x_own, x_other, dy_own, dy_other, gains)
 
 
-def attention_kernel(place_ref, an_ref, dy_ref, bias_ref, cos_ref, sa_ref, sb_ref, qf_ref, kf_ref, *refs, keys, bq):
+def attention_kernel(place_ref, an_ref, dy_ref, bias_ref, turn_ref, mark_ref, *refs, keys, bq):
     length = an_ref.shape[0]
     width = 2 * HD
-    count = len(keys)
-    piece_refs, refs = refs[: sum(map(len, keys))], refs[sum(map(len, keys)) :]
+    piece_refs, refs = refs[: len(keys)], refs[len(keys) :]
     att_ref, dmix_ref, sum_ref, qkv_ref, out_ref, mixed_scr, do_scr, dk_scr, dv_scr = refs
+    count = mixed_scr.shape[0]
     seq, pair = pl.program_id(0), pl.program_id(1)
 
     @pl.when((seq == 0) & (pair == 0))
     def _():
-        at = 0
-        for j, pair_keys in enumerate(keys):
-            for ref, (key, lead) in zip(piece_refs[at : at + len(pair_keys)], pair_keys):
-                into = place_rows(ref, key, place_ref, qkv_ref)
+        for ref, (key, parts) in zip(piece_refs, keys):
+            into = place_rows(ref, key, place_ref, qkv_ref)
+            for j, lead in parts:
                 qkv_ref[into, j * 3 * width : (j + 1) * 3 * width] = ref[:, lead : lead + 3 * width]
                 out_ref[into, j * width : (j + 1) * width] = ref[:, lead + 3 * width : lead + 4 * width]
-            at += len(pair_keys)
 
     @pl.when(pair == 0)
     def _():
@@ -103,9 +101,14 @@
                 do_scr[j, r : r + step, :] = do[:, j * width : (j + 1) * width]
 
     mixed = mixed_scr.at[pair]
-    cos, sa, sb = cos_ref[...], sa_ref[...], sb_ref[...]
     scale = 1.0 / math.sqrt(HD)
     half = ROT // 2
+    lane = lax.broadcasted_iota(jnp.int32, (length, width), 1)
+    dim = lane % HD
+    table = turn_ref[...]
+    cos = jnp.where(dim < half, table, jnp.where(dim < ROT, pltpu.roll(table, half, 1), 1.0))
+    sa = jnp.where(dim < half, -pltpu.roll(table, width - half, 1), 0.0)
+    sb = jnp.where((dim >= half) & (dim < ROT), table, 0.0)
 
     def turn(v, c, a, b, sign):
         side = pltpu.roll(v, width - half, 1) * a + pltpu.roll(v, half, 1) * b
@@ -115,11 +118,10 @@
     k = turn(mixed[:, width : 2 * width], cos, sa, sb, 1).astype(BF16)
     v = mixed[:, 2 * width : 3 * width].astype(BF16)
     do = do_scr[pair]
-    lane = lax.broadcasted_iota(jnp.int32, (length, width), 1)
     zero = jnp.zeros((), BF16)
     qs = (q.astype(F32) * scale).astype(BF16)
-    qf = qf_ref[...]
-    kaug = jnp.concatenate([k, kf_ref[...]], axis=1)
+    qf = jnp.where((mark_ref[...].astype(F32) > 0.5) | (lane >= 8), 0.0, -MASKED).astype(BF16)
+    kaug = jnp.concatenate([k, mark_ref[...]], axis=1)
     heads = []
     for h in range(2):
         m = (lane // HD) == h
@@ -138,25 +140,22 @@
     for i in range(blocks):
         r0 = i * bq
         w = r0 + bq
-        att = dq = dkp = dvp = None
+        att = dq = dkp = dvp = 0.0
+        staged = []
         for qaug, qm, km, vm, dom in heads:
             s = dot32(qaug[r0:w], kaug[:w], NT)
             diagonal = jnp.where(causal, s[:, r0:], -MASKED)
             s = diagonal if i == 0 else jnp.concatenate([s[:, :r0], diagonal], axis=1)
+            staged.append((s, dot32(dom[r0:w], v[:w], NT)))
+        for (s, dp), (qaug, qm, km, vm, dom) in zip(staged, heads):
             e = jnp.exp(s - jnp.max(s, axis=1, keepdims=True))
             p = e * (1.0 / jnp.sum(e, axis=1, keepdims=True))
             pb = p.astype(BF16)
             o = dot32(pb, vm[:w], NN)
-            dp = dot32(dom[r0:w], v[:w], NT)
-            delta = jnp.sum(p * dp, axis=1, keepdims=True)
+            delta = jnp.sum(o * dom[r0:w].astype(F32), axis=1, keepdims=True)
             ds = (p * (dp - delta)).astype(BF16)
-            x = dot32(ds, km[:w], NN)
-            a = dot32(pb, dom[r0:w], TN)
-            b = dot32(ds, qm[r0:w], TN)
-            if att is None:
-                att, dq, dvp, dkp = o, x, a, b
-            else:
-                att, dq, dvp, dkp = att + o, dq + x, dvp + a, dkp + b
+            att, dq = att + o, dq + dot32(ds, km[:w], NN)
+            dvp, dkp = dvp + dot32(pb, dom[r0:w], TN), dkp + dot32(ds, qm[r0:w], TN)
         att_ref[r0:w, :] = att.astype(BF16)
         dmix_ref[r0:w, 0:width] = turn(dq * scale, cos[r0:w], sa[r0:w], sb[r0:w], -1).astype(BF16)
         if i > 0:
@@ -177,14 +176,14 @@
         sum_ref[pair] += part
 
 
-def attention(pairs, place, an, dy, bias, tables, length):
+def attention(pieces, place, an, dy, bias, tables, length):
     rows, depth = an.shape
     width = 2 * HD
     seqs = rows // length
-    count = len(pairs)
+    count = bias.shape[1] // (3 * width)
     row = pl.BlockSpec((length, depth), lambda s, j, p: (s, 0))
     table = pl.BlockSpec((length, width), lambda s, j, p: (s, 0))
-    pieces = [piece for pair in pairs for piece, _, _ in pair]
+    arrays = [v[0] for v in pieces]
     units = seqs * count
     shapes = [
         jax.ShapeDtypeStruct((rows, count * width), BF16),
@@ -194,11 +193,11 @@
         jax.ShapeDtypeStruct((depth, count * width), BF16),
     ]
     return pl.pallas_call(
-        partial(attention_kernel, keys=[[v[1:] for v in pair] for pair in pairs], bq=min(512, length)),
+        partial(attention_kernel, keys=[v[1:] for v in pieces], bq=min(512, length)),
         grid_spec=pltpu.PrefetchScalarGridSpec(
             num_scalar_prefetch=1,
             grid=(seqs, count),
-            in_specs=[row, row, whole_spec(bias)] + [table] * 5 + [whole_spec(v) for v in pieces],
+            in_specs=[row, row, whole_spec(bias), table, table] + [whole_spec(v) for v in arrays],
             out_specs=[
                 pl.BlockSpec((length, width), lambda s, j, p: (s, j)),
                 pl.BlockSpec((length, 3 * width), lambda s, j, p: (s, j)),
@@ -219,80 +218,87 @@
             transcendentals=units * 2 * length * length,
         ),
         name="attention",
-    )(place, an, dy, bias, *tables, *pieces)
-
-
-def mlp_kernel(place_ref, mn_ref, dy_ref, bias_ref, *refs, keys):
-    piece_refs, refs = refs[: sum(map(len, keys))], refs[sum(map(len, keys)) :]
+    )(place, an, dy, bias, *tables, *arrays)
+
+
+def mlp_kernel(place_ref, mn_ref, dy_ref, bias_ref, *refs, keys, count):
+    piece_refs, refs = refs[: len(keys)], refs[len(keys) :]
     act_ref, dgate_ref, sum_ref, up_ref, down_ref = refs
-    units = up_ref.shape[1] // len(keys)
+    units = up_ref.shape[1] // count
     step = pl.program_id(0)
 
     @pl.when(step == 0)
     def _():
-        at = 0
-        for j, slot_keys in enumerate(keys):
-            for ref, (key, lead) in zip(piece_refs[at : at + len(slot_keys)], slot_keys):
-                into = place_rows(ref, key, place_ref, up_ref)
+        sum_ref[...] = jnp.zeros_like(sum_ref)
+        for ref, (key, parts) in zip(piece_refs, keys):
+            into = place_rows(ref, key, place_ref, up_ref)
+            for j, lead in parts:
                 up_ref[into, j * units : (j + 1) * units] = ref[:, lead : lead + units]
                 down_ref[into, j * units : (j + 1) * units] = ref[:, lead + units : lead + 2 * units]
-            at += len(slot_keys)
-
-    part = []
+
     for c in range(0, up_ref.shape[1], units):
         col = slice(c, c + units)
         gate = dot32(mn_ref[...], up_ref[:, col], NN) + bias_ref[:, col]
         dact = dot32(dy_ref[...], down_ref[:, col], NN)
-        e = jnp.exp(gate * gate * -0.5)
-        pdf = e * (1.0 / math.sqrt(2.0 * math.pi))
         cdf = 0.5 + 0.5 * lax.erf(gate * math.sqrt(0.5))
+        pdf = jnp.exp(gate * gate * -0.5) * (1.0 / math.sqrt(2.0 * math.pi))
         act_ref[:, col] = (gate * cdf).astype(BF16)
         dgate = (dact * (cdf + gate * pdf)).astype(BF16)
         dgate_ref[:, col] = dgate
-        part.append(jnp.sum(dgate.astype(F32), axis=0, keepdims=True))
-    part = jnp.concatenate(part, axis=1)
-
-    @pl.when(step == 0)
-    def _():
-        sum_ref[...] = part
-
-    @pl.when(step > 0)
-    def _():
-        sum_ref[...] += part
-
-
-def mlp_front(slots, place, mn, dy, bias):
+        sum_ref[:, col] += jnp.sum(dgate.astype(F32), axis=0, keepdims=True)
+
+
+def mlp(pieces, place, mn, dy, bias, count):
     rows, depth = mn.shape
-    units = bias.shape[1] // len(slots)
-    count = len(slots)
+    units = bias.shape[1]
     br = min(512, rows)
     row = pl.BlockSpec((br, depth), lambda r, p: (r, 0))
-    tile = pl.BlockSpec((br, count * units), lambda r, p: (r, 0))
-    pieces = [piece for slot in slots for piece, _, _ in slot]
+    tile = pl.BlockSpec((br, units), lambda r, p: (r, 0))
+    arrays = [v[0] for v in pieces]
     shapes = [
-        jax.ShapeDtypeStruct((rows, count * units), BF16),
-        jax.ShapeDtypeStruct((rows, count * units), BF16),
-        jax.ShapeDtypeStruct((1, count * units), F32),
-        jax.ShapeDtypeStruct((depth, count * units), BF16),
-        jax.ShapeDtypeStruct((depth, count * units), BF16),
+        jax.ShapeDtypeStruct((rows, units), BF16),
+        jax.ShapeDtypeStruct((rows, units), BF16),
+        jax.ShapeDtypeStruct((1, units), F32),
+        jax.ShapeDtypeStruct((depth, units), BF16),
+        jax.ShapeDtypeStruct((depth, units), BF16),
     ]
     return pl.pallas_call(
-        partial(mlp_kernel, keys=[[v[1:] for v in slot] for slot in slots]),
+        partial(mlp_kernel, keys=[v[1:] for v in pieces], count=count),
         grid_spec=pltpu.PrefetchScalarGridSpec(
             num_scalar_prefetch=1,
             grid=(rows // br,),
-            in_specs=[row, row, whole_spec(bias)] + [whole_spec(v) for v in pieces],
+            in_specs=[row, row, whole_spec(bias)] + [whole_spec(v) for v in arrays],
             out_specs=[tile, tile] + [whole_spec(v) for v in shapes[2:]],
         ),
         out_shape=shapes,
         compiler_params=pltpu.CompilerParams(vmem_limit_bytes=VMEM_BYTES),
         cost_estimate=pl.CostEstimate(
-            flops=4 * rows * depth * count * units,
-            bytes_accessed=rows * depth * 4 + count * (units * depth * 8 + rows * units * 4),
-            transcendentals=2 * rows * count * units,
+            flops=4 * rows * depth * units,
+            bytes_accessed=rows * depth * 4 + units * depth * 8 + rows * units * 4,
+            transcendentals=2 * rows * units,
         ),
-        name="mlp_front",
-    )(place, mn, dy, bias, *pieces)
+        name="mlp",
+    )(place, mn, dy, bias, *arrays)
+
+
+def block_shapes(places, depth, wa, wb, count):
+    if places != 4:
+        return (0,), [jax.ShapeDtypeStruct((depth, wa + wb), BF16)]
+    far = jax.ShapeDtypeStruct((depth // 4, (wa + wb) // count), BF16)
+    near = jax.ShapeDtypeStruct((depth // 4, wa + wb), BF16)
+    return (3, 1, 2, 0), [far] * count + [near] * 3
+
+
+def put_blocks(outs, sum_a, sum_b, place_ref, count, keys):
+    wa, wb = sum_a.shape[1] // count, sum_b.shape[1] // count
+    width = wa + wb
+    for j in range(count):
+        for n, key in enumerate(keys):
+            out = outs[j] if key == 3 else outs[n + count - 1 if len(keys) > 1 else 0]
+            at = place_rows(out, key, place_ref, sum_a)
+            first = 0 if key == 3 else j * width
+            out[:, first : first + wa] = sum_a[at, j * wa : (j + 1) * wa].astype(BF16)
+            out[:, first + wa : first + width] = sum_b[at, j * wb : (j + 1) * wb].astype(BF16)
 
 
 def grads_kernel(place_ref, left_a, left_b, right_a, right_b, *refs, count, keys):
@@ -311,27 +317,15 @@
 
     @pl.when(step == pl.num_programs(0) - 1)
     def _():
-        wa, wb = right_a.shape[1] // count, right_b.shape[1] // count
-        width = wa + wb
-        for j in range(count):
-            for n, key in enumerate(keys):
-                out = outs[j] if key == 3 else outs[n + count - 1 if len(keys) > 1 else 0]
-                at = place_rows(out, key, place_ref, sum_a)
-                first = 0 if key == 3 else j * width
-                out[:, first : first + wa] = sum_a[at, j * wa : (j + 1) * wa].astype(BF16)
-                out[:, first + wa : first + width] = sum_b[at, j * wb : (j + 1) * wb].astype(BF16)
+        put_blocks(outs, sum_a, sum_b, place_ref, count, keys)
 
 
 def weight_grads(place, places, left_a, right_a, left_b, right_b, count):
     rows, depth = left_a.shape
-    keys = (3, 1, 2, 0) if places == 4 else (0,)
-    size = depth // len(keys)
     br = min(512, rows)
     wa, wb = right_a.shape[1], right_b.shape[1]
     block = lambda v: pl.BlockSpec((br, v.shape[1]), lambda i, p: (i, 0))
-    far = jax.ShapeDtypeStruct((size, (wa + wb) // count), BF16)
-    near = jax.ShapeDtypeStruct((size, wa + wb), BF16)
-    shapes = [far] * count + [near] * 3 if places == 4 else [near]
+    keys, shapes = block_shapes(places, depth, wa, wb, count)
     found = pl.pallas_call(
         partial(grads_kernel, count=count, keys=keys),
         grid_spec=pltpu.PrefetchScalarGridSpec(
@@ -506,6 +500,12 @@
             value, "fsdp", scatter_dimension=0, tiled=True, axis_index_groups=self.cores
         )
 
+    def back(self, value):
+        return lax.ppermute(value, "tp", [(i, (i - 1) % self.tp) for i in range(self.tp)])
+
+    def across(self, value):
+        return lax.ppermute(value, "tp", [(i, (i + 2) % self.tp) for i in range(self.tp)])
+
     def ring_sum(self, total, terms):
         for term in terms:
             total = term if total is None else total + term
@@ -543,22 +543,14 @@
 
 
 def tables_of(segment_rows):
-    seqs, length = segment_rows.shape
-    width = 2 * HD
+    length = segment_rows.shape[1]
     starts = jnp.sum((segment_rows[:, None, :] < segment_rows[:, :, None]).astype(jnp.int32), axis=-1)
     places = (jnp.arange(length, dtype=jnp.int32)[None] - starts).reshape(-1).astype(F32)
     inverse_freq = jnp.power(10000.0, -jnp.arange(0, ROT, 2, dtype=F32) / ROT)
-    angles = places[:, None] * jnp.tile(inverse_freq, width // (ROT // 2))[None, :]
-    lane = jnp.arange(width, dtype=jnp.int32)[None, :]
-    turn = lane % HD
-    cos = jnp.where(turn < ROT, jnp.cos(angles), 1.0)
-    sine = jnp.sin(angles)
-    sa = jnp.where(turn < ROT // 2, -sine, 0.0)
-    sb = jnp.where((turn >= ROT // 2) & (turn < ROT), sine, 0.0)
-    same = segment_rows.reshape(-1, 1) == lane
-    key_mark = jnp.where(same, 1.0, 0.0).astype(BF16)
-    query_mark = jnp.where(same | (lane >= 8), 0.0, -MASKED).astype(BF16)
-    return cos, sa, sb, query_mark, key_mark
+    angles = inverse_freq[:, None] * places[None, :]
+    turns = jnp.concatenate([jnp.cos(angles), jnp.sin(angles)], axis=0)
+    marks = segment_rows.reshape(-1, 1) == jnp.arange(2 * HD, dtype=jnp.int32)[None, :]
+    return jnp.tile(turns.T, (1, 2 * HD // ROT)), marks.astype(BF16)
 
 
 def body(
@@ -600,7 +592,7 @@
     half = tp // 2
     per = max(1, 2 * HD // head_cols)
 
-    by_hops = links.places == 4 and per == 1
+    by_hops = links.places == 4 and per == 1 and tp == 4
     place = jnp.full((1,), links.place if by_hops else 0, jnp.int32)
 
     def join_pair(slots):
@@ -623,6 +615,7 @@
         return [blocks[:, :, j].reshape(lead, -1) for j in range(per)]
 
     groups = [list(range(0, half)), list(range(half, tp))]
+    mlp_groups = [[1, 3], [0, 2]] if by_hops else groups
 
     lane_of = [(links.lane - s) % tp for s in range(tp)]
     qkv_bias_lanes = pick(qkv_bias.reshape(3, tp, 2, head_cols), links.core, 2)
@@ -638,7 +631,7 @@
         for g in groups
     ]
     up_bias_groups = [
-        jnp.concatenate([pick(up_bias_lanes, lane_of[s], 0) for s in g]).astype(F32)[None] for g in groups
+        jnp.concatenate([pick(up_bias_lanes, lane_of[s], 0) for s in g]).astype(F32)[None] for g in mlp_groups
     ]
 
     gains = jnp.stack([v.astype(F32) for v in (attn_gain, attn_shift, mlp_gain, mlp_shift)])
@@ -657,18 +650,17 @@
         return links.far_place(parts) if by_hops else ()
 
     def pieces_of(piece, got, last, width):
+        both = tuple((j, j * width) for j in range(half))
         if not by_hops:
-            return [[(got, 0, j * width)] for j in range(half)]
-        return [[(piece, 0, j * width), (got[0], 1, j * width), (got[1], 2, j * width), (last[j], 3, 0)] for j in (0, 1)]
-
-    def pairs_of(slots):
-        if per == 1:
-            return slots
-        columns = [v[0][0][:, v[0][2] : v[0][2] + 4 * head_cols] for v in slots]
-        return [[(join_pair(columns[i : i + per]), 0, 0)] for i in range(0, half, per)]
-
-    def attention_part(g, slots, an, dy):
-        return attention(pairs_of(slots), place, an, dy, qkv_bias_groups[g], tables, length)
+            return [(got, 0, both)]
+        return [(piece, 0, both), (got[0], 1, both), (got[1], 2, both), (last[0], 3, ((0, 0),)), (last[1], 3, ((1, 0),))]
+
+    def attention_part(g, pieces, an, dy):
+        if per > 1:
+            slots = jnp.split(pieces[0][0], half, axis=1)
+            whole = jnp.concatenate([join_pair(slots[i : i + per]) for i in range(0, half, per)], axis=1)
+            pieces = [(whole, 0, tuple((j, j * 8 * HD) for j in range(half // per)))]
+        return attention(pieces, place, an, dy, qkv_bias_groups[g], tables, length)
 
     def attention_grads(attended, dmixed):
         found = weight_grads(place, links.places if by_hops else 1, an, dmixed, dy2, attended, half // per)
@@ -676,6 +668,9 @@
             return found
         pairs = jnp.split(found[0], half // per, axis=1)
         return [jnp.concatenate([v for pair in pairs for v in split_pair(pair, 4)], axis=1)]
+
+    def mlp_part(g, pieces, mn, dy):
+        return mlp(pieces, place, mn, dy, up_bias_groups[g], half)
 
     def mlp_grads(active, dgate):
         return weight_grads(place, links.places if by_hops else 1, mn, dgate, dy2, active, half)
@@ -704,7 +699,9 @@
 
         pair_sums = [v[i] for v in (qkv_sum0, qkv_sum1) for i in range(half // per)]
         qkv_bias_part = spread([v.reshape(3, head_cols) for d in pair_sums for v in split_pair(d, 3)])
-        up_bias_part = spread([v for part in (gate_sum0, gate_sum1) for v in jnp.split(part, half, axis=1)])
+        gate_sums = [v for part in (gate_sum0, gate_sum1) for v in jnp.split(part, half, axis=1)]
+        order = mlp_groups[0] + mlp_groups[1]
+        up_bias_part = spread([gate_sums[order.index(s)] for s in range(tp)])
         bias_part = jnp.sum(cotangent.astype(F32), axis=0)
         pieces = [
             *(sums_own + sums_other)[:4],
@@ -717,76 +714,76 @@
     sizes = [depth] * 4 + [qkv_bias.size, depth, up_bias.size]
 
     attn_cols, mlp_cols = 4 * head_cols, 2 * unit_cols
-    ring = links.ring
+    ring, back = links.ring, links.back
     own_segments = lax.dynamic_slice_in_dim(segments, links.lane * rows // length, rows // length, 0)
     pair_segments = jnp.concatenate([own_segments, links.swap(own_segments)], axis=0)
     attn_slots, pair_segments = sync((attn_slots, pair_segments))
-    for s in range(1, half):
-        attn_slots.append(ring(attn_slots[-1]))
     if by_hops:
-        got = [links.near_places(attn_slots[0])]
+        attn = {0: attn_slots[0], 1: ring(attn_slots[0])}
+        units = {0: mlp_slots[0]}
+        got = [links.near_places(attn[0])]
+        attn, units, pair_segments = sync((attn, units, pair_segments))
+        got.append(links.near_places(attn[1]))
+        units[1], units[3] = ring(units[0]), back(units[0])
         tables = tables_of(pair_segments)
-        attn_slots, tables, x_other, dy_other = sync((attn_slots, tables, x_other, dy_other))
-        got.append(links.near_places(attn_slots[1]))
-        last = [links.hop(got[0][1], 1)]
-        mlp_slots.append(ring(mlp_slots[0]))
+        got, x_other, dy_other = sync((got, x_other, dy_other))
+        last = [links.hop(got[0][1], 1), links.hop(got[1][0], 2)]
         normed = prepare(tokens, x_other, cotangent, dy_other, gains)
-        got, last, normed = sync((got, last, normed))
-        last.append(links.hop(got[1][0], 2))
-        group_a = [[(attn_slots[j], 0, 0), (got[j][0], 1, 0), (got[j][1], 2, 0), (last[j], 3, 0)] for j in (0, 1)]
+        units, last, normed, tables = sync((units, last, normed, tables))
+        piece_b = group_piece([units[1], units[3]])
+        piece_b, normed = sync((piece_b, normed))
+        group_a = [
+            (v, key, ((j, 0),))
+            for j in (0, 1)
+            for v, key in ((attn[j], 0), (got[j][0], 1), (got[j][1], 2), (last[j], 3))
+        ]
     else:
+        attn, units = {0: attn_slots[0]}, {0: mlp_slots[0]}
+        for s in range(1, tp):
+            attn[s] = ring(attn[s - 1])
+            units[s] = ring(units[s - 1])
         tables = tables_of(pair_segments)
         normed = prepare(tokens, x_other, cotangent, dy_other, gains)
-        for s in range(1, half):
-            mlp_slots.append(ring(mlp_slots[-1]))
-        group_a = pieces_of(None, near(group_piece(attn_slots)), None, attn_cols)
-    arrays = [[v[0] for v in slot] for slot in group_a]
-    arrays, mlp_slots, attn_slots, normed = sync((arrays, mlp_slots, attn_slots, normed))
-    group_a = [[(v, *w[1:]) for v, w in zip(vs, slot)] for vs, slot in zip(arrays, group_a)]
+        group_a = pieces_of(None, near(group_piece([attn[s] for s in groups[0]])), None, attn_cols)
     an, mn, dy2 = normed
-    piece_b = group_piece(mlp_slots)
-    piece_b, an, attn_slots = sync((piece_b, an, attn_slots))
-
-    def ring_on(slots, count):
-        for _ in range(count):
-            slots.append(ring(slots[-1]))
-        return slots
+    if not by_hops:
+        piece_b, piece_c, piece_d = [
+            group_piece([v[s] for s in g]) for v, g in ((units, groups[0]), (units, groups[1]), (attn, groups[1]))
+        ]
+    piece_b, an = sync((piece_b, an))
 
     near_b = near(piece_b)
-    mlp_slots = ring_on(mlp_slots, 1)
-    attn_slots = ring_on(attn_slots, 1)
+    if by_hops:
+        units[2], attn[2], attn[3] = ring(units[1]), ring(attn[1]), back(attn[0])
     att0, dmix0, qkv_sum0, qkv0, out0 = attention_part(0, group_a, an, dy2)
-    near_b, mlp_slots, attn_slots, att0, dmix0 = sync((near_b, mlp_slots, attn_slots, att0, dmix0))
+    near_b, attn, units, att0 = sync((near_b, attn, units, att0))
     parts_b = far_parts(near_b)
-    parts_b, mlp_slots, attn_slots, att0 = sync((parts_b, mlp_slots, attn_slots, att0))
+    if by_hops:
+        piece_c = group_piece([units[0], units[2]])
+    parts_b, piece_c, att0 = sync((parts_b, piece_c, att0))
 
     far_b = far(parts_b)
-    mlp_slots = ring_on(mlp_slots, half - 1)
-    attn_slots = ring_on(attn_slots, half - 1)
-    grad_a0 = attention_grads(att0, dmix0)
-    far_b, mlp_slots, attn_slots, grad_a0 = sync((far_b, mlp_slots, attn_slots, grad_a0))
-    piece_c = group_piece(mlp_slots[half:])
-    piece_c, mn = sync((piece_c, mn))
+    grad_a = attention_grads(att0, dmix0)
+    far_b, grad_a, attn, mn = sync((far_b, grad_a, attn, mn))
 
     near_c = near(piece_c)
-    group_b = pieces_of(piece_b, near_b, far_b, mlp_cols)
-    act0, dgate0, gate_sum0, up0, down0 = mlp_front(group_b, place, mn, dy2, up_bias_groups[0])
+    act0, dgate0, gate_sum0, up0, down0 = mlp_part(0, pieces_of(piece_b, near_b, far_b, mlp_cols), mn, dy2)
     near_c, act0 = sync((near_c, act0))
     parts_c = far_parts(near_c)
     parts_c, act0 = sync((parts_c, act0))
 
     far_c = far(parts_c)
-    far_a = sum_far(grad_a0)
+    back_a = sum_far(grad_a)
     grad_b = mlp_grads(act0, dgate0)
-    far_c, far_a, grad_b = sync((far_c, far_a, grad_b))
-    piece_d = group_piece(attn_slots[half:])
-    sent_a = add_far(grad_a0, far_a)
+    far_c, back_a, grad_b, mn = sync((far_c, back_a, grad_b, mn))
+    if by_hops:
+        piece_d = group_piece([attn[2], attn[3]])
+    sent_a = add_far(grad_a, back_a)
     piece_d, sent_a, mn = sync((piece_d, sent_a, mn))
 
     near_d = near(piece_d)
     near_a = sum_near(sent_a)
-    group_c = pieces_of(piece_c, near_c, far_c, mlp_cols)
-    act1, dgate1, gate_sum1, up1, down1 = mlp_front(group_c, place, mn, dy2, up_bias_groups[1])
+    act1, dgate1, gate_sum1, up1, down1 = mlp_part(1, pieces_of(piece_c, near_c, far_c, mlp_cols), mn, dy2)
     near_d, near_a, act1 = sync((near_d, near_a, act1))
     parts_d = far_parts(near_d)
     parts_d, act1 = sync((parts_d, act1))
@@ -794,76 +791,84 @@
     far_d = far(parts_d)
     back_b = sum_far(grad_b)
     grad_c = mlp_grads(act1, dgate1)
-    far_d, back_b, grad_c = sync((far_d, back_b, grad_c))
+    far_d, back_b, grad_c, an = sync((far_d, back_b, grad_c, an))
     sent_b = add_far(grad_b, back_b)
-    sum_a = place_sum(grad_a0, near_a)
-    sent_b, sum_a, an = sync((sent_b, sum_a, an))
+    sum_a = place_sum(grad_a, near_a)
+    sent_b, sum_a, grad_c, an = sync((sent_b, sum_a, grad_c, an))
 
     back_near_b = sum_near(sent_b)
     back_c = sum_far(grad_c)
-    ring_a = links.ring_sum(None, sum_a[1:])
-    group_d = pieces_of(piece_d, near_d, far_d, attn_cols)
-    att1, dmix1, qkv_sum1, qkv1, out1 = attention_part(1, group_d, an, dy2)
-    back_near_b, back_c, ring_a, att1 = sync((back_near_b, back_c, ring_a, att1))
+    att1, dmix1, qkv_sum1, qkv1, out1 = attention_part(1, pieces_of(piece_d, near_d, far_d, attn_cols), an, dy2)
+    back_near_b, back_c, att1 = sync((back_near_b, back_c, att1))
     sent_c = add_far(grad_c, back_c)
     sum_b = place_sum(grad_b, back_near_b)
     sent_c, sum_b, att1 = sync((sent_c, sum_b, att1))
 
     back_near_c = sum_near(sent_c)
-    ring_m = links.ring_sum(None, sum_b[1:])
+    lanes_m = ring(sum_b[1].astype(BF16)) if by_hops else ()
     grad_d = attention_grads(att1, dmix1)
-    ring_m, grad_d, dgate1 = sync((ring_m, grad_d, dgate1))
+    grad_d, dgate1 = sync((grad_d, dgate1))
 
     back_d = sum_far(grad_d)
     terms = ((dgate0, up0), (dgate1, up1), (dmix0, qkv0), (dmix1, qkv1))
     sent_pull, sums_other = pull_back(terms, x_other, gains, rows, BF16)
-    back_near_c, back_d, sent_pull = sync((back_near_c, back_d, sent_pull))
+    back_near_c, back_d, lanes_m, sent_pull, att1 = sync((back_near_c, back_d, lanes_m, sent_pull, att1))
     sum_c = place_sum(grad_c, back_near_c)
+    last_m = sum_c[1].astype(BF16) if by_hops else ()
     sent_d = add_far(grad_d, back_d)
-    term_m = ring_m + sum_c[0]
-    sum_c, sent_d, term_m, dgate1 = sync((sum_c, sent_d, term_m, dgate1))
-
-    near_e = sum_near(sent_d)
-    ring_m = links.ring_sum(None, [term_m] + sum_c[1:-1])
+    sent_d, last_m, sent_pull, att1 = sync((sent_d, last_m, sent_pull, att1))
+
+    back_near_d = sum_near(sent_d)
+    last_m = back(last_m) if by_hops else ()
     other_pull = links.swap(sent_pull)
+    out_terms = ((att0, out0), (att1, out1), (act0, down0), (act1, down1))
+    (sent_out,) = branch_out(out_terms, rows)
+    back_near_d, other_pull, last_m, sent_out, dgate1 = sync((back_near_d, other_pull, last_m, sent_out, dgate1))
+    sum_d = place_sum(grad_d, back_near_d)
+    lanes_a = [v.astype(BF16) for v in sum_d]
+    if by_hops:
+        last_m = (sum_b[0] + last_m.astype(F32)).astype(BF16)
+    lanes_a, last_m, sent_out, dgate1 = sync((lanes_a, last_m, sent_out, dgate1))
+
+    other_out = links.swap(sent_out)
+    if by_hops:
+        lanes_a = [back(lanes_a[0]), ring(lanes_a[1])]
+        last_m = back(last_m)
     terms = ((dgate0, up0), (dgate1, up1), (dmix0, qkv0), (dmix1, qkv1))
     pulled, sums_own = pull_back(terms, tokens, gains, 0, F32)
-    near_e, ring_m, other_pull, pulled = sync((near_e, ring_m, other_pull, pulled))
-    sum_d = place_sum(grad_d, near_e)
-    term_m = ring_m + sum_c[-1]
-    term_a = ring_a + sum_d[0]
+    lanes_a, last_m, other_out, sums_own, att1 = sync((lanes_a, last_m, other_out, sums_own, att1))
     small = small_sums()
-    sum_d, term_m, term_a, small, att1 = sync((sum_d, term_m, term_a, small, att1))
-
     steps = links.sum_steps()
-    ring_m = links.ring_sum(None, [term_m])
-    ring_a = links.ring_sum(None, [term_a] + sum_d[1:-1])
+    if by_hops:
+        last_a = (sum_a[1] + lanes_a[0].astype(F32)).astype(BF16)
+        sum_m = sum_c[0] + lanes_m.astype(F32) + last_m.astype(F32)
+    else:
+        last_a = ()
+        sum_m = links.ring_sum(None, sum_b[1:] + sum_c) + sum_b[0]
+    small, last_a, sum_m, att1 = sync((small, last_a, sum_m, att1))
+
+    if by_hops:
+        last_a = back(last_a)
+    mlp_own = unpair_rows(links, sum_m)
     small = links.sum_step(small, steps[0])
-    out_terms = ((att0, out0), (att1, out1), (act0, down0), (act1, down1))
-    (sent_out,) = branch_out(out_terms, rows)
-    ring_m, ring_a, small, sent_out = sync((ring_m, ring_a, small, sent_out))
-    term_a = ring_a + sum_d[-1]
-    sum_m = ring_m + sum_b[0]
-    term_a, sum_m, small, sent_out = sync((term_a, sum_m, small, sent_out))
-
-    other_out = links.swap(sent_out)
-    ring_a = links.ring_sum(None, [term_a])
-    mlp_own = unpair_rows(links, sum_m)
-    small = links.sum_step(small, steps[1])
-    other_out, small, att1, mlp_own, ring_a = sync((other_out, small, att1, mlp_own, ring_a))
-
-    sum_e = ring_a + sum_a[0]
-    sum_e, small, att1 = sync((sum_e, small, att1))
-    attn_own = unpair_rows(links, sum_e)
-    small = links.sum_step(small, steps[2])
     end_bias = (out_bias.astype(F32) + down_bias.astype(F32))[None]
     out_terms = ((att0, out0), (att1, out1), (act0, down0), (act1, down1))
     output, input_grad = branch_out(
         out_terms, rows, [tokens, other_out, end_bias, cotangent, pulled, other_pull]
     )
-    small, attn_own, output, input_grad = sync((small, attn_own, output, input_grad))
-    for step in steps[3:]:
-        small = links.sum_step(small, step)
+    small, last_a, mlp_own, output, input_grad = sync((small, last_a, mlp_own, output, input_grad))
+    if by_hops:
+        sum_e = sum_a[0] + lanes_a[1].astype(F32) + last_a.astype(F32)
+    else:
+        sum_e = links.ring_sum(None, sum_a[1:] + sum_d) + sum_a[0]
+    attn_own = unpair_rows(links, sum_e)
+    small = links.sum_step(links.sum_step(small, steps[1]), steps[2])
+    if tp == 4 and links.fsdp == 8:
+        a, b, c = [lax.ppermute(small, "tp", [(i, i ^ bit) for i in range(tp)]) for bit in (1, 2, 3)]
+        small = (small + a) + (b + c)
+    else:
+        for step in steps[3:]:
+            small = links.sum_step(small, step)
     up_grad = jnp.concatenate([v[:, :unit_cols] for v in mlp_own], axis=1)
     down_grad = jnp.concatenate([v[:, unit_cols:] for v in mlp_own], axis=1).T
     qkv_grad = jnp.concatenate([v[:, :qkv_cols].reshape(-1, 3, head_cols) for v in attn_own], axis=2)

time: 376 us -> 372 us (0.989)
  starting transfers between devices: 56.5 us -> 70.4 us
  local copies, waits for them, and re-layouts: 25.3 us -> 17.4 us
  Pallas kernels: 223 us -> 217 us
  other arithmetic: 27.4 us -> 23.4 us
    ppermute x0 -> x9, starting transfers between devices: none -> 25.4 us  [the longest x6 20.9 us: back(): lax.ppermute(value, 'tp', [(i, (i - 1) % self.tp) for i in range(self.tp)])]
    ppermute x12 -> x6, starting transfers between devices: 16.6 us -> 5.64 us  [ring(): lax.ppermute(value, 'tp', [(i, (i + 1) % self.tp) for i in range(self.tp)])]
    pallas_call x4, Pallas kernels: 112 us -> 105 us  [the longest x2 71.9 us: attention(): pl.pallas_call(partial(attention_kernel, keys=[v[1:] for v in pieces], bq...]
    ppermute x0 -> x9, waiting for transfers between devices: none -> 6.3 us  [the longest x3 3.48 us: body(): lax.ppermute(small, 'tp', [(i, i ^ bit) for i in range(tp)])]
    ppermute x12 -> x6, waiting for transfers between devices: 16.2 us -> 10 us  [ring(): lax.ppermute(value, 'tp', [(i, (i + 1) % self.tp) for i in range(self.tp)])]
    select_n x1, other arithmetic: 5.88 us -> 0.05 us  [unpair_rows(): jnp.where(links.core == 0, mine, got)]
    unnamed x126 -> x132, local copies, waits for them, and re-layouts: 11.3 us -> 6.69 us
    ppermute x5 -> x3, waiting for transfers between devices: 9.44 us -> 6.25 us  [sum_step(): lax.ppermute(value, name, [(i, i ^ bit) for i in range(size)])]
  transfers between devices with their start and end apart: 60 -> 61, of which waited for: 8 -> 16; matrix products, arithmetic and copies ran while one was open for 9% -> 4% of each run, Pallas kernels for 60% -> 59%
where the time goes in v4:
time: 372 us; the launch traced here: 366 us
  Pallas kernels  217 us (58%)
  starting transfers between devices  70.4 us (19%)
  waiting for transfers between devices  35.3 us (9%)
  other arithmetic  23.4 us (6%)
  local copies, waits for them, and re-layouts  17.4 us (5%)
    pallas_call x2, Pallas kernels, attention(): pl.pallas_call(partial(attention_kernel, keys=[v[1:] for v in pieces], bq...  71.9 us
    pallas_call x4, Pallas kernels, weight_grads(): pl.pallas_call(partial(grads_kernel, count=count, keys=keys), grid_spec=p...  47.8 us
    ppermute x34, starting transfers between devices, hop(): lax.ppermute(value, 'fsdp', [(i, i ^ 2 * bit) for i in range(self.fsdp)])  36.5 us
    pallas_call x2, Pallas kernels, mlp(): pl.pallas_call(partial(mlp_kernel, keys=[v[1:] for v in pieces], count=co...  33.6 us
    pallas_call x2, Pallas kernels, pull_back(): pl.pallas_call(pull_kernel, grid=(rows // br,), in_specs=specs + [tile, w...  29.4 us
    pallas_call x2, Pallas kernels, branch_out(): pl.pallas_call(partial(out_kernel, own=own), grid=(rows // br,), in_specs...  24.7 us
    ppermute x6, starting transfers between devices, back(): lax.ppermute(value, 'tp', [(i, (i - 1) % self.tp) for i in range(self.tp)])  20.9 us
    ppermute x34, waiting for transfers between devices, hop(): lax.ppermute(value, 'fsdp', [(i, i ^ 2 * bit) for i in range(self.fsdp)])  12.7 us
  transfers between devices with their start and end apart: 61, of which 16 were waited for; matrix products, arithmetic and copies ran while one was open for 4% of the time, Pallas kernels for 59%

profile of v4, /device:TPU:0, one launch (start us, length us, event | category | flops | bytes accessed | tf_op | source)
XLA Modules:
  0.0 366.2 jit_solution(17727471587349561751)
XLA Ops:
  15.1 4.9 %collective-permute-done.2.refs_4_ = bf16[256,512]{1,0:T(8,128)(2,1)} collective-permute-done((bf16[256,512]{1,0:T(8,128)(2,1)S(1)}, bf16[256,512]{1,0:T(8,128)(2,1)}, u32[]{:S(2)}, u32[]{:S(2)}) %collective-permute-start.2) | collective-permute-done | bytes 262176 | tf_op jit(solution)/shard_map/ppermute | solution.py:470
  25.4 2.9 collective-permute-done.8.refs_5_
  33.5 9.7 %prepare.1 = (bf16[2048,1024]{1,0:T(8,128)(2,1)}, bf16[2048,1024]{1,0:T(8,128)(2,1)}, bf16[2048,1024]{1,0:T(8,128)(2,1)}) custom-call(bf16[1024,1024]{1,0:T(8,128)(2,1)} %refs_8_.3, bf16[1024,1024]{1,0:T(8,128)(2,1)} %collective-permute-done.10.x_other.refs_8_, bf16[1024,1024]{1,0:T(8,128)(2,1)} %refs_11_.1, ...), custom_call_target="tpu_custom_call" | custom-call | flops 41943040 | bytes 33554432 | tf_op jit(solution)/shard_map/prepare/pallas_call | solution.py:63
  43.2 9.9 %collective-permute-start.17 = (bf16[256,512]{1,0:T(8,128)(2,1)S(1)}, bf16[256,512]{1,0:T(8,128)(2,1)}, u32[]{:S(2)}, u32[]{:S(2)}) collective-permute-start(bf16[256,512]{1,0:T(8,128)(2,1)S(1)} %pad_maximum_fusion.6.refs_0_), channel_id=1, source_target_pairs={{0,3},{1,0},{2,1},{3,2},{4,7},{5,4},{6,5},{7,6},{8,11},{9,8},{10,9... | collective-permute-start | bytes 786440 | tf_op jit(solution)/shard_map/ppermute | solution.py:504
  57.3 36.0 %attention.2 = (bf16[2048,256]{1,0:T(8,128)(2,1)}, bf16[2048,768]{1,0:T(8,128)(2,1)}, f32[2,1,384]{2,1,0:T(1,128)}, bf16[1024,768]{1,0:T(8,128)(2,1)}, bf16[1024,256]{1,0:T(8,128)(2,1)}) custom-call(s32[1]{0:T(128)} %bitcast.place_ref, bf16[2048,1024]{1,0:T(8,128)(2,1)} %get-tuple-element.323.an_ref.left_a, ...), custom_call_target="tpu_custom_call" | custom-call | flops 21474836480 | bytes 37748736 | tf_op jit(solution)/shard_map/attention/pallas_call | solution.py:195
  102.0 9.3 %weight_grads.4 = (bf16[256,512]{1,0:T(8,128)(2,1)}, bf16[256,512]{1,0:T(8,128)(2,1)}, bf16[256,1024]{1,0:T(8,128)(2,1)}, bf16[256,1024]{1,0:T(8,128)(2,1)}, bf16[256,1024]{1,0:T(8,128)(2,1)}) custom-call(s32[1]{0:T(128)} %bitcast.place_ref, bf16[2048,1024]{1,0:T(8,128)(2,1)} %get-tuple-element.323.an_ref.left_a, ...), custom_call_target="tpu_custom_call" | custom-call | flops 4294967296 | bytes 14680064 | tf_op jit(solution)/shard_map/weight_grads/pallas_call | solution.py:329
  116.3 17.0 %mlp.2 = (bf16[2048,1024]{1,0:T(8,128)(2,1)}, bf16[2048,1024]{1,0:T(8,128)(2,1)}, f32[1,1024]{1,0:T(1,128)}, bf16[1024,1024]{1,0:T(8,128)(2,1)}, bf16[1024,1024]{1,0:T(8,128)(2,1)}) custom-call(s32[1]{0:T(128)} %bitcast.place_ref, bf16[2048,1024]{1,0:T(8,128)(2,1)} %get-tuple-element.293.mn_ref.left_a, bf16[2048,1024]{1,0:T(8,128)(2,1)} %get-tuple-element.238.dy_ref.left_b, ...), custom_call_target="tpu_custom_call" | custom-call | flops 8589934592 | bytes 25165824 | tf_op jit(solution)/shard_map/mlp/pallas_call | solution.py:265
  137.8 14.4 %weight_grads.5 = (bf16[256,1024]{1,0:T(8,128)(2,1)}, bf16[256,1024]{1,0:T(8,128)(2,1)}, bf16[256,2048]{1,0:T(8,128)(2,1)}, bf16[256,2048]{1,0:T(8,128)(2,1)}, bf16[256,2048]{1,0:T(8,128)(2,1)}) custom-call(s32[1]{0:T(128)} %bitcast.place_ref, bf16[2048,1024]{1,0:T(8,128)(2,1)} %get-tuple-element.293.mn_ref.left_a, ...), custom_call_target="tpu_custom_call" | custom-call | flops 8589934592 | bytes 20971520 | tf_op jit(solution)/shard_map/weight_grads/pallas_call | solution.py:329
  157.1 16.6 %mlp.3 = (bf16[2048,1024]{1,0:T(8,128)(2,1)}, bf16[2048,1024]{1,0:T(8,128)(2,1)}, f32[1,1024]{1,0:T(1,128)}, bf16[1024,1024]{1,0:T(8,128)(2,1)}, bf16[1024,1024]{1,0:T(8,128)(2,1)}) custom-call(s32[1]{0:T(128)} %bitcast.place_ref, bf16[2048,1024]{1,0:T(8,128)(2,1)} %get-tuple-element.293.mn_ref.left_a, bf16[2048,1024]{1,0:T(8,128)(2,1)} %get-tuple-element.238.dy_ref.left_b, ...), custom_call_target="tpu_custom_call" | custom-call | flops 8589934592 | bytes 25165824 | tf_op jit(solution)/shard_map/mlp/pallas_call | solution.py:265
  175.4 4.8 %collective-permute-done.30 = bf16[256,1024]{1,0:T(8,128)(2,1)S(1)} collective-permute-done((bf16[256,1024]{1,0:T(8,128)(2,1)S(1)}, bf16[256,1024]{1,0:T(8,128)(2,1)S(1)}, u32[]{:S(2)}, u32[]{:S(2)}) %collective-permute-start.30) | collective-permute-done | bytes 524320 | tf_op jit(solution)/shard_map/ppermute | solution.py:467
  181.3 14.5 %weight_grads.6 = (bf16[256,1024]{1,0:T(8,128)(2,1)}, bf16[256,1024]{1,0:T(8,128)(2,1)}, bf16[256,2048]{1,0:T(8,128)(2,1)}, bf16[256,2048]{1,0:T(8,128)(2,1)}, bf16[256,2048]{1,0:T(8,128)(2,1)}) custom-call(s32[1]{0:T(128)} %bitcast.place_ref, bf16[2048,1024]{1,0:T(8,128)(2,1)} %get-tuple-element.293.mn_ref.left_a, ...), custom_call_target="tpu_custom_call" | custom-call | flops 8589934592 | bytes 20971520 | tf_op jit(solution)/shard_map/weight_grads/pallas_call | solution.py:329
  203.0 35.8 %attention.3 = (bf16[2048,256]{1,0:T(8,128)(2,1)}, bf16[2048,768]{1,0:T(8,128)(2,1)}, f32[2,1,384]{2,1,0:T(1,128)}, bf16[1024,768]{1,0:T(8,128)(2,1)}, bf16[1024,256]{1,0:T(8,128)(2,1)}) custom-call(s32[1]{0:T(128)} %bitcast.place_ref, bf16[2048,1024]{1,0:T(8,128)(2,1)} %get-tuple-element.323.an_ref.left_a, ...), custom_call_target="tpu_custom_call" | custom-call | flops 21474836480 | bytes 37748736 | tf_op jit(solution)/shard_map/attention/pallas_call | solution.py:195
  239.5 2.8 fusion.5
  245.7 9.5 %weight_grads.7 = (bf16[256,512]{1,0:T(8,128)(2,1)}, bf16[256,512]{1,0:T(8,128)(2,1)}, bf16[256,1024]{1,0:T(8,128)(2,1)}, bf16[256,1024]{1,0:T(8,128)(2,1)}, bf16[256,1024]{1,0:T(8,128)(2,1)}) custom-call(s32[1]{0:T(128)} %bitcast.place_ref, bf16[2048,1024]{1,0:T(8,128)(2,1)} %get-tuple-element.323.an_ref.left_a, ...), custom_call_target="tpu_custom_call" | custom-call | flops 4294967296 | bytes 14680064 | tf_op jit(solution)/shard_map/weight_grads/pallas_call | solution.py:329
  256.7 14.6 %pull_back.2 = (bf16[1024,1024]{1,0:T(8,128)(2,1)}, f32[8,1024]{1,0:T(8,128)}) custom-call(bf16[2048,1024]{1,0:T(8,128)(2,1)} %get-tuple-element.275.right_a.refs_0_, bf16[1024,1024]{1,0:T(8,128)(2,1)} %get-tuple-element.353.refs_1_, bf16[2048,1024]{1,0:T(8,128)(2,1)} %get-tuple-element.386.right_a.refs_2_, bf16[1024,1024]{1,0:T(8,128)(2,1)} %get-tuple-element.355.refs_3_, ...), custom_call_target="tpu_custom_call" | custom-call | flops 7516192768 | bytes 23068672 | tf_op jit(solution)/shard_map/pull_back/pallas_call | solution.py:388
  279.4 3.4 collective-permute-start.47
  282.8 10.3 %branch_out.2 = bf16[1024,1024]{1,0:T(8,128)(2,1)} custom-call(bf16[2048,256]{1,0:T(8,128)(2,1)} %get-tuple-element.255.right_b.refs_0_, bf16[1024,256]{1,0:T(8,128)(2,1)} %get-tuple-element.371.refs_1_, bf16[2048,256]{1,0:T(8,128)(2,1)} %get-tuple-element.402.right_b.refs_2_, bf16[1024,256]{1,0:T(8,128)(2,1)} %get-tuple-element.373.refs_3_, ...), custom_call_target="tpu_custom_call" | custom-call | flops 5368709120 | bytes 12582912 | tf_op jit(solution)/shard_map/branch_out/pallas_call | solution.py:435
  297.5 4.3 %collective-permute-start.50 = (bf16[256,1024]{1,0:T(8,128)(2,1)}, bf16[256,1024]{1,0:T(8,128)(2,1)S(1)}, u32[]{:S(2)}, u32[]{:S(2)}) collective-permute-start(bf16[256,1024]{1,0:T(8,128)(2,1)} %add_convert_fusion), channel_id=1, source_target_pairs={{0,3},{1,0},{2,1},{3,2},{4,7},{5,4},{6,5},{7,6},{8,11},{9,8},{10,9... | collective-permute-start | bytes 1572872 | tf_op jit(solution)/shard_map/ppermute | solution.py:504
  303.9 14.8 %pull_back.3 = (f32[1024,1024]{1,0:T(8,128)}, f32[8,1024]{1,0:T(8,128)}) custom-call(bf16[2048,1024]{1,0:T(8,128)(2,1)} %get-tuple-element.275.right_a.refs_0_, bf16[1024,1024]{1,0:T(8,128)(2,1)} %get-tuple-element.353.refs_1_, bf16[2048,1024]{1,0:T(8,128)(2,1)} %get-tuple-element.386.right_a.refs_2_, bf16[1024,1024]{1,0:T(8,128)(2,1)} %get-tuple-element.355.refs_3_, ...), custom_call_target="tpu_custom_call" | custom-call | flops 7516192768 | bytes 23068672 | tf_op jit(solution)/shard_map/pull_back/pallas_call | solution.py:388
  320.2 5.1 %collective-permute-done.49 = bf16[256,512]{1,0:T(8,128)(2,1)S(1)} collective-permute-done((bf16[256,512]{1,0:T(8,128)(2,1)S(1)}, bf16[256,512]{1,0:T(8,128)(2,1)S(1)}, u32[]{:S(2)}, u32[]{:S(2)}) %collective-permute-start.49) | collective-permute-done | bytes 262176 | tf_op jit(solution)/shard_map/ppermute | solution.py:470
  329.1 14.5 %branch_out.3 = (bf16[1024,1024]{1,0:T(8,128)(2,1)}, f32[1024,1024]{1,0:T(8,128)}) custom-call(bf16[2048,256]{1,0:T(8,128)(2,1)} %get-tuple-element.255.right_b.refs_0_, bf16[1024,256]{1,0:T(8,128)(2,1)} %get-tuple-element.371.refs_1_, bf16[2048,256]{1,0:T(8,128)(2,1)} %get-tuple-element.402.right_b.refs_2_, bf16[1024,256]{1,0:T(8,128)(2,1)} %get-tuple-element.373.refs_3_, ...), custom_call_target="tpu_custom_call" | custom-call | flops 5368709120 | bytes 29360128 | tf_op jit(solution)/shard_map/branch_out/pallas_call | solution.py:435
  344.6 3.5 collective-permute-done.55
  349.4 2.8 collective-permute-done.56
  357.7 3.5 collective-permute-done.59
  (351 shorter events, 98.7 us)
Async XLA Ops:
  5.6 25.0 %collective-permute-start.10 = (bf16[1024,1024]{1,0:T(8,128)(2,1)}, bf16[1024,1024]{1,0:T(8,128)(2,1)}, u32[]{:S(2)}, u32[]{:S(2)}) collective-permute-start(bf16[1024,1024]{1,0:T(8,128)(2,1)} %refs_8_.3), channel_id=1, source_target_pairs={{0,4},{4,0},{8,12},{12,8},{16,20},{20,16},{24,28},{28,24},{1,5},{5... | collective-permute-start | bytes 6291464 | tf_op jit(solution)/shard_map/ppermute | solution.py:464
  5.7 24.9 %collective-permute-start.11 = (bf16[1024,1024]{1,0:T(8,128)(2,1)S(1)}, bf16[1024,1024]{1,0:T(8,128)(2,1)}, u32[]{:S(2)}, u32[]{:S(2)}) collective-permute-start(bf16[1024,1024]{1,0:T(8,128)(2,1)S(1)} %copy-done.2), channel_id=1, source_target_pairs={{0,4},{4,0},{8,12},{12,8},{16,20},{20,16},{24,28},{28,24},{1,5},{5... | collective-permute-start | bytes 6291464 | tf_op jit(solution)/shard_map/ppermute | solution.py:464
  28.3 25.2 %collective-permute-start.5 = (bf16[256,1024]{1,0:T(8,128)(2,1)S(1)}, bf16[256,1024]{1,0:T(8,128)(2,1)S(1)}, u32[]{:S(2)}, u32[]{:S(2)}) collective-permute-start(bf16[256,1024]{1,0:T(8,128)(2,1)S(1)} %pad_maximum_fusion.2), channel_id=1, source_target_pairs={{0,3},{1,0},{2,1},{3,2},{4,7},{5,4},{6,5},{7,6},{8,11},{9,8},{10,9... | collective-permute-start | bytes 1572872 | tf_op jit(solution)/shard_map/ppermute | solution.py:504
  30.6 62.7 %collective-permute-start.16 = (bf16[256,512]{1,0:T(8,128)(2,1)}, bf16[256,512]{1,0:T(8,128)(2,1)}, u32[]{:S(2)}, u32[]{:S(2)}) collective-permute-start(bf16[256,512]{1,0:T(8,128)(2,1)} %collective-permute-done.2.refs_4_), channel_id=1, source_target_pairs={{0,1},{1,2},{2,3},{3,0},{4,5},{5,6},{6,7},{7,4},{8,9},{9,10},{10,1... | collective-permute-start | bytes 786440 | tf_op jit(solution)/shard_map/ppermute | solution.py:470
  30.6 22.9 %collective-permute-start.12 = (bf16[256,512]{1,0:T(8,128)(2,1)S(1)}, bf16[256,512]{1,0:T(8,128)(2,1)S(1)}, u32[]{:S(2)}, u32[]{:S(2)}) collective-permute-start(bf16[256,512]{1,0:T(8,128)(2,1)S(1)} %collective-permute-done.7.refs_2_), channel_id=1, source_target_pairs={{0,8},{4,12},{8,0},{12,4},{16,24},{20,28},{24,16},{28,20},{1,9},{5... | collective-permute-start | bytes 786440 | tf_op jit(solution)/shard_map/ppermute | solution.py:467
  43.2 50.1 %collective-permute-start.17 = (bf16[256,512]{1,0:T(8,128)(2,1)S(1)}, bf16[256,512]{1,0:T(8,128)(2,1)}, u32[]{:S(2)}, u32[]{:S(2)}) collective-permute-start(bf16[256,512]{1,0:T(8,128)(2,1)S(1)} %pad_maximum_fusion.6.refs_0_), channel_id=1, source_target_pairs={{0,3},{1,0},{2,1},{3,2},{4,7},{5,4},{6,5},{7,6},{8,11},{9,8},{10,9... | collective-permute-start | bytes 786440 | tf_op jit(solution)/shard_map/ppermute | solution.py:504
  54.4 39.0 %collective-permute-start.14 = (bf16[256,2048]{1,0:T(8,128)(2,1)S(1)}, bf16[256,2048]{1,0:T(8,128)(2,1)}, u32[]{:S(2)}, u32[]{:S(2)}) collective-permute-start(bf16[256,2048]{1,0:T(8,128)(2,1)S(1)} %pad_maximum_fusion.refs_0_), channel_id=1, source_target_pairs={{0,8},{4,12},{8,0},{12,4},{16,24},{20,28},{24,16},{28,20},{1,9},{5... | collective-permute-start | bytes 3145736 | tf_op jit(solution)/shard_map/ppermute | solution.py:467
  55.0 38.3 %collective-permute-start.15 = (bf16[256,2048]{1,0:T(8,128)(2,1)S(1)}, bf16[256,2048]{1,0:T(8,128)(2,1)}, u32[]{:S(2)}, u32[]{:S(2)}) collective-permute-start(bf16[256,2048]{1,0:T(8,128)(2,1)S(1)} %pad_maximum_fusion.refs_0_), channel_id=1, source_target_pairs={{0,16},{4,20},{8,24},{12,28},{16,0},{20,4},{24,8},{28,12},{1,17},{... | collective-permute-start | bytes 3145736 | tf_op jit(solution)/shard_map/ppermute | solution.py:467
  55.5 37.8 %collective-permute-start.18 = (bf16[256,1024]{1,0:T(8,128)(2,1)S(1)}, bf16[256,1024]{1,0:T(8,128)(2,1)}, u32[]{:S(2)}, u32[]{:S(2)}) collective-permute-start(bf16[256,1024]{1,0:T(8,128)(2,1)S(1)} %collective-permute-done.4), channel_id=1, source_target_pairs={{0,1},{1,2},{2,3},{3,0},{4,5},{5,6},{6,7},{7,4},{8,9},{9,10},{10,1... | collective-permute-start | bytes 1572872 | tf_op jit(solution)/shard_map/ppermute | solution.py:470
  101.0 33.1 %collective-permute-start.19 = (bf16[256,2048]{1,0:T(8,128)(2,1)S(1)}, bf16[256,2048]{1,0:T(8,128)(2,1)S(1)}, u32[]{:S(2)}, u32[]{:S(2)}) collective-permute-start(bf16[256,2048]{1,0:T(8,128)(2,1)S(1)} %pad_maximum_fusion.1.refs_0_), channel_id=1, source_target_pairs={{0,8},{4,12},{8,0},{12,4},{16,24},{20,28},{24,16},{28,20},{1,9},{5... | collective-permute-start | bytes 3145736 | tf_op jit(solution)/shard_map/ppermute | solution.py:467
  101.5 34.1 %collective-permute-start.20 = (bf16[256,2048]{1,0:T(8,128)(2,1)S(1)}, bf16[256,2048]{1,0:T(8,128)(2,1)S(1)}, u32[]{:S(2)}, u32[]{:S(2)}) collective-permute-start(bf16[256,2048]{1,0:T(8,128)(2,1)S(1)} %pad_maximum_fusion.1.refs_0_), channel_id=1, source_target_pairs={{0,16},{4,20},{8,24},{12,28},{16,0},{20,4},{24,8},{28,12},{1,17},{... | collective-permute-start | bytes 3145736 | tf_op jit(solution)/shard_map/ppermute | solution.py:467
  113.1 39.1 %collective-permute-start.25 = (bf16[256,512]{1,0:T(8,128)(2,1)}, bf16[256,512]{1,0:T(8,128)(2,1)S(1)}, u32[]{:S(2)}, u32[]{:S(2)}) collective-permute-start(bf16[256,512]{1,0:T(8,128)(2,1)} %get-tuple-element.273), channel_id=1, source_target_pairs={{0,16},{4,20},{8,24},{12,28},{16,0},{20,4},{24,8},{28,12},{1,17},{... | collective-permute-start | bytes 786440 | tf_op jit(solution)/shard_map/ppermute | solution.py:467
  114.7 37.6 %collective-permute-start.26 = (bf16[256,512]{1,0:T(8,128)(2,1)}, bf16[256,512]{1,0:T(8,128)(2,1)S(1)}, u32[]{:S(2)}, u32[]{:S(2)}) collective-permute-start(bf16[256,512]{1,0:T(8,128)(2,1)} %get-tuple-element.274), channel_id=1, source_target_pairs={{0,8},{4,12},{8,0},{12,4},{16,24},{20,28},{24,16},{28,20},{1,9},{5... | collective-permute-start | bytes 786440 | tf_op jit(solution)/shard_map/ppermute | solution.py:467
  155.1 25.1 %collective-permute-start.30 = (bf16[256,1024]{1,0:T(8,128)(2,1)S(1)}, bf16[256,1024]{1,0:T(8,128)(2,1)S(1)}, u32[]{:S(2)}, u32[]{:S(2)}) collective-permute-start(bf16[256,1024]{1,0:T(8,128)(2,1)S(1)} %fusion.7), channel_id=1, source_target_pairs={{0,16},{4,20},{8,24},{12,28},{16,0},{20,4},{24,8},{28,12},{1,17},{... | collective-permute-start | bytes 1572872 | tf_op jit(solution)/shard_map/ppermute | solution.py:467
  156.6 39.6 %collective-permute-start.33 = (bf16[256,1024]{1,0:T(8,128)(2,1)}, bf16[256,1024]{1,0:T(8,128)(2,1)S(1)}, u32[]{:S(2)}, u32[]{:S(2)}) collective-permute-start(bf16[256,1024]{1,0:T(8,128)(2,1)} %get-tuple-element.302), channel_id=1, source_target_pairs={{0,16},{4,20},{8,24},{12,28},{16,0},{20,4},{24,8},{28,12},{1,17},{... | collective-permute-start | bytes 1572872 | tf_op jit(solution)/shard_map/ppermute | solution.py:467
  198.8 40.0 %collective-permute-start.35 = (bf16[256,2048]{1,0:T(8,128)(2,1)S(1)}, bf16[256,2048]{1,0:T(8,128)(2,1)S(1)}, u32[]{:S(2)}, u32[]{:S(2)}) collective-permute-start(bf16[256,2048]{1,0:T(8,128)(2,1)S(1)} %fusion.2), channel_id=1, source_target_pairs={{0,8},{4,12},{8,0},{12,4},{16,24},{20,28},{24,16},{28,20},{1,9},{5... | collective-permute-start | bytes 3145736 | tf_op jit(solution)/shard_map/ppermute | solution.py:467
  200.4 38.5 %collective-permute-start.36 = (bf16[256,2048]{1,0:T(8,128)(2,1)}, bf16[256,2048]{1,0:T(8,128)(2,1)S(1)}, u32[]{:S(2)}, u32[]{:S(2)}) collective-permute-start(bf16[256,2048]{1,0:T(8,128)(2,1)} %fusion.3), channel_id=1, source_target_pairs={{0,16},{4,20},{8,24},{12,28},{16,0},{20,4},{24,8},{28,12},{1,17},{... | collective-permute-start | bytes 3145736 | tf_op jit(solution)/shard_map/ppermute | solution.py:467
  202.0 36.9 %collective-permute-start.37 = (bf16[256,1024]{1,0:T(8,128)(2,1)S(1)}, bf16[256,1024]{1,0:T(8,128)(2,1)S(1)}, u32[]{:S(2)}, u32[]{:S(2)}) collective-permute-start(bf16[256,1024]{1,0:T(8,128)(2,1)S(1)} %copy-done.43), channel_id=1, source_target_pairs={{0,16},{4,20},{8,24},{12,28},{16,0},{20,4},{24,8},{28,12},{1,17},{... | collective-permute-start | bytes 1572872 | tf_op jit(solution)/shard_map/ppermute | solution.py:467
  202.4 36.4 %collective-permute-start.38 = (bf16[256,1024]{1,0:T(8,128)(2,1)S(1)}, bf16[256,1024]{1,0:T(8,128)(2,1)S(1)}, u32[]{:S(2)}, u32[]{:S(2)}) collective-permute-start(bf16[256,1024]{1,0:T(8,128)(2,1)S(1)} %copy-done.42), channel_id=1, source_target_pairs={{0,8},{4,12},{8,0},{12,4},{16,24},{20,28},{24,16},{28,20},{1,9},{5... | collective-permute-start | bytes 1572872 | tf_op jit(solution)/shard_map/ppermute | solution.py:467
  242.6 28.8 %collective-permute-start.39 = (bf16[256,2048]{1,0:T(8,128)(2,1)S(1)}, bf16[256,2048]{1,0:T(8,128)(2,1)S(1)}, u32[]{:S(2)}, u32[]{:S(2)}) collective-permute-start(bf16[256,2048]{1,0:T(8,128)(2,1)S(1)} %fusion.4), channel_id=1, source_target_pairs={{0,8},{4,12},{8,0},{12,4},{16,24},{20,28},{24,16},{28,20},{1,9},{5... | collective-permute-start | bytes 3145736 | tf_op jit(solution)/shard_map/ppermute | solution.py:467
  244.1 27.3 %collective-permute-start.40 = (bf16[256,2048]{1,0:T(8,128)(2,1)}, bf16[256,2048]{1,0:T(8,128)(2,1)S(1)}, u32[]{:S(2)}, u32[]{:S(2)}) collective-permute-start(bf16[256,2048]{1,0:T(8,128)(2,1)} %fusion.5), channel_id=1, source_target_pairs={{0,16},{4,20},{8,24},{12,28},{16,0},{20,4},{24,8},{28,12},{1,17},{... | collective-permute-start | bytes 3145736 | tf_op jit(solution)/shard_map/ppermute | solution.py:467
  296.1 29.2 %collective-permute-start.51 = (bf16[1024,1024]{1,0:T(8,128)(2,1)}, bf16[1024,1024]{1,0:T(8,128)(2,1)}, u32[]{:S(2)}, u32[]{:S(2)}) collective-permute-start(bf16[1024,1024]{1,0:T(8,128)(2,1)} %branch_out.2), channel_id=1, source_target_pairs={{0,4},{4,0},{8,12},{12,8},{16,20},{20,16},{24,28},{28,24},{1,5},{5... | collective-permute-start | bytes 6291464 | tf_op jit(solution)/shard_map/ppermute | solution.py:464
  297.5 27.8 %collective-permute-start.50 = (bf16[256,1024]{1,0:T(8,128)(2,1)}, bf16[256,1024]{1,0:T(8,128)(2,1)S(1)}, u32[]{:S(2)}, u32[]{:S(2)}) collective-permute-start(bf16[256,1024]{1,0:T(8,128)(2,1)} %add_convert_fusion), channel_id=1, source_target_pairs={{0,3},{1,0},{2,1},{3,2},{4,7},{5,4},{6,5},{7,6},{8,11},{9,8},{10,9... | collective-permute-start | bytes 1572872 | tf_op jit(solution)/shard_map/ppermute | solution.py:504
  301.9 23.4 %collective-permute-start.49 = (bf16[256,512]{1,0:T(8,128)(2,1)S(1)}, bf16[256,512]{1,0:T(8,128)(2,1)S(1)}, u32[]{:S(2)}, u32[]{:S(2)}) collective-permute-start(bf16[256,512]{1,0:T(8,128)(2,1)S(1)} %get-tuple-element.383), channel_id=1, source_target_pairs={{0,1},{1,2},{2,3},{3,0},{4,5},{5,6},{6,7},{7,4},{8,9},{9,10},{10,1... | collective-permute-start | bytes 786440 | tf_op jit(solution)/shard_map/ppermute | solution.py:470
  (94 other events, 1053.2 us)

commit v5 on v4

--- a/solution.py
+++ b/solution.py
@@ -754,7 +754,7 @@
 
     near_b = near(piece_b)
     if by_hops:
-        units[2], attn[2], attn[3] = ring(units[1]), ring(attn[1]), back(attn[0])
+        units[2] = ring(units[1])
     att0, dmix0, qkv_sum0, qkv0, out0 = attention_part(0, group_a, an, dy2)
     near_b, attn, units, att0 = sync((near_b, attn, units, att0))
     parts_b = far_parts(near_b)
@@ -763,12 +763,14 @@
     parts_b, piece_c, att0 = sync((parts_b, piece_c, att0))
 
     far_b = far(parts_b)
+    if by_hops:
+        attn[2], attn[3] = ring(attn[1]), back(attn[0])
     grad_a = attention_grads(att0, dmix0)
-    far_b, grad_a, attn, mn = sync((far_b, grad_a, attn, mn))
+    far_b, grad_a, mn = sync((far_b, grad_a, mn))
 
     near_c = near(piece_c)
     act0, dgate0, gate_sum0, up0, down0 = mlp_part(0, pieces_of(piece_b, near_b, far_b, mlp_cols), mn, dy2)
-    near_c, act0 = sync((near_c, act0))
+    near_c, attn, act0 = sync((near_c, attn, act0))
     parts_c = far_parts(near_c)
     parts_c, act0 = sync((parts_c, act0))
 

time: 372 us -> 369 us (level)
  starting transfers between devices: 70.4 us -> 66.4 us
    ppermute x6, waiting for transfers between devices: 2.82 us -> 11.2 us  [back(): lax.ppermute(value, 'tp', [(i, (i - 1) % self.tp) for i in range(self.tp)])]
    ppermute x6, starting transfers between devices: 20.9 us -> 14.2 us  [back(): lax.ppermute(value, 'tp', [(i, (i - 1) % self.tp) for i in range(self.tp)])]
    ppermute x34, waiting for transfers between devices: 12.7 us -> 8.37 us  [hop(): lax.ppermute(value, 'fsdp', [(i, i ^ 2 * bit) for i in range(self.fsdp)])]
  transfers between devices with their start and end apart: 61 -> 61, of which waited for: 16 -> 12; matrix products, arithmetic and copies ran while one was open for 4% -> 4% of each run, Pallas kernels for 59% -> 60%
where the time goes in v5:
time: 369 us; the launch traced here: 364 us
  Pallas kernels  216 us (59%)
  starting transfers between devices  66.4 us (18%)
  waiting for transfers between devices  38.3 us (10%)
  other arithmetic  22.4 us (6%)
  local copies, waits for them, and re-layouts  17.5 us (5%)
    pallas_call x2, Pallas kernels, attention(): pl.pallas_call(partial(attention_kernel, keys=[v[1:] for v in pieces], bq...  71.7 us
    pallas_call x4, Pallas kernels, weight_grads(): pl.pallas_call(partial(grads_kernel, count=count, keys=keys), grid_spec=p...  47.8 us
    ppermute x34, starting transfers between devices, hop(): lax.ppermute(value, 'fsdp', [(i, i ^ 2 * bit) for i in range(self.fsdp)])  37.4 us
    pallas_call x2, Pallas kernels, mlp(): pl.pallas_call(partial(mlp_kernel, keys=[v[1:] for v in pieces], count=co...  33.1 us
    pallas_call x2, Pallas kernels, pull_back(): pl.pallas_call(pull_kernel, grid=(rows // br,), in_specs=specs + [tile, w...  29.4 us
    pallas_call x2, Pallas kernels, branch_out(): pl.pallas_call(partial(out_kernel, own=own), grid=(rows // br,), in_specs...  24.7 us
    ppermute x6, starting transfers between devices, back(): lax.ppermute(value, 'tp', [(i, (i - 1) % self.tp) for i in range(self.tp)])  14.2 us
    ppermute x6, waiting for transfers between devices, back(): lax.ppermute(value, 'tp', [(i, (i - 1) % self.tp) for i in range(self.tp)])  11.2 us
  transfers between devices with their start and end apart: 61, of which 12 were waited for; matrix products, arithmetic and copies ran while one was open for 4% of the time, Pallas kernels for 60%

profile of v5, /device:TPU:0, one launch (start us, length us, event | category | flops | bytes accessed | tf_op | source)
XLA Modules:
  0.0 363.7 jit_solution(243889752253589432)
XLA Ops:
  8.3 2.7 collective-permute-start.2
  15.1 4.8 %collective-permute-done.2.refs_4_ = bf16[256,512]{1,0:T(8,128)(2,1)S(1)} collective-permute-done((bf16[256,512]{1,0:T(8,128)(2,1)S(1)}, bf16[256,512]{1,0:T(8,128)(2,1)S(1)}, u32[]{:S(2)}, u32[]{:S(2)}) %collective-permute-start.2) | collective-permute-done | bytes 262176 | tf_op jit(solution)/shard_map/ppermute | solution.py:470
  32.9 9.7 %prepare.1 = (bf16[2048,1024]{1,0:T(8,128)(2,1)}, bf16[2048,1024]{1,0:T(8,128)(2,1)}, bf16[2048,1024]{1,0:T(8,128)(2,1)}) custom-call(bf16[1024,1024]{1,0:T(8,128)(2,1)} %refs_8_.3, bf16[1024,1024]{1,0:T(8,128)(2,1)} %collective-permute-done.10.x_other.refs_8_, bf16[1024,1024]{1,0:T(8,128)(2,1)} %refs_11_.1, ...), custom_call_target="tpu_custom_call" | custom-call | flops 41943040 | bytes 33554432 | tf_op jit(solution)/shard_map/prepare/pallas_call | solution.py:63
  42.7 8.7 %collective-permute-done.5 = bf16[256,1024]{1,0:T(8,128)(2,1)S(1)} collective-permute-done((bf16[256,1024]{1,0:T(8,128)(2,1)S(1)}, bf16[256,1024]{1,0:T(8,128)(2,1)S(1)}, u32[]{:S(2)}, u32[]{:S(2)}) %collective-permute-start.5) | collective-permute-done | bytes 524320 | tf_op jit(solution)/shard_map/ppermute | solution.py:504
  55.5 35.8 %attention.2 = (bf16[2048,256]{1,0:T(8,128)(2,1)}, bf16[2048,768]{1,0:T(8,128)(2,1)}, f32[2,1,384]{2,1,0:T(1,128)}, bf16[1024,768]{1,0:T(8,128)(2,1)}, bf16[1024,256]{1,0:T(8,128)(2,1)}) custom-call(s32[1]{0:T(128)} %bitcast.place_ref, bf16[2048,1024]{1,0:T(8,128)(2,1)} %get-tuple-element.323.an_ref.left_a, ...), custom_call_target="tpu_custom_call" | custom-call | flops 21474836480 | bytes 37748736 | tf_op jit(solution)/shard_map/attention/pallas_call | solution.py:195
  100.7 9.4 %weight_grads.4 = (bf16[256,512]{1,0:T(8,128)(2,1)}, bf16[256,512]{1,0:T(8,128)(2,1)}, bf16[256,1024]{1,0:T(8,128)(2,1)}, bf16[256,1024]{1,0:T(8,128)(2,1)}, bf16[256,1024]{1,0:T(8,128)(2,1)}) custom-call(s32[1]{0:T(128)} %bitcast.place_ref, bf16[2048,1024]{1,0:T(8,128)(2,1)} %get-tuple-element.323.an_ref.left_a, ...), custom_call_target="tpu_custom_call" | custom-call | flops 4294967296 | bytes 14680064 | tf_op jit(solution)/shard_map/weight_grads/pallas_call | solution.py:329
  110.2 3.7 %collective-permute-start.20 = (bf16[256,512]{1,0:T(8,128)(2,1)S(1)}, bf16[256,512]{1,0:T(8,128)(2,1)S(1)}, u32[]{:S(2)}, u32[]{:S(2)}) collective-permute-start(bf16[256,512]{1,0:T(8,128)(2,1)S(1)} %copy-done.22), channel_id=1, source_target_pairs={{0,3},{1,0},{2,1},{3,2},{4,7},{5,4},{6,5},{7,6},{8,11},{9,8},{10,9... | collective-permute-start | bytes 786440 | tf_op jit(solution)/shard_map/ppermute | solution.py:504
  115.2 16.5 %mlp.2 = (bf16[2048,1024]{1,0:T(8,128)(2,1)}, bf16[2048,1024]{1,0:T(8,128)(2,1)}, f32[1,1024]{1,0:T(1,128)}, bf16[1024,1024]{1,0:T(8,128)(2,1)}, bf16[1024,1024]{1,0:T(8,128)(2,1)}) custom-call(s32[1]{0:T(128)} %bitcast.place_ref, bf16[2048,1024]{1,0:T(8,128)(2,1)} %get-tuple-element.293.mn_ref.left_a, bf16[2048,1024]{1,0:T(8,128)(2,1)} %get-tuple-element.238.dy_ref.left_b, ...), custom_call_target="tpu_custom_call" | custom-call | flops 8589934592 | bytes 25165824 | tf_op jit(solution)/shard_map/mlp/pallas_call | solution.py:265
  135.7 14.4 %weight_grads.5 = (bf16[256,1024]{1,0:T(8,128)(2,1)}, bf16[256,1024]{1,0:T(8,128)(2,1)}, bf16[256,2048]{1,0:T(8,128)(2,1)}, bf16[256,2048]{1,0:T(8,128)(2,1)}, bf16[256,2048]{1,0:T(8,128)(2,1)}) custom-call(s32[1]{0:T(128)} %bitcast.place_ref, bf16[2048,1024]{1,0:T(8,128)(2,1)} %get-tuple-element.293.mn_ref.left_a, ...), custom_call_target="tpu_custom_call" | custom-call | flops 8589934592 | bytes 20971520 | tf_op jit(solution)/shard_map/weight_grads/pallas_call | solution.py:329
  155.2 16.6 %mlp.3 = (bf16[2048,1024]{1,0:T(8,128)(2,1)}, bf16[2048,1024]{1,0:T(8,128)(2,1)}, f32[1,1024]{1,0:T(1,128)}, bf16[1024,1024]{1,0:T(8,128)(2,1)}, bf16[1024,1024]{1,0:T(8,128)(2,1)}) custom-call(s32[1]{0:T(128)} %bitcast.place_ref, bf16[2048,1024]{1,0:T(8,128)(2,1)} %get-tuple-element.293.mn_ref.left_a, bf16[2048,1024]{1,0:T(8,128)(2,1)} %get-tuple-element.238.dy_ref.left_b, ...), custom_call_target="tpu_custom_call" | custom-call | flops 8589934592 | bytes 25165824 | tf_op jit(solution)/shard_map/mlp/pallas_call | solution.py:265
  173.3 4.4 %collective-permute-done.30 = bf16[256,1024]{1,0:T(8,128)(2,1)S(1)} collective-permute-done((bf16[256,1024]{1,0:T(8,128)(2,1)S(1)}, bf16[256,1024]{1,0:T(8,128)(2,1)S(1)}, u32[]{:S(2)}, u32[]{:S(2)}) %collective-permute-start.30) | collective-permute-done | bytes 524320 | tf_op jit(solution)/shard_map/ppermute | solution.py:467
  179.4 14.5 %weight_grads.6 = (bf16[256,1024]{1,0:T(8,128)(2,1)}, bf16[256,1024]{1,0:T(8,128)(2,1)}, bf16[256,2048]{1,0:T(8,128)(2,1)}, bf16[256,2048]{1,0:T(8,128)(2,1)}, bf16[256,2048]{1,0:T(8,128)(2,1)}) custom-call(s32[1]{0:T(128)} %bitcast.place_ref, bf16[2048,1024]{1,0:T(8,128)(2,1)} %get-tuple-element.293.mn_ref.left_a, ...), custom_call_target="tpu_custom_call" | custom-call | flops 8589934592 | bytes 20971520 | tf_op jit(solution)/shard_map/weight_grads/pallas_call | solution.py:329
  201.1 35.9 %attention.3 = (bf16[2048,256]{1,0:T(8,128)(2,1)}, bf16[2048,768]{1,0:T(8,128)(2,1)}, f32[2,1,384]{2,1,0:T(1,128)}, bf16[1024,768]{1,0:T(8,128)(2,1)}, bf16[1024,256]{1,0:T(8,128)(2,1)}) custom-call(s32[1]{0:T(128)} %bitcast.place_ref, bf16[2048,1024]{1,0:T(8,128)(2,1)} %get-tuple-element.323.an_ref.left_a, ...), custom_call_target="tpu_custom_call" | custom-call | flops 21474836480 | bytes 37748736 | tf_op jit(solution)/shard_map/attention/pallas_call | solution.py:195
  237.7 2.8 fusion.5
  243.2 9.5 %weight_grads.7 = (bf16[256,512]{1,0:T(8,128)(2,1)}, bf16[256,512]{1,0:T(8,128)(2,1)}, bf16[256,1024]{1,0:T(8,128)(2,1)}, bf16[256,1024]{1,0:T(8,128)(2,1)}, bf16[256,1024]{1,0:T(8,128)(2,1)}) custom-call(s32[1]{0:T(128)} %bitcast.place_ref, bf16[2048,1024]{1,0:T(8,128)(2,1)} %get-tuple-element.323.an_ref.left_a, ...), custom_call_target="tpu_custom_call" | custom-call | flops 4294967296 | bytes 14680064 | tf_op jit(solution)/shard_map/weight_grads/pallas_call | solution.py:329
  255.0 14.6 %pull_back.2 = (bf16[1024,1024]{1,0:T(8,128)(2,1)}, f32[8,1024]{1,0:T(8,128)}) custom-call(bf16[2048,1024]{1,0:T(8,128)(2,1)} %get-tuple-element.275.right_a.refs_0_, bf16[1024,1024]{1,0:T(8,128)(2,1)} %get-tuple-element.353.refs_1_, bf16[2048,1024]{1,0:T(8,128)(2,1)} %get-tuple-element.386.right_a.refs_2_, bf16[1024,1024]{1,0:T(8,128)(2,1)} %get-tuple-element.355.refs_3_, ...), custom_call_target="tpu_custom_call" | custom-call | flops 7516192768 | bytes 23068672 | tf_op jit(solution)/shard_map/pull_back/pallas_call | solution.py:388
  277.6 2.7 collective-permute-start.47
  280.3 10.3 %branch_out.2 = bf16[1024,1024]{1,0:T(8,128)(2,1)} custom-call(bf16[2048,256]{1,0:T(8,128)(2,1)} %get-tuple-element.257.right_b.refs_0_, bf16[1024,256]{1,0:T(8,128)(2,1)} %get-tuple-element.371.refs_1_, bf16[2048,256]{1,0:T(8,128)(2,1)} %get-tuple-element.402.right_b.refs_2_, bf16[1024,256]{1,0:T(8,128)(2,1)} %get-tuple-element.373.refs_3_, ...), custom_call_target="tpu_custom_call" | custom-call | flops 5368709120 | bytes 12582912 | tf_op jit(solution)/shard_map/branch_out/pallas_call | solution.py:435
  295.1 4.3 %collective-permute-start.50 = (bf16[256,1024]{1,0:T(8,128)(2,1)}, bf16[256,1024]{1,0:T(8,128)(2,1)S(1)}, u32[]{:S(2)}, u32[]{:S(2)}) collective-permute-start(bf16[256,1024]{1,0:T(8,128)(2,1)} %add_convert_fusion), channel_id=1, source_target_pairs={{0,3},{1,0},{2,1},{3,2},{4,7},{5,4},{6,5},{7,6},{8,11},{9,8},{10,9... | collective-permute-start | bytes 1572872 | tf_op jit(solution)/shard_map/ppermute | solution.py:504
  301.4 14.8 %pull_back.3 = (f32[1024,1024]{1,0:T(8,128)}, f32[8,1024]{1,0:T(8,128)}) custom-call(bf16[2048,1024]{1,0:T(8,128)(2,1)} %get-tuple-element.275.right_a.refs_0_, bf16[1024,1024]{1,0:T(8,128)(2,1)} %get-tuple-element.353.refs_1_, bf16[2048,1024]{1,0:T(8,128)(2,1)} %get-tuple-element.386.right_a.refs_2_, bf16[1024,1024]{1,0:T(8,128)(2,1)} %get-tuple-element.355.refs_3_, ...), custom_call_target="tpu_custom_call" | custom-call | flops 7516192768 | bytes 23068672 | tf_op jit(solution)/shard_map/pull_back/pallas_call | solution.py:388
  317.7 5.1 %collective-permute-done.49 = bf16[256,512]{1,0:T(8,128)(2,1)S(1)} collective-permute-done((bf16[256,512]{1,0:T(8,128)(2,1)S(1)}, bf16[256,512]{1,0:T(8,128)(2,1)S(1)}, u32[]{:S(2)}, u32[]{:S(2)}) %collective-permute-start.49) | collective-permute-done | bytes 262176 | tf_op jit(solution)/shard_map/ppermute | solution.py:470
  326.6 14.5 %branch_out.3 = (bf16[1024,1024]{1,0:T(8,128)(2,1)}, f32[1024,1024]{1,0:T(8,128)}) custom-call(bf16[2048,256]{1,0:T(8,128)(2,1)} %get-tuple-element.257.right_b.refs_0_, bf16[1024,256]{1,0:T(8,128)(2,1)} %get-tuple-element.371.refs_1_, bf16[2048,256]{1,0:T(8,128)(2,1)} %get-tuple-element.402.right_b.refs_2_, bf16[1024,256]{1,0:T(8,128)(2,1)} %get-tuple-element.373.refs_3_, ...), custom_call_target="tpu_custom_call" | custom-call | flops 5368709120 | bytes 29360128 | tf_op jit(solution)/shard_map/branch_out/pallas_call | solution.py:435
  342.6 3.0 collective-permute-done.55
  355.2 3.5 collective-permute-done.59
  (359 shorter events, 98.9 us)
Async XLA Ops:
  5.6 24.7 %collective-permute-start.10 = (bf16[1024,1024]{1,0:T(8,128)(2,1)}, bf16[1024,1024]{1,0:T(8,128)(2,1)}, u32[]{:S(2)}, u32[]{:S(2)}) collective-permute-start(bf16[1024,1024]{1,0:T(8,128)(2,1)} %refs_8_.3), channel_id=1, source_target_pairs={{0,4},{4,0},{8,12},{12,8},{16,20},{20,16},{24,28},{28,24},{1,5},{5... | collective-permute-start | bytes 6291464 | tf_op jit(solution)/shard_map/ppermute | solution.py:464
  5.7 24.6 %collective-permute-start.11 = (bf16[1024,1024]{1,0:T(8,128)(2,1)S(1)}, bf16[1024,1024]{1,0:T(8,128)(2,1)}, u32[]{:S(2)}, u32[]{:S(2)}) collective-permute-start(bf16[1024,1024]{1,0:T(8,128)(2,1)S(1)} %copy-done.2), channel_id=1, source_target_pairs={{0,4},{4,0},{8,12},{12,8},{16,20},{20,16},{24,28},{28,24},{1,5},{5... | collective-permute-start | bytes 6291464 | tf_op jit(solution)/shard_map/ppermute | solution.py:464
  28.0 23.5 %collective-permute-start.5 = (bf16[256,1024]{1,0:T(8,128)(2,1)S(1)}, bf16[256,1024]{1,0:T(8,128)(2,1)S(1)}, u32[]{:S(2)}, u32[]{:S(2)}) collective-permute-start(bf16[256,1024]{1,0:T(8,128)(2,1)S(1)} %pad_maximum_fusion.2), channel_id=1, source_target_pairs={{0,3},{1,0},{2,1},{3,2},{4,7},{5,4},{6,5},{7,6},{8,11},{9,8},{10,9... | collective-permute-start | bytes 1572872 | tf_op jit(solution)/shard_map/ppermute | solution.py:504
  52.3 39.1 %collective-permute-start.14 = (bf16[256,2048]{1,0:T(8,128)(2,1)S(1)}, bf16[256,2048]{1,0:T(8,128)(2,1)}, u32[]{:S(2)}, u32[]{:S(2)}) collective-permute-start(bf16[256,2048]{1,0:T(8,128)(2,1)S(1)} %pad_maximum_fusion.refs_0_), channel_id=1, source_target_pairs={{0,8},{4,12},{8,0},{12,4},{16,24},{20,28},{24,16},{28,20},{1,9},{5... | collective-permute-start | bytes 3145736 | tf_op jit(solution)/shard_map/ppermute | solution.py:467
  52.9 38.5 %collective-permute-start.15 = (bf16[256,2048]{1,0:T(8,128)(2,1)S(1)}, bf16[256,2048]{1,0:T(8,128)(2,1)}, u32[]{:S(2)}, u32[]{:S(2)}) collective-permute-start(bf16[256,2048]{1,0:T(8,128)(2,1)S(1)} %pad_maximum_fusion.refs_0_), channel_id=1, source_target_pairs={{0,16},{4,20},{8,24},{12,28},{16,0},{20,4},{24,8},{28,12},{1,17},{... | collective-permute-start | bytes 3145736 | tf_op jit(solution)/shard_map/ppermute | solution.py:467
  53.6 37.8 %collective-permute-start.16 = (bf16[256,1024]{1,0:T(8,128)(2,1)S(1)}, bf16[256,1024]{1,0:T(8,128)(2,1)}, u32[]{:S(2)}, u32[]{:S(2)}) collective-permute-start(bf16[256,1024]{1,0:T(8,128)(2,1)S(1)} %collective-permute-done.4), channel_id=1, source_target_pairs={{0,1},{1,2},{2,3},{3,0},{4,5},{5,6},{6,7},{7,4},{8,9},{9,10},{10,1... | collective-permute-start | bytes 1572872 | tf_op jit(solution)/shard_map/ppermute | solution.py:470
  98.5 34.6 %collective-permute-start.17 = (bf16[256,2048]{1,0:T(8,128)(2,1)S(1)}, bf16[256,2048]{1,0:T(8,128)(2,1)S(1)}, u32[]{:S(2)}, u32[]{:S(2)}) collective-permute-start(bf16[256,2048]{1,0:T(8,128)(2,1)S(1)} %pad_maximum_fusion.1.refs_0_), channel_id=1, source_target_pairs={{0,8},{4,12},{8,0},{12,4},{16,24},{20,28},{24,16},{28,20},{1,9},{5... | collective-permute-start | bytes 3145736 | tf_op jit(solution)/shard_map/ppermute | solution.py:467
  99.4 34.1 %collective-permute-start.18 = (bf16[256,2048]{1,0:T(8,128)(2,1)S(1)}, bf16[256,2048]{1,0:T(8,128)(2,1)S(1)}, u32[]{:S(2)}, u32[]{:S(2)}) collective-permute-start(bf16[256,2048]{1,0:T(8,128)(2,1)S(1)} %pad_maximum_fusion.1.refs_0_), channel_id=1, source_target_pairs={{0,16},{4,20},{8,24},{12,28},{16,0},{20,4},{24,8},{28,12},{1,17},{... | collective-permute-start | bytes 3145736 | tf_op jit(solution)/shard_map/ppermute | solution.py:467
  100.1 31.7 %collective-permute-start.19 = (bf16[256,512]{1,0:T(8,128)(2,1)S(1)}, bf16[256,512]{1,0:T(8,128)(2,1)S(1)}, u32[]{:S(2)}, u32[]{:S(2)}) collective-permute-start(bf16[256,512]{1,0:T(8,128)(2,1)S(1)} %copy-done.50), channel_id=1, source_target_pairs={{0,1},{1,2},{2,3},{3,0},{4,5},{5,6},{6,7},{7,4},{8,9},{9,10},{10,1... | collective-permute-start | bytes 786440 | tf_op jit(solution)/shard_map/ppermute | solution.py:470
  110.2 22.9 %collective-permute-start.20 = (bf16[256,512]{1,0:T(8,128)(2,1)S(1)}, bf16[256,512]{1,0:T(8,128)(2,1)S(1)}, u32[]{:S(2)}, u32[]{:S(2)}) collective-permute-start(bf16[256,512]{1,0:T(8,128)(2,1)S(1)} %copy-done.22), channel_id=1, source_target_pairs={{0,3},{1,0},{2,1},{3,2},{4,7},{5,4},{6,5},{7,6},{8,11},{9,8},{10,9... | collective-permute-start | bytes 786440 | tf_op jit(solution)/shard_map/ppermute | solution.py:504
  113.8 36.4 %collective-permute-start.25 = (bf16[256,512]{1,0:T(8,128)(2,1)}, bf16[256,512]{1,0:T(8,128)(2,1)S(1)}, u32[]{:S(2)}, u32[]{:S(2)}) collective-permute-start(bf16[256,512]{1,0:T(8,128)(2,1)} %get-tuple-element.273), channel_id=1, source_target_pairs={{0,16},{4,20},{8,24},{12,28},{16,0},{20,4},{24,8},{28,12},{1,17},{... | collective-permute-start | bytes 786440 | tf_op jit(solution)/shard_map/ppermute | solution.py:467
  151.6 21.7 %collective-permute-start.28 = (bf16[256,1024]{1,0:T(8,128)(2,1)S(1)}, bf16[256,1024]{1,0:T(8,128)(2,1)S(1)}, u32[]{:S(2)}, u32[]{:S(2)}) collective-permute-start(bf16[256,1024]{1,0:T(8,128)(2,1)S(1)} %pad_maximum_fusion.3.refs_0_), channel_id=1, source_target_pairs={{0,16},{4,20},{8,24},{12,28},{16,0},{20,4},{24,8},{28,12},{1,17},{... | collective-permute-start | bytes 1572872 | tf_op jit(solution)/shard_map/ppermute | solution.py:467
  153.2 24.5 %collective-permute-start.30 = (bf16[256,1024]{1,0:T(8,128)(2,1)S(1)}, bf16[256,1024]{1,0:T(8,128)(2,1)S(1)}, u32[]{:S(2)}, u32[]{:S(2)}) collective-permute-start(bf16[256,1024]{1,0:T(8,128)(2,1)S(1)} %fusion.7), channel_id=1, source_target_pairs={{0,16},{4,20},{8,24},{12,28},{16,0},{20,4},{24,8},{28,12},{1,17},{... | collective-permute-start | bytes 1572872 | tf_op jit(solution)/shard_map/ppermute | solution.py:467
  154.6 39.7 %collective-permute-start.33 = (bf16[256,1024]{1,0:T(8,128)(2,1)}, bf16[256,1024]{1,0:T(8,128)(2,1)S(1)}, u32[]{:S(2)}, u32[]{:S(2)}) collective-permute-start(bf16[256,1024]{1,0:T(8,128)(2,1)} %get-tuple-element.302), channel_id=1, source_target_pairs={{0,16},{4,20},{8,24},{12,28},{16,0},{20,4},{24,8},{28,12},{1,17},{... | collective-permute-start | bytes 1572872 | tf_op jit(solution)/shard_map/ppermute | solution.py:467
  171.9 22.5 %collective-permute-start.34 = (bf16[256,1024]{1,0:T(8,128)(2,1)S(1)}, bf16[256,1024]{1,0:T(8,128)(2,1)S(1)}, u32[]{:S(2)}, u32[]{:S(2)}) collective-permute-start(bf16[256,1024]{1,0:T(8,128)(2,1)S(1)} %copy-done.42), channel_id=1, source_target_pairs={{0,8},{4,12},{8,0},{12,4},{16,24},{20,28},{24,16},{28,20},{1,9},{5... | collective-permute-start | bytes 1572872 | tf_op jit(solution)/shard_map/ppermute | solution.py:467
  197.0 40.0 %collective-permute-start.35 = (bf16[256,2048]{1,0:T(8,128)(2,1)S(1)}, bf16[256,2048]{1,0:T(8,128)(2,1)S(1)}, u32[]{:S(2)}, u32[]{:S(2)}) collective-permute-start(bf16[256,2048]{1,0:T(8,128)(2,1)S(1)} %fusion.2), channel_id=1, source_target_pairs={{0,8},{4,12},{8,0},{12,4},{16,24},{20,28},{24,16},{28,20},{1,9},{5... | collective-permute-start | bytes 3145736 | tf_op jit(solution)/shard_map/ppermute | solution.py:467
  198.4 38.6 %collective-permute-start.36 = (bf16[256,2048]{1,0:T(8,128)(2,1)}, bf16[256,2048]{1,0:T(8,128)(2,1)S(1)}, u32[]{:S(2)}, u32[]{:S(2)}) collective-permute-start(bf16[256,2048]{1,0:T(8,128)(2,1)} %fusion.3), channel_id=1, source_target_pairs={{0,16},{4,20},{8,24},{12,28},{16,0},{20,4},{24,8},{28,12},{1,17},{... | collective-permute-start | bytes 3145736 | tf_op jit(solution)/shard_map/ppermute | solution.py:467
  199.5 37.5 %collective-permute-start.37 = (bf16[256,1024]{1,0:T(8,128)(2,1)S(1)}, bf16[256,1024]{1,0:T(8,128)(2,1)S(1)}, u32[]{:S(2)}, u32[]{:S(2)}) collective-permute-start(bf16[256,1024]{1,0:T(8,128)(2,1)S(1)} %copy-done.45), channel_id=1, source_target_pairs={{0,16},{4,20},{8,24},{12,28},{16,0},{20,4},{24,8},{28,12},{1,17},{... | collective-permute-start | bytes 1572872 | tf_op jit(solution)/shard_map/ppermute | solution.py:467
  200.4 36.6 %collective-permute-start.38 = (bf16[256,1024]{1,0:T(8,128)(2,1)S(1)}, bf16[256,1024]{1,0:T(8,128)(2,1)S(1)}, u32[]{:S(2)}, u32[]{:S(2)}) collective-permute-start(bf16[256,1024]{1,0:T(8,128)(2,1)S(1)} %copy-done.43), channel_id=1, source_target_pairs={{0,8},{4,12},{8,0},{12,4},{16,24},{20,28},{24,16},{28,20},{1,9},{5... | collective-permute-start | bytes 1572872 | tf_op jit(solution)/shard_map/ppermute | solution.py:467
  240.7 28.9 %collective-permute-start.39 = (bf16[256,2048]{1,0:T(8,128)(2,1)S(1)}, bf16[256,2048]{1,0:T(8,128)(2,1)S(1)}, u32[]{:S(2)}, u32[]{:S(2)}) collective-permute-start(bf16[256,2048]{1,0:T(8,128)(2,1)S(1)} %fusion.4), channel_id=1, source_target_pairs={{0,8},{4,12},{8,0},{12,4},{16,24},{20,28},{24,16},{28,20},{1,9},{5... | collective-permute-start | bytes 3145736 | tf_op jit(solution)/shard_map/ppermute | solution.py:467
  242.1 27.5 %collective-permute-start.40 = (bf16[256,2048]{1,0:T(8,128)(2,1)}, bf16[256,2048]{1,0:T(8,128)(2,1)S(1)}, u32[]{:S(2)}, u32[]{:S(2)}) collective-permute-start(bf16[256,2048]{1,0:T(8,128)(2,1)} %fusion.5), channel_id=1, source_target_pairs={{0,16},{4,20},{8,24},{12,28},{16,0},{20,4},{24,8},{28,12},{1,17},{... | collective-permute-start | bytes 3145736 | tf_op jit(solution)/shard_map/ppermute | solution.py:467
  293.6 29.2 %collective-permute-start.51 = (bf16[1024,1024]{1,0:T(8,128)(2,1)}, bf16[1024,1024]{1,0:T(8,128)(2,1)}, u32[]{:S(2)}, u32[]{:S(2)}) collective-permute-start(bf16[1024,1024]{1,0:T(8,128)(2,1)} %branch_out.2), channel_id=1, source_target_pairs={{0,4},{4,0},{8,12},{12,8},{16,20},{20,16},{24,28},{28,24},{1,5},{5... | collective-permute-start | bytes 6291464 | tf_op jit(solution)/shard_map/ppermute | solution.py:464
  295.1 27.8 %collective-permute-start.50 = (bf16[256,1024]{1,0:T(8,128)(2,1)}, bf16[256,1024]{1,0:T(8,128)(2,1)S(1)}, u32[]{:S(2)}, u32[]{:S(2)}) collective-permute-start(bf16[256,1024]{1,0:T(8,128)(2,1)} %add_convert_fusion), channel_id=1, source_target_pairs={{0,3},{1,0},{2,1},{3,2},{4,7},{5,4},{6,5},{7,6},{8,11},{9,8},{10,9... | collective-permute-start | bytes 1572872 | tf_op jit(solution)/shard_map/ppermute | solution.py:504
  299.6 23.2 %collective-permute-start.49 = (bf16[256,512]{1,0:T(8,128)(2,1)S(1)}, bf16[256,512]{1,0:T(8,128)(2,1)S(1)}, u32[]{:S(2)}, u32[]{:S(2)}) collective-permute-start(bf16[256,512]{1,0:T(8,128)(2,1)S(1)} %get-tuple-element.383), channel_id=1, source_target_pairs={{0,1},{1,2},{2,3},{3,0},{4,5},{5,6},{6,7},{7,4},{8,9},{9,10},{10,1... | collective-permute-start | bytes 786440 | tf_op jit(solution)/shard_map/ppermute | solution.py:470
  (98 other events, 1086.3 us)

commit v6 on v5

--- a/solution.py
+++ b/solution.py
@@ -55,7 +55,7 @@
 
 def prepare(x_own, x_other, dy_own, dy_other, gains):
     rows, depth = x_own.shape
-    br = min(512, rows)
+    br = min(1024, rows)
     half = rows // br
     own = pl.BlockSpec((br, depth), lambda i: (jnp.minimum(i, half - 1), 0))
     other = pl.BlockSpec((br, depth), lambda i: (jnp.maximum(i - half, 0), 0))
@@ -322,7 +322,7 @@
 
 def weight_grads(place, places, left_a, right_a, left_b, right_b, count):
     rows, depth = left_a.shape
-    br = min(512, rows)
+    br = min(512 if right_a.shape[1] == right_b.shape[1] else 1024, rows)
     wa, wb = right_a.shape[1], right_b.shape[1]
     block = lambda v: pl.BlockSpec((br, v.shape[1]), lambda i, p: (i, 0))
     keys, shapes = block_shapes(places, depth, wa, wb, count)

time: 369 us -> 370 us (level)
  no operation moved by 1% of the time
where the time goes in v6:
time: 370 us; the launch traced here: 363 us
  Pallas kernels  217 us (59%)
  starting transfers between devices  66.6 us (18%)
  waiting for transfers between devices  37.6 us (10%)
  other arithmetic  22.4 us (6%)
  local copies, waits for them, and re-layouts  17.5 us (5%)
    pallas_call x2, Pallas kernels, attention(): pl.pallas_call(partial(attention_kernel, keys=[v[1:] for v in pieces], bq...  71.7 us
    pallas_call x4, Pallas kernels, weight_grads(): pl.pallas_call(partial(grads_kernel, count=count, keys=keys), grid_spec=p...  47.5 us
    ppermute x34, starting transfers between devices, hop(): lax.ppermute(value, 'fsdp', [(i, i ^ 2 * bit) for i in range(self.fsdp)])  37.6 us
    pallas_call x2, Pallas kernels, mlp(): pl.pallas_call(partial(mlp_kernel, keys=[v[1:] for v in pieces], count=co...  33.1 us
    pallas_call x2, Pallas kernels, pull_back(): pl.pallas_call(pull_kernel, grid=(rows // br,), in_specs=specs + [tile, w...  29.6 us
    pallas_call x2, Pallas kernels, branch_out(): pl.pallas_call(partial(out_kernel, own=own), grid=(rows // br,), in_specs...  24.5 us
    ppermute x6, starting transfers between devices, back(): lax.ppermute(value, 'tp', [(i, (i - 1) % self.tp) for i in range(self.tp)])  14.2 us
    ppermute x6, waiting for transfers between devices, back(): lax.ppermute(value, 'tp', [(i, (i - 1) % self.tp) for i in range(self.tp)])  10.5 us
  transfers between devices with their start and end apart: 61, of which 12 were waited for; matrix products, arithmetic and copies ran while one was open for 4% of the time, Pallas kernels for 60%

profile of v6, /device:TPU:0, one launch (start us, length us, event | category | flops | bytes accessed | tf_op | source)
XLA Modules:
  0.0 363.3 jit_solution(15136973374398024541)
XLA Ops:
  8.3 2.7 collective-permute-start.2
  15.1 4.8 %collective-permute-done.2.refs_4_ = bf16[256,512]{1,0:T(8,128)(2,1)S(1)} collective-permute-done((bf16[256,512]{1,0:T(8,128)(2,1)S(1)}, bf16[256,512]{1,0:T(8,128)(2,1)S(1)}, u32[]{:S(2)}, u32[]{:S(2)}) %collective-permute-start.2) | collective-permute-done | bytes 262176 | tf_op jit(solution)/shard_map/ppermute | solution.py:470
  32.9 10.2 %prepare.1 = (bf16[2048,1024]{1,0:T(8,128)(2,1)}, bf16[2048,1024]{1,0:T(8,128)(2,1)}, bf16[2048,1024]{1,0:T(8,128)(2,1)}) custom-call(bf16[1024,1024]{1,0:T(8,128)(2,1)} %refs_8_.3, bf16[1024,1024]{1,0:T(8,128)(2,1)} %collective-permute-done.10.x_other.refs_8_, bf16[1024,1024]{1,0:T(8,128)(2,1)} %refs_11_.1, ...), custom_call_target="tpu_custom_call" | custom-call | flops 41943040 | bytes 33554432 | tf_op jit(solution)/shard_map/prepare/pallas_call | solution.py:63
  43.2 8.3 %collective-permute-done.5 = bf16[256,1024]{1,0:T(8,128)(2,1)S(1)} collective-permute-done((bf16[256,1024]{1,0:T(8,128)(2,1)S(1)}, bf16[256,1024]{1,0:T(8,128)(2,1)S(1)}, u32[]{:S(2)}, u32[]{:S(2)}) %collective-permute-start.5) | collective-permute-done | bytes 524320 | tf_op jit(solution)/shard_map/ppermute | solution.py:504
  55.5 35.8 %attention.2 = (bf16[2048,256]{1,0:T(8,128)(2,1)}, bf16[2048,768]{1,0:T(8,128)(2,1)}, f32[2,1,384]{2,1,0:T(1,128)}, bf16[1024,768]{1,0:T(8,128)(2,1)}, bf16[1024,256]{1,0:T(8,128)(2,1)}) custom-call(s32[1]{0:T(128)} %bitcast.place_ref, bf16[2048,1024]{1,0:T(8,128)(2,1)} %get-tuple-element.323.an_ref.left_a, ...), custom_call_target="tpu_custom_call" | custom-call | flops 21474836480 | bytes 37748736 | tf_op jit(solution)/shard_map/attention/pallas_call | solution.py:195
  100.7 9.2 %weight_grads.4 = (bf16[256,512]{1,0:T(8,128)(2,1)}, bf16[256,512]{1,0:T(8,128)(2,1)}, bf16[256,1024]{1,0:T(8,128)(2,1)}, bf16[256,1024]{1,0:T(8,128)(2,1)}, bf16[256,1024]{1,0:T(8,128)(2,1)}) custom-call(s32[1]{0:T(128)} %bitcast.place_ref, bf16[2048,1024]{1,0:T(8,128)(2,1)} %get-tuple-element.323.an_ref.left_a, ...), custom_call_target="tpu_custom_call" | custom-call | flops 4294967296 | bytes 14680064 | tf_op jit(solution)/shard_map/weight_grads/pallas_call | solution.py:329
  110.0 3.7 %collective-permute-start.20 = (bf16[256,512]{1,0:T(8,128)(2,1)S(1)}, bf16[256,512]{1,0:T(8,128)(2,1)S(1)}, u32[]{:S(2)}, u32[]{:S(2)}) collective-permute-start(bf16[256,512]{1,0:T(8,128)(2,1)S(1)} %copy-done.22), channel_id=1, source_target_pairs={{0,3},{1,0},{2,1},{3,2},{4,7},{5,4},{6,5},{7,6},{8,11},{9,8},{10,9... | collective-permute-start | bytes 786440 | tf_op jit(solution)/shard_map/ppermute | solution.py:504
  115.1 16.5 %mlp.2 = (bf16[2048,1024]{1,0:T(8,128)(2,1)}, bf16[2048,1024]{1,0:T(8,128)(2,1)}, f32[1,1024]{1,0:T(1,128)}, bf16[1024,1024]{1,0:T(8,128)(2,1)}, bf16[1024,1024]{1,0:T(8,128)(2,1)}) custom-call(s32[1]{0:T(128)} %bitcast.place_ref, bf16[2048,1024]{1,0:T(8,128)(2,1)} %get-tuple-element.293.mn_ref.left_a, bf16[2048,1024]{1,0:T(8,128)(2,1)} %get-tuple-element.238.dy_ref.left_b, ...), custom_call_target="tpu_custom_call" | custom-call | flops 8589934592 | bytes 25165824 | tf_op jit(solution)/shard_map/mlp/pallas_call | solution.py:265
  135.7 14.4 %weight_grads.5 = (bf16[256,1024]{1,0:T(8,128)(2,1)}, bf16[256,1024]{1,0:T(8,128)(2,1)}, bf16[256,2048]{1,0:T(8,128)(2,1)}, bf16[256,2048]{1,0:T(8,128)(2,1)}, bf16[256,2048]{1,0:T(8,128)(2,1)}) custom-call(s32[1]{0:T(128)} %bitcast.place_ref, bf16[2048,1024]{1,0:T(8,128)(2,1)} %get-tuple-element.293.mn_ref.left_a, ...), custom_call_target="tpu_custom_call" | custom-call | flops 8589934592 | bytes 20971520 | tf_op jit(solution)/shard_map/weight_grads/pallas_call | solution.py:329
  155.2 16.6 %mlp.3 = (bf16[2048,1024]{1,0:T(8,128)(2,1)}, bf16[2048,1024]{1,0:T(8,128)(2,1)}, f32[1,1024]{1,0:T(1,128)}, bf16[1024,1024]{1,0:T(8,128)(2,1)}, bf16[1024,1024]{1,0:T(8,128)(2,1)}) custom-call(s32[1]{0:T(128)} %bitcast.place_ref, bf16[2048,1024]{1,0:T(8,128)(2,1)} %get-tuple-element.293.mn_ref.left_a, bf16[2048,1024]{1,0:T(8,128)(2,1)} %get-tuple-element.238.dy_ref.left_b, ...), custom_call_target="tpu_custom_call" | custom-call | flops 8589934592 | bytes 25165824 | tf_op jit(solution)/shard_map/mlp/pallas_call | solution.py:265
  173.3 4.4 %collective-permute-done.30 = bf16[256,1024]{1,0:T(8,128)(2,1)S(1)} collective-permute-done((bf16[256,1024]{1,0:T(8,128)(2,1)S(1)}, bf16[256,1024]{1,0:T(8,128)(2,1)S(1)}, u32[]{:S(2)}, u32[]{:S(2)}) %collective-permute-start.30) | collective-permute-done | bytes 524320 | tf_op jit(solution)/shard_map/ppermute | solution.py:467
  179.4 14.5 %weight_grads.6 = (bf16[256,1024]{1,0:T(8,128)(2,1)}, bf16[256,1024]{1,0:T(8,128)(2,1)}, bf16[256,2048]{1,0:T(8,128)(2,1)}, bf16[256,2048]{1,0:T(8,128)(2,1)}, bf16[256,2048]{1,0:T(8,128)(2,1)}) custom-call(s32[1]{0:T(128)} %bitcast.place_ref, bf16[2048,1024]{1,0:T(8,128)(2,1)} %get-tuple-element.293.mn_ref.left_a, ...), custom_call_target="tpu_custom_call" | custom-call | flops 8589934592 | bytes 20971520 | tf_op jit(solution)/shard_map/weight_grads/pallas_call | solution.py:329
  201.1 35.9 %attention.3 = (bf16[2048,256]{1,0:T(8,128)(2,1)}, bf16[2048,768]{1,0:T(8,128)(2,1)}, f32[2,1,384]{2,1,0:T(1,128)}, bf16[1024,768]{1,0:T(8,128)(2,1)}, bf16[1024,256]{1,0:T(8,128)(2,1)}) custom-call(s32[1]{0:T(128)} %bitcast.place_ref, bf16[2048,1024]{1,0:T(8,128)(2,1)} %get-tuple-element.323.an_ref.left_a, ...), custom_call_target="tpu_custom_call" | custom-call | flops 21474836480 | bytes 37748736 | tf_op jit(solution)/shard_map/attention/pallas_call | solution.py:195
  237.7 2.8 fusion.5
  243.2 9.3 %weight_grads.7 = (bf16[256,512]{1,0:T(8,128)(2,1)}, bf16[256,512]{1,0:T(8,128)(2,1)}, bf16[256,1024]{1,0:T(8,128)(2,1)}, bf16[256,1024]{1,0:T(8,128)(2,1)}, bf16[256,1024]{1,0:T(8,128)(2,1)}) custom-call(s32[1]{0:T(128)} %bitcast.place_ref, bf16[2048,1024]{1,0:T(8,128)(2,1)} %get-tuple-element.323.an_ref.left_a, ...), custom_call_target="tpu_custom_call" | custom-call | flops 4294967296 | bytes 14680064 | tf_op jit(solution)/shard_map/weight_grads/pallas_call | solution.py:329
  254.8 14.6 %pull_back.2 = (bf16[1024,1024]{1,0:T(8,128)(2,1)}, f32[8,1024]{1,0:T(8,128)}) custom-call(bf16[2048,1024]{1,0:T(8,128)(2,1)} %get-tuple-element.275.right_a.refs_0_, bf16[1024,1024]{1,0:T(8,128)(2,1)} %get-tuple-element.353.refs_1_, bf16[2048,1024]{1,0:T(8,128)(2,1)} %get-tuple-element.386.right_a.refs_2_, bf16[1024,1024]{1,0:T(8,128)(2,1)} %get-tuple-element.355.refs_3_, ...), custom_call_target="tpu_custom_call" | custom-call | flops 7516192768 | bytes 23068672 | tf_op jit(solution)/shard_map/pull_back/pallas_call | solution.py:388
  277.4 2.7 collective-permute-start.47
  280.1 10.3 %branch_out.2 = bf16[1024,1024]{1,0:T(8,128)(2,1)} custom-call(bf16[2048,256]{1,0:T(8,128)(2,1)} %get-tuple-element.257.right_b.refs_0_, bf16[1024,256]{1,0:T(8,128)(2,1)} %get-tuple-element.371.refs_1_, bf16[2048,256]{1,0:T(8,128)(2,1)} %get-tuple-element.402.right_b.refs_2_, bf16[1024,256]{1,0:T(8,128)(2,1)} %get-tuple-element.373.refs_3_, ...), custom_call_target="tpu_custom_call" | custom-call | flops 5368709120 | bytes 12582912 | tf_op jit(solution)/shard_map/branch_out/pallas_call | solution.py:435
  294.9 4.3 %collective-permute-start.50 = (bf16[256,1024]{1,0:T(8,128)(2,1)}, bf16[256,1024]{1,0:T(8,128)(2,1)S(1)}, u32[]{:S(2)}, u32[]{:S(2)}) collective-permute-start(bf16[256,1024]{1,0:T(8,128)(2,1)} %add_convert_fusion), channel_id=1, source_target_pairs={{0,3},{1,0},{2,1},{3,2},{4,7},{5,4},{6,5},{7,6},{8,11},{9,8},{10,9... | collective-permute-start | bytes 1572872 | tf_op jit(solution)/shard_map/ppermute | solution.py:504
  301.2 15.1 %pull_back.3 = (f32[1024,1024]{1,0:T(8,128)}, f32[8,1024]{1,0:T(8,128)}) custom-call(bf16[2048,1024]{1,0:T(8,128)(2,1)} %get-tuple-element.275.right_a.refs_0_, bf16[1024,1024]{1,0:T(8,128)(2,1)} %get-tuple-element.353.refs_1_, bf16[2048,1024]{1,0:T(8,128)(2,1)} %get-tuple-element.386.right_a.refs_2_, bf16[1024,1024]{1,0:T(8,128)(2,1)} %get-tuple-element.355.refs_3_, ...), custom_call_target="tpu_custom_call" | custom-call | flops 7516192768 | bytes 23068672 | tf_op jit(solution)/shard_map/pull_back/pallas_call | solution.py:388
  317.5 5.1 %collective-permute-done.49 = bf16[256,512]{1,0:T(8,128)(2,1)S(1)} collective-permute-done((bf16[256,512]{1,0:T(8,128)(2,1)S(1)}, bf16[256,512]{1,0:T(8,128)(2,1)S(1)}, u32[]{:S(2)}, u32[]{:S(2)}) %collective-permute-start.49) | collective-permute-done | bytes 262176 | tf_op jit(solution)/shard_map/ppermute | solution.py:470
  326.5 14.2 %branch_out.3 = (bf16[1024,1024]{1,0:T(8,128)(2,1)}, f32[1024,1024]{1,0:T(8,128)}) custom-call(bf16[2048,256]{1,0:T(8,128)(2,1)} %get-tuple-element.257.right_b.refs_0_, bf16[1024,256]{1,0:T(8,128)(2,1)} %get-tuple-element.371.refs_1_, bf16[2048,256]{1,0:T(8,128)(2,1)} %get-tuple-element.402.right_b.refs_2_, bf16[1024,256]{1,0:T(8,128)(2,1)} %get-tuple-element.373.refs_3_, ...), custom_call_target="tpu_custom_call" | custom-call | flops 5368709120 | bytes 29360128 | tf_op jit(solution)/shard_map/branch_out/pallas_call | solution.py:435
  342.2 3.0 collective-permute-done.55
  354.8 3.5 collective-permute-done.59
  (359 shorter events, 98.8 us)
Async XLA Ops:
  5.6 24.7 %collective-permute-start.10 = (bf16[1024,1024]{1,0:T(8,128)(2,1)}, bf16[1024,1024]{1,0:T(8,128)(2,1)}, u32[]{:S(2)}, u32[]{:S(2)}) collective-permute-start(bf16[1024,1024]{1,0:T(8,128)(2,1)} %refs_8_.3), channel_id=1, source_target_pairs={{0,4},{4,0},{8,12},{12,8},{16,20},{20,16},{24,28},{28,24},{1,5},{5... | collective-permute-start | bytes 6291464 | tf_op jit(solution)/shard_map/ppermute | solution.py:464
  5.7 24.6 %collective-permute-start.11 = (bf16[1024,1024]{1,0:T(8,128)(2,1)S(1)}, bf16[1024,1024]{1,0:T(8,128)(2,1)}, u32[]{:S(2)}, u32[]{:S(2)}) collective-permute-start(bf16[1024,1024]{1,0:T(8,128)(2,1)S(1)} %copy-done.2), channel_id=1, source_target_pairs={{0,4},{4,0},{8,12},{12,8},{16,20},{20,16},{24,28},{28,24},{1,5},{5... | collective-permute-start | bytes 6291464 | tf_op jit(solution)/shard_map/ppermute | solution.py:464
  28.0 23.5 %collective-permute-start.5 = (bf16[256,1024]{1,0:T(8,128)(2,1)S(1)}, bf16[256,1024]{1,0:T(8,128)(2,1)S(1)}, u32[]{:S(2)}, u32[]{:S(2)}) collective-permute-start(bf16[256,1024]{1,0:T(8,128)(2,1)S(1)} %pad_maximum_fusion.2), channel_id=1, source_target_pairs={{0,3},{1,0},{2,1},{3,2},{4,7},{5,4},{6,5},{7,6},{8,11},{9,8},{10,9... | collective-permute-start | bytes 1572872 | tf_op jit(solution)/shard_map/ppermute | solution.py:504
  52.3 39.1 %collective-permute-start.14 = (bf16[256,2048]{1,0:T(8,128)(2,1)S(1)}, bf16[256,2048]{1,0:T(8,128)(2,1)}, u32[]{:S(2)}, u32[]{:S(2)}) collective-permute-start(bf16[256,2048]{1,0:T(8,128)(2,1)S(1)} %pad_maximum_fusion.refs_0_), channel_id=1, source_target_pairs={{0,8},{4,12},{8,0},{12,4},{16,24},{20,28},{24,16},{28,20},{1,9},{5... | collective-permute-start | bytes 3145736 | tf_op jit(solution)/shard_map/ppermute | solution.py:467
  52.9 38.5 %collective-permute-start.15 = (bf16[256,2048]{1,0:T(8,128)(2,1)S(1)}, bf16[256,2048]{1,0:T(8,128)(2,1)}, u32[]{:S(2)}, u32[]{:S(2)}) collective-permute-start(bf16[256,2048]{1,0:T(8,128)(2,1)S(1)} %pad_maximum_fusion.refs_0_), channel_id=1, source_target_pairs={{0,16},{4,20},{8,24},{12,28},{16,0},{20,4},{24,8},{28,12},{1,17},{... | collective-permute-start | bytes 3145736 | tf_op jit(solution)/shard_map/ppermute | solution.py:467
  53.6 37.8 %collective-permute-start.16 = (bf16[256,1024]{1,0:T(8,128)(2,1)S(1)}, bf16[256,1024]{1,0:T(8,128)(2,1)}, u32[]{:S(2)}, u32[]{:S(2)}) collective-permute-start(bf16[256,1024]{1,0:T(8,128)(2,1)S(1)} %collective-permute-done.4), channel_id=1, source_target_pairs={{0,1},{1,2},{2,3},{3,0},{4,5},{5,6},{6,7},{7,4},{8,9},{9,10},{10,1... | collective-permute-start | bytes 1572872 | tf_op jit(solution)/shard_map/ppermute | solution.py:470
  98.5 34.6 %collective-permute-start.17 = (bf16[256,2048]{1,0:T(8,128)(2,1)S(1)}, bf16[256,2048]{1,0:T(8,128)(2,1)S(1)}, u32[]{:S(2)}, u32[]{:S(2)}) collective-permute-start(bf16[256,2048]{1,0:T(8,128)(2,1)S(1)} %pad_maximum_fusion.1.refs_0_), channel_id=1, source_target_pairs={{0,8},{4,12},{8,0},{12,4},{16,24},{20,28},{24,16},{28,20},{1,9},{5... | collective-permute-start | bytes 3145736 | tf_op jit(solution)/shard_map/ppermute | solution.py:467
  99.4 34.1 %collective-permute-start.18 = (bf16[256,2048]{1,0:T(8,128)(2,1)S(1)}, bf16[256,2048]{1,0:T(8,128)(2,1)S(1)}, u32[]{:S(2)}, u32[]{:S(2)}) collective-permute-start(bf16[256,2048]{1,0:T(8,128)(2,1)S(1)} %pad_maximum_fusion.1.refs_0_), channel_id=1, source_target_pairs={{0,16},{4,20},{8,24},{12,28},{16,0},{20,4},{24,8},{28,12},{1,17},{... | collective-permute-start | bytes 3145736 | tf_op jit(solution)/shard_map/ppermute | solution.py:467
  100.1 31.5 %collective-permute-start.19 = (bf16[256,512]{1,0:T(8,128)(2,1)S(1)}, bf16[256,512]{1,0:T(8,128)(2,1)S(1)}, u32[]{:S(2)}, u32[]{:S(2)}) collective-permute-start(bf16[256,512]{1,0:T(8,128)(2,1)S(1)} %copy-done.50), channel_id=1, source_target_pairs={{0,1},{1,2},{2,3},{3,0},{4,5},{5,6},{6,7},{7,4},{8,9},{9,10},{10,1... | collective-permute-start | bytes 786440 | tf_op jit(solution)/shard_map/ppermute | solution.py:470
  110.0 23.0 %collective-permute-start.20 = (bf16[256,512]{1,0:T(8,128)(2,1)S(1)}, bf16[256,512]{1,0:T(8,128)(2,1)S(1)}, u32[]{:S(2)}, u32[]{:S(2)}) collective-permute-start(bf16[256,512]{1,0:T(8,128)(2,1)S(1)} %copy-done.22), channel_id=1, source_target_pairs={{0,3},{1,0},{2,1},{3,2},{4,7},{5,4},{6,5},{7,6},{8,11},{9,8},{10,9... | collective-permute-start | bytes 786440 | tf_op jit(solution)/shard_map/ppermute | solution.py:504
  113.7 36.5 %collective-permute-start.25 = (bf16[256,512]{1,0:T(8,128)(2,1)}, bf16[256,512]{1,0:T(8,128)(2,1)S(1)}, u32[]{:S(2)}, u32[]{:S(2)}) collective-permute-start(bf16[256,512]{1,0:T(8,128)(2,1)} %get-tuple-element.273), channel_id=1, source_target_pairs={{0,16},{4,20},{8,24},{12,28},{16,0},{20,4},{24,8},{28,12},{1,17},{... | collective-permute-start | bytes 786440 | tf_op jit(solution)/shard_map/ppermute | solution.py:467
  151.6 21.7 %collective-permute-start.28 = (bf16[256,1024]{1,0:T(8,128)(2,1)S(1)}, bf16[256,1024]{1,0:T(8,128)(2,1)S(1)}, u32[]{:S(2)}, u32[]{:S(2)}) collective-permute-start(bf16[256,1024]{1,0:T(8,128)(2,1)S(1)} %pad_maximum_fusion.3.refs_0_), channel_id=1, source_target_pairs={{0,16},{4,20},{8,24},{12,28},{16,0},{20,4},{24,8},{28,12},{1,17},{... | collective-permute-start | bytes 1572872 | tf_op jit(solution)/shard_map/ppermute | solution.py:467
  153.2 24.5 %collective-permute-start.30 = (bf16[256,1024]{1,0:T(8,128)(2,1)S(1)}, bf16[256,1024]{1,0:T(8,128)(2,1)S(1)}, u32[]{:S(2)}, u32[]{:S(2)}) collective-permute-start(bf16[256,1024]{1,0:T(8,128)(2,1)S(1)} %fusion.7), channel_id=1, source_target_pairs={{0,16},{4,20},{8,24},{12,28},{16,0},{20,4},{24,8},{28,12},{1,17},{... | collective-permute-start | bytes 1572872 | tf_op jit(solution)/shard_map/ppermute | solution.py:467
  154.6 39.7 %collective-permute-start.33 = (bf16[256,1024]{1,0:T(8,128)(2,1)}, bf16[256,1024]{1,0:T(8,128)(2,1)S(1)}, u32[]{:S(2)}, u32[]{:S(2)}) collective-permute-start(bf16[256,1024]{1,0:T(8,128)(2,1)} %get-tuple-element.302), channel_id=1, source_target_pairs={{0,16},{4,20},{8,24},{12,28},{16,0},{20,4},{24,8},{28,12},{1,17},{... | collective-permute-start | bytes 1572872 | tf_op jit(solution)/shard_map/ppermute | solution.py:467
  171.9 22.5 %collective-permute-start.34 = (bf16[256,1024]{1,0:T(8,128)(2,1)S(1)}, bf16[256,1024]{1,0:T(8,128)(2,1)S(1)}, u32[]{:S(2)}, u32[]{:S(2)}) collective-permute-start(bf16[256,1024]{1,0:T(8,128)(2,1)S(1)} %copy-done.42), channel_id=1, source_target_pairs={{0,8},{4,12},{8,0},{12,4},{16,24},{20,28},{24,16},{28,20},{1,9},{5... | collective-permute-start | bytes 1572872 | tf_op jit(solution)/shard_map/ppermute | solution.py:467
  197.0 40.0 %collective-permute-start.35 = (bf16[256,2048]{1,0:T(8,128)(2,1)S(1)}, bf16[256,2048]{1,0:T(8,128)(2,1)S(1)}, u32[]{:S(2)}, u32[]{:S(2)}) collective-permute-start(bf16[256,2048]{1,0:T(8,128)(2,1)S(1)} %fusion.2), channel_id=1, source_target_pairs={{0,8},{4,12},{8,0},{12,4},{16,24},{20,28},{24,16},{28,20},{1,9},{5... | collective-permute-start | bytes 3145736 | tf_op jit(solution)/shard_map/ppermute | solution.py:467
  198.4 38.6 %collective-permute-start.36 = (bf16[256,2048]{1,0:T(8,128)(2,1)}, bf16[256,2048]{1,0:T(8,128)(2,1)S(1)}, u32[]{:S(2)}, u32[]{:S(2)}) collective-permute-start(bf16[256,2048]{1,0:T(8,128)(2,1)} %fusion.3), channel_id=1, source_target_pairs={{0,16},{4,20},{8,24},{12,28},{16,0},{20,4},{24,8},{28,12},{1,17},{... | collective-permute-start | bytes 3145736 | tf_op jit(solution)/shard_map/ppermute | solution.py:467
  199.5 37.5 %collective-permute-start.37 = (bf16[256,1024]{1,0:T(8,128)(2,1)S(1)}, bf16[256,1024]{1,0:T(8,128)(2,1)S(1)}, u32[]{:S(2)}, u32[]{:S(2)}) collective-permute-start(bf16[256,1024]{1,0:T(8,128)(2,1)S(1)} %copy-done.45), channel_id=1, source_target_pairs={{0,16},{4,20},{8,24},{12,28},{16,0},{20,4},{24,8},{28,12},{1,17},{... | collective-permute-start | bytes 1572872 | tf_op jit(solution)/shard_map/ppermute | solution.py:467
  200.4 36.6 %collective-permute-start.38 = (bf16[256,1024]{1,0:T(8,128)(2,1)S(1)}, bf16[256,1024]{1,0:T(8,128)(2,1)S(1)}, u32[]{:S(2)}, u32[]{:S(2)}) collective-permute-start(bf16[256,1024]{1,0:T(8,128)(2,1)S(1)} %copy-done.43), channel_id=1, source_target_pairs={{0,8},{4,12},{8,0},{12,4},{16,24},{20,28},{24,16},{28,20},{1,9},{5... | collective-permute-start | bytes 1572872 | tf_op jit(solution)/shard_map/ppermute | solution.py:467
  240.7 28.7 %collective-permute-start.39 = (bf16[256,2048]{1,0:T(8,128)(2,1)S(1)}, bf16[256,2048]{1,0:T(8,128)(2,1)S(1)}, u32[]{:S(2)}, u32[]{:S(2)}) collective-permute-start(bf16[256,2048]{1,0:T(8,128)(2,1)S(1)} %fusion.4), channel_id=1, source_target_pairs={{0,8},{4,12},{8,0},{12,4},{16,24},{20,28},{24,16},{28,20},{1,9},{5... | collective-permute-start | bytes 3145736 | tf_op jit(solution)/shard_map/ppermute | solution.py:467
  242.1 27.3 %collective-permute-start.40 = (bf16[256,2048]{1,0:T(8,128)(2,1)}, bf16[256,2048]{1,0:T(8,128)(2,1)S(1)}, u32[]{:S(2)}, u32[]{:S(2)}) collective-permute-start(bf16[256,2048]{1,0:T(8,128)(2,1)} %fusion.5), channel_id=1, source_target_pairs={{0,16},{4,20},{8,24},{12,28},{16,0},{20,4},{24,8},{28,12},{1,17},{... | collective-permute-start | bytes 3145736 | tf_op jit(solution)/shard_map/ppermute | solution.py:467
  293.4 29.2 %collective-permute-start.51 = (bf16[1024,1024]{1,0:T(8,128)(2,1)}, bf16[1024,1024]{1,0:T(8,128)(2,1)}, u32[]{:S(2)}, u32[]{:S(2)}) collective-permute-start(bf16[1024,1024]{1,0:T(8,128)(2,1)} %branch_out.2), channel_id=1, source_target_pairs={{0,4},{4,0},{8,12},{12,8},{16,20},{20,16},{24,28},{28,24},{1,5},{5... | collective-permute-start | bytes 6291464 | tf_op jit(solution)/shard_map/ppermute | solution.py:464
  294.9 27.8 %collective-permute-start.50 = (bf16[256,1024]{1,0:T(8,128)(2,1)}, bf16[256,1024]{1,0:T(8,128)(2,1)S(1)}, u32[]{:S(2)}, u32[]{:S(2)}) collective-permute-start(bf16[256,1024]{1,0:T(8,128)(2,1)} %add_convert_fusion), channel_id=1, source_target_pairs={{0,3},{1,0},{2,1},{3,2},{4,7},{5,4},{6,5},{7,6},{8,11},{9,8},{10,9... | collective-permute-start | bytes 1572872 | tf_op jit(solution)/shard_map/ppermute | solution.py:504
  299.4 23.2 %collective-permute-start.49 = (bf16[256,512]{1,0:T(8,128)(2,1)S(1)}, bf16[256,512]{1,0:T(8,128)(2,1)S(1)}, u32[]{:S(2)}, u32[]{:S(2)}) collective-permute-start(bf16[256,512]{1,0:T(8,128)(2,1)S(1)} %get-tuple-element.383), channel_id=1, source_target_pairs={{0,1},{1,2},{2,3},{3,0},{4,5},{5,6},{6,7},{7,4},{8,9},{9,10},{10,1... | collective-permute-start | bytes 786440 | tf_op jit(solution)/shard_map/ppermute | solution.py:470
  (98 other events, 1088.4 us)
